TPU v7x, 256 devices: a whole 4x4x8 slice. The times are simulated.
256 devices in a mesh: gx: 16 (over z_lo, y), gy: 4 (over x), gz: 4 (over z_hi, core).
Axes of the slice: x: 4, y: 4, z: 8 (z_hi: 2, z_lo: 4; z = z_hi * 4 + z_lo), core: 2. Of those that a mesh axis runs over, the one named last changes fastest.
Arguments:
- displacement: float32 [3, 1024, 128, 512], P(None, 'gx', 'gy', 'gz'), as said below
- density: float32 [1024, 128, 512], P('gx', 'gy', 'gz'), may hold values from 0.1 to 0.9
- cell_flags: int32 [1024, 128, 512], P('gx', 'gy', 'gz'), may hold values from 0 to 2
- trim_level: int32 [1024, 128, 512], P('gx', 'gy', 'gz'), may hold values from 0 to 3
Outputs:
- projected: float32 [1024, 128, 512], P('gx', 'gy', 'gz')
- filtered: float32 [1024, 128, 512], P('gx', 'gy', 'gz')
Inputs may be any that keep to these rules, and one draw needn't show every extreme that they name: `displacement`: displacements of order one.
All inputs are finite; a program needn't handle non-finite values.
Results may differ from a plain program's by a relative error of at most 0.0003.
Values sent between devices are 32-bit elements; how exact they have to be, the bound alone decides.
No kernel may reach another device: no remote copies, remote signals or barrier semaphores. Data moves between devices by JAX's collectives and lax.ppermute only.
A program may use at most 128 MiB of HBM per device.

v0:
```python
import math

import jax
import jax.numpy as jnp
from jax import lax
from jax.sharding import PartitionSpec as P

SWEEPS = 4


LAMBDA = 0.3 / 0.52
SHEAR_MODULUS = 1.0 / 2.6
FILTER_COEF = 0.75
SPREAD_MID = 5.5
SPREAD_HALF = 4.5
STEP_SIZE = 0.3
SHARPNESS = 8.0
THRESHOLD = 0.5
GAUSS_POINTS = [0.5 - 0.5 / math.sqrt(3.0), 0.5 + 0.5 / math.sqrt(3.0)]
VALUES = [
    [(1.0 - t) ** 2 / 2.0, (1.0 + 2.0 * t - 2.0 * t * t) / 2.0, t * t / 2.0] for t in GAUSS_POINTS
]
SLOPES = [[t - 1.0, 1.0 - 2.0 * t, t] for t in GAUSS_POINTS]


def with_halo(block, sides, width):
    for axis, dim in sides:
        count = lax.axis_size(axis)
        forward = [(i, i + 1) for i in range(count - 1)]
        backward = [(target, source) for source, target in forward]
        low = lax.ppermute(
            lax.slice_in_dim(block, block.shape[dim] - width, None, axis=dim), axis, forward
        )
        high = lax.ppermute(lax.slice_in_dim(block, 0, width, axis=dim), axis, backward)
        block = jnp.concatenate([low, block, high], axis=dim)
    return block


def spline_pass(field, axis, weights):
    length = field.shape[axis] - 2
    total = weights[0] * lax.slice_in_dim(field, 0, length, axis=axis)
    total = total + weights[1] * lax.slice_in_dim(field, 1, length + 1, axis=axis)
    return total + weights[2] * lax.slice_in_dim(field, 2, length + 2, axis=axis)


def point_energy(grads):
    trace = grads[0][0] + grads[1][1] + grads[2][2]
    squares = grads[0][0] ** 2 + grads[1][1] ** 2 + grads[2][2] ** 2
    squares = squares + 0.5 * (
        (grads[0][1] + grads[1][0]) ** 2
        + (grads[0][2] + grads[2][0]) ** 2
        + (grads[1][2] + grads[2][1]) ** 2
    )
    return LAMBDA * trace * trace + 2.0 * SHEAR_MODULUS * squares


def strain_energy(padded):
    along_z = [
        [
            (
                spline_pass(padded[component], 2, VALUES[point]),
                spline_pass(padded[component], 2, SLOPES[point]),
            )
            for point in range(2)
        ]
        for component in range(3)
    ]
    total = 0.0
    for point_z in range(2):
        for point_y in range(2):
            partial_y = []
            for component in range(3):
                value_z, slope_z = along_z[component][point_z]
                partial_y.append(
                    (
                        spline_pass(value_z, 1, VALUES[point_y]),
                        spline_pass(value_z, 1, SLOPES[point_y]),
                        spline_pass(slope_z, 1, VALUES[point_y]),
                    )
                )
            for point_x in range(2):
                grads = []
                for component in range(3):
                    plain, slope_y, slope_zz = partial_y[component]
                    grads.append(
                        (
                            spline_pass(plain, 0, SLOPES[point_x]),
                            spline_pass(slope_y, 0, VALUES[point_x]),
                            spline_pass(slope_zz, 0, VALUES[point_x]),
                        )
                    )
                total = total + point_energy(grads)
    return total * 0.125


def cell_source(energy, density, cell_flags, trim_level):
    trimmed = (1.0 + trim_level.astype(jnp.float32)) / 5.0
    share = jnp.where(cell_flags == 1, 1.0, jnp.where(cell_flags == 2, trimmed, 0.001))
    return -3.0 * density * density * density * share * energy


def stencil(padded):
    center = padded[1:-1, 1:-1, 1:-1]
    beside = padded[2:, 1:-1, 1:-1] + padded[:-2, 1:-1, 1:-1]
    beside = beside + padded[1:-1, 2:, 1:-1] + padded[1:-1, :-2, 1:-1]
    beside = beside + padded[1:-1, 1:-1, 2:] + padded[1:-1, 1:-1, :-2]
    return (1.0 + 6.0 * FILTER_COEF) * center - FILTER_COEF * beside


def chebyshev(source, apply_fn):
    sigma = SPREAD_MID / SPREAD_HALF
    solution = jnp.zeros_like(source)
    residual = source
    direction = source / SPREAD_MID
    rho_old = 1.0 / sigma
    for sweep_index in range(SWEEPS):
        image = apply_fn(direction)
        solution = solution + direction
        residual = residual - image
        rho_new = 1.0 / (2.0 * sigma - rho_old)
        direction = rho_new * rho_old * direction + 2.0 * rho_new / SPREAD_HALF * residual
        rho_old = rho_new
    return solution + direction


def projection(density, filtered, scale):
    trial = density - STEP_SIZE * (filtered / scale + 1.0)
    lower = math.tanh(SHARPNESS * THRESHOLD)
    return (lower + jnp.tanh(SHARPNESS * (trial - THRESHOLD))) / (
        lower + math.tanh(SHARPNESS * (1.0 - THRESHOLD))
    )


def body(displacement, density, cell_flags, trim_level):
    padded = with_halo(displacement, (("gx", 1), ("gy", 2), ("gz", 3)), 1)
    energy = strain_energy(padded)
    source = cell_source(energy, density, cell_flags, trim_level)
    brick_x, brick_y, brick_z = source.shape
    count_y = lax.axis_size("gy")
    count_z = lax.axis_size("gz")
    groups = count_y * count_z
    planes = brick_x // groups
    pieces = source.reshape(groups, planes, brick_y, brick_z)
    arrived = lax.all_to_all(pieces, ("gy", "gz"), split_axis=0, concat_axis=0, tiled=True)
    arrived = arrived.reshape(count_y, count_z, planes, brick_y, brick_z).transpose(2, 0, 3, 1, 4)
    slab_source = arrived.reshape(planes, count_y * brick_y, count_z * brick_z)

    def apply_slab(direction):
        rimmed = with_halo(direction, ((("gx", "gy", "gz"), 0),), 1)
        return stencil(jnp.pad(rimmed, ((0, 0), (1, 1), (1, 1))))

    slab_filtered = chebyshev(slab_source, apply_slab)
    outgoing = slab_filtered.reshape(planes, count_y, brick_y, count_z, brick_z).transpose(
        1, 3, 0, 2, 4
    )
    outgoing = outgoing.reshape(groups, planes, brick_y, brick_z)
    filtered = lax.all_to_all(
        outgoing, ("gy", "gz"), split_axis=0, concat_axis=0, tiled=True
    ).reshape(brick_x, brick_y, brick_z)
    total = lax.psum(jnp.sum(jnp.abs(filtered)), ("gx", "gy", "gz"))
    cells = filtered.size * lax.axis_size(("gx", "gy", "gz"))
    scale = total / cells + 1e-06
    return (projection(density, filtered, scale), filtered)


def solution(mesh):
    return jax.shard_map(
        body,
        mesh=mesh,
        in_specs=(
            P(None, "gx", "gy", "gz"),
            P("gx", "gy", "gz"),
            P("gx", "gy", "gz"),
            P("gx", "gy", "gz"),
        ),
        out_specs=(P("gx", "gy", "gz"), P("gx", "gy", "gz")),
        check_vma=False,
    )
```

profile of v0, /device:TPU:1, one launch (start us, length us, event | category | flops | bytes accessed | tf_op | source)
XLA Modules:
  0.0 373.6 jit_solution(13153826491728520258)
XLA Ops:
  1.5 4.0 %collective-permute-start = (f32[3,1,32,128]{3,2,1,0:T(8,128)S(1)}, f32[3,1,32,128]{3,2,1,0:T(8,128)S(1)}, u32[]{:S(2)}, u32[]{:S(2)}) collective-permute-start(f32[3,1,32,128]{3,2,1,0:T(8,128)S(1)} %get-tuple-element.20), channel_id=1, source_target_pairs={{0,16},{16,32},{32,48},{48,64},{64,80},{80,96},{96,112},{112,128},... | collective-permute-start | bytes 147464 | tf_op jit(solution)/shard_map/ppermute | solution.py:31
  10.5 3.1 collective-permute-start.2
  15.3 3.7 %collective-permute-done.3 = f32[3,66,1,128]{3,2,1,0:T(1,128)S(1)} collective-permute-done((f32[3,66,1,128]{3,2,1,0:T(1,128)S(1)}, f32[3,66,1,128]{3,2,1,0:T(1,128)S(1)}, u32[]{:S(2)}, u32[]{:S(2)}) %collective-permute-start.3) | collective-permute-done | bytes 101408 | tf_op jit(solution)/shard_map/ppermute | solution.py:34
  19.6 4.4 %fusion.40 = (f32[3,66,34,1]{3,2,1,0:T(8,128)}, f32[3,66,34,1]{3,2,1,0:T(8,128)}) fusion(f32[3,66,34,128]{3,2,1,0:T(8,128)S(1)} %pad_maximum_fusion.1), kind=kLoop, calls=%fused_computation.176 | loop fusion | bytes 107712 | tf_op jit(solution)/shard_map/slice | solution.py:32
  24.0 3.6 copy.38
  27.6 12.2 %collective-permute-start.4 = (f32[3,66,34,1]{1,3,2,0:T(1,128)S(1)}, f32[3,66,34,1]{1,3,2,0:T(1,128)S(1)}, u32[]{:S(2)}, u32[]{:S(2)}) collective-permute-start(f32[3,66,34,1]{1,3,2,0:T(1,128)S(1)} %copy.38), channel_id=1, source_target_pairs={{0,1},{1,2},{2,3},{4,5},{5,6},{6,7},{8,9},{9,10},{10,11},{12,13},{... | collective-permute-start | bytes 80792 | tf_op jit(solution)/shard_map/ppermute | solution.py:31
  39.8 4.2 %copy.39 = f32[3,66,34,1]{1,3,2,0:T(1,128)} copy(f32[3,66,34,1]{3,2,1,0:T(8,128)} %get-tuple-element.16) | data formatting | bytes 53856 | tf_op jit(solution)/shard_map/slice | solution.py:34
  45.9 3.2 copy.40
  49.2 4.6 %collective-permute-done.5 = f32[3,66,34,1]{1,3,2,0:T(1,128)} collective-permute-done((f32[3,66,34,1]{1,3,2,0:T(1,128)}, f32[3,66,34,1]{1,3,2,0:T(1,128)}, u32[]{:S(2)}, u32[]{:S(2)}) %collective-permute-start.5) | collective-permute-done | bytes 26960 | tf_op jit(solution)/shard_map/ppermute | solution.py:34
  53.8 3.9 %copy.41 = f32[3,66,34,1]{3,2,1,0:T(8,128)} copy(f32[3,66,34,1]{1,3,2,0:T(1,128)} %collective-permute-done.5) | data formatting | bytes 53856 | tf_op jit(solution)/shard_map/ppermute | solution.py:34
  57.7 8.2 %pad_maximum_fusion = f32[3,66,34,130]{3,2,1,0:T(8,128)S(1)} fusion(f32[3,66,34,1]{3,2,1,0:T(8,128)} %copy.41, f32[3,66,1,128]{3,2,1,0:T(1,128)S(1)} %collective-permute-done.3, f32[3,66,32,128]{3,2,1,0:T(8,128)S(1)} %constant_dynamic-update-slice_fusion, f32[3,66,1,128]{3,2,1,0:T(1,128)S(1)} %collective-permute-done.2, f32[3,66,34,1]{3,2,1,0:T(8,128)} %copy.40), kind=kLoop, calls=%fused_computation | loop fusion | flops 3500640 | bytes 7001280 | tf_op jit(solution)/shard_map/concatenate | solution.py:35
  75.6 2.7 multiply_add_fusion.41
  79.4 2.7 multiply_add_fusion.46
  82.1 2.7 multiply_add_fusion.28
  84.8 2.9 multiply_add_fusion.24
  87.6 2.9 multiply_add_fusion.27
  90.5 3.1 multiply_add_fusion.22
  93.6 38.0 %fusion.4 = f32[64,32,128]{2,1,0:T(8,128)} fusion(f32[64,32,128]{2,1,0:T(8,128)} %param.5, f32[66,32,128]{2,1,0:T(8,128)} %get-tuple-element.64, f32[66,32,128]{2,1,0:T(8,128)} %get-tuple-element.68, f32[66,32,128]{2,1,0:T(8,128)} %get-tuple-element.66, f32[66,32,128]{2,1,0:T(8,128)} %get-tuple-element.62, f32[66,32,128]{2,1,0:T(8,128)} %get-tuple-element.56, ...), kind=kLoop, calls=%fused_computation.85 | loop fusion | flops 137363456 | bytes 117440512 | tf_op jit(solution)/shard_map/mul | solution.py:99
  131.6 24.6 %all_to_all.10 = f32[16,4,32,128]{3,2,1,0:T(8,128)S(1)} all-to-all(f32[16,4,32,128]{3,2,1,0:T(8,128)} %bitcast.15), channel_id=1, replica_groups=mesh['gx'=16,'gy'=4,'gz'=4] {'gy','gz'}, dimensions={0} | all-to-all | bytes 2097152 | tf_op jit(solution)/shard_map/all_to_all | solution.py:144
  157.5 3.0 collective-permute-start.7
  162.4 5.0 %collective-permute-done.7 = f32[1,128,512]{2,1,0:T(8,128)S(1)} collective-permute-done((f32[1,128,512]{2,1,0:T(8,128)S(1)}, f32[1,128,512]{2,1,0:T(8,128)S(1)}, u32[]{:S(2)}, u32[]{:S(2)}) %collective-permute-start.7) | collective-permute-done | bytes 262176 | tf_op jit(solution)/shard_map/ppermute | solution.py:31
  167.4 4.7 %collective-permute-done.6 = f32[1,128,512]{2,1,0:T(8,128)S(1)} collective-permute-done((f32[1,128,512]{2,1,0:T(8,128)S(1)}, f32[1,128,512]{2,1,0:T(8,128)S(1)}, u32[]{:S(2)}, u32[]{:S(2)}) %collective-permute-start.6) | collective-permute-done | bytes 262176 | tf_op jit(solution)/shard_map/ppermute | solution.py:34
  173.9 3.6 collective-permute-start.9
  179.4 4.7 %collective-permute-done.9 = f32[1,128,512]{2,1,0:T(8,128)S(1)} collective-permute-done((f32[1,128,512]{2,1,0:T(8,128)S(1)}, f32[1,128,512]{2,1,0:T(8,128)S(1)}, u32[]{:S(2)}, u32[]{:S(2)}) %collective-permute-start.9) | collective-permute-done | bytes 262176 | tf_op jit(solution)/shard_map/ppermute | solution.py:31
  184.1 5.8 %collective-permute-done.8 = f32[1,128,512]{2,1,0:T(8,128)S(1)} collective-permute-done((f32[1,128,512]{2,1,0:T(8,128)S(1)}, f32[1,128,512]{2,1,0:T(8,128)S(1)}, u32[]{:S(2)}, u32[]{:S(2)}) %collective-permute-start.8) | collective-permute-done | bytes 262176 | tf_op jit(solution)/shard_map/ppermute | solution.py:34
  196.5 6.5 %collective-permute-done.11 = f32[1,128,512]{2,1,0:T(8,128)S(1)} collective-permute-done((f32[1,128,512]{2,1,0:T(8,128)S(1)}, f32[1,128,512]{2,1,0:T(8,128)S(1)}, u32[]{:S(2)}, u32[]{:S(2)}) %collective-permute-start.11) | collective-permute-done | bytes 262176 | tf_op jit(solution)/shard_map/ppermute | solution.py:31
  203.0 4.7 %collective-permute-done.10 = f32[1,128,512]{2,1,0:T(8,128)S(1)} collective-permute-done((f32[1,128,512]{2,1,0:T(8,128)S(1)}, f32[1,128,512]{2,1,0:T(8,128)S(1)}, u32[]{:S(2)}, u32[]{:S(2)}) %collective-permute-start.10) | collective-permute-done | bytes 262176 | tf_op jit(solution)/shard_map/ppermute | solution.py:34
  209.5 3.6 collective-permute-start.13
  215.1 7.0 %collective-permute-done.13 = f32[1,128,512]{2,1,0:T(8,128)S(1)} collective-permute-done((f32[1,128,512]{2,1,0:T(8,128)S(1)}, f32[1,128,512]{2,1,0:T(8,128)S(1)}, u32[]{:S(2)}, u32[]{:S(2)}) %collective-permute-start.13) | collective-permute-done | bytes 262176 | tf_op jit(solution)/shard_map/ppermute | solution.py:31
  222.0 6.2 %collective-permute-done.12 = f32[1,128,512]{2,1,0:T(8,128)S(1)} collective-permute-done((f32[1,128,512]{2,1,0:T(8,128)S(1)}, f32[1,128,512]{2,1,0:T(8,128)S(1)}, u32[]{:S(2)}, u32[]{:S(2)}) %collective-permute-start.12) | collective-permute-done | bytes 262176 | tf_op jit(solution)/shard_map/ppermute | solution.py:34
  230.7 37.0 %all_to_all.11 = f32[16,4,32,128]{3,2,1,0:T(8,128)S(1)} all-to-all(f32[16,4,32,128]{3,2,1,0:T(8,128)S(1)} %bitcast.18), channel_id=1, replica_groups=mesh['gx'=16,'gy'=4,'gz'=4] {'gy','gz'}, dimensions={0} | all-to-all | bytes 2097152 | tf_op jit(solution)/shard_map/all_to_all | solution.py:157
  268.5 102.0 %psum.7 = f32[]{:T(128)} all-reduce(f32[]{:T(128)} %abs_reduce_fusion), channel_id=1, replica_groups=mesh['gx'=16,'gy'=4,'gz'=4] {'gx','gy','gz'}, use_global_device_ids=true, to_apply=%region_1.2 | all-reduce | flops 1 | bytes 8 | tf_op jit(solution)/shard_map/psum | solution.py:160
  (47 shorter events, 43.3 us)
Async XLA Ops:
  1.5 5.3 %collective-permute-start = (f32[3,1,32,128]{3,2,1,0:T(8,128)S(1)}, f32[3,1,32,128]{3,2,1,0:T(8,128)S(1)}, u32[]{:S(2)}, u32[]{:S(2)}) collective-permute-start(f32[3,1,32,128]{3,2,1,0:T(8,128)S(1)} %get-tuple-element.20), channel_id=1, source_target_pairs={{0,16},{16,32},{32,48},{48,64},{64,80},{80,96},{96,112},{112,128},... | collective-permute-start | bytes 147464 | tf_op jit(solution)/shard_map/ppermute | solution.py:31
  5.5 4.8 %collective-permute-start.1 = (f32[3,1,32,128]{3,2,1,0:T(8,128)S(1)}, f32[3,1,32,128]{3,2,1,0:T(8,128)S(1)}, u32[]{:S(2)}, u32[]{:S(2)}) collective-permute-start(f32[3,1,32,128]{3,2,1,0:T(8,128)S(1)} %get-tuple-element.19), channel_id=1, source_target_pairs={{16,0},{32,16},{48,32},{64,48},{80,64},{96,80},{112,96},{128,112},... | collective-permute-start | bytes 147464 | tf_op jit(solution)/shard_map/ppermute | solution.py:34
  10.5 4.8 %collective-permute-start.2 = (f32[3,66,1,128]{3,2,1,0:T(1,128)S(1)}, f32[3,66,1,128]{3,2,1,0:T(1,128)S(1)}, u32[]{:S(2)}, u32[]{:S(2)}) collective-permute-start(f32[3,66,1,128]{3,2,1,0:T(1,128)S(1)} %get-tuple-element.17), channel_id=1, source_target_pairs={{0,4},{4,8},{8,12},{1,5},{5,9},{9,13},{2,6},{6,10},{10,14},{3,7},{... | collective-permute-start | bytes 304136 | tf_op jit(solution)/shard_map/ppermute | solution.py:31
  13.6 5.4 %collective-permute-start.3 = (f32[3,66,1,128]{3,2,1,0:T(1,128)S(1)}, f32[3,66,1,128]{3,2,1,0:T(1,128)S(1)}, u32[]{:S(2)}, u32[]{:S(2)}) collective-permute-start(f32[3,66,1,128]{3,2,1,0:T(1,128)S(1)} %get-tuple-element.18), channel_id=1, source_target_pairs={{4,0},{8,4},{12,8},{5,1},{9,5},{13,9},{6,2},{10,6},{14,10},{7,3},{... | collective-permute-start | bytes 304136 | tf_op jit(solution)/shard_map/ppermute | solution.py:34
  27.6 18.3 %collective-permute-start.4 = (f32[3,66,34,1]{1,3,2,0:T(1,128)S(1)}, f32[3,66,34,1]{1,3,2,0:T(1,128)S(1)}, u32[]{:S(2)}, u32[]{:S(2)}) collective-permute-start(f32[3,66,34,1]{1,3,2,0:T(1,128)S(1)} %copy.38), channel_id=1, source_target_pairs={{0,1},{1,2},{2,3},{4,5},{5,6},{6,7},{8,9},{9,10},{10,11},{12,13},{... | collective-permute-start | bytes 80792 | tf_op jit(solution)/shard_map/ppermute | solution.py:31
  44.0 9.8 %collective-permute-start.5 = (f32[3,66,34,1]{1,3,2,0:T(1,128)}, f32[3,66,34,1]{1,3,2,0:T(1,128)}, u32[]{:S(2)}, u32[]{:S(2)}) collective-permute-start(f32[3,66,34,1]{1,3,2,0:T(1,128)} %copy.39), channel_id=1, source_target_pairs={{1,0},{2,1},{3,2},{5,4},{6,5},{7,6},{9,8},{10,9},{11,10},{13,12},{... | collective-permute-start | bytes 80792 | tf_op jit(solution)/shard_map/ppermute | solution.py:34
  157.5 10.0 %collective-permute-start.7 = (f32[1,128,512]{2,1,0:T(8,128)S(1)}, f32[1,128,512]{2,1,0:T(8,128)S(1)}, u32[]{:S(2)}, u32[]{:S(2)}) collective-permute-start(f32[1,128,512]{2,1,0:T(8,128)S(1)} %get-tuple-element.75), channel_id=1, source_target_pairs={{0,1},{1,2},{2,3},{3,4},{4,5},{5,6},{6,7},{7,8},{8,9},{9,10},{10,1... | collective-permute-start | bytes 786440 | tf_op jit(solution)/shard_map/ppermute | solution.py:31
  160.5 11.6 %collective-permute-start.6 = (f32[1,128,512]{2,1,0:T(8,128)S(1)}, f32[1,128,512]{2,1,0:T(8,128)S(1)}, u32[]{:S(2)}, u32[]{:S(2)}) collective-permute-start(f32[1,128,512]{2,1,0:T(8,128)S(1)} %get-tuple-element.76), channel_id=1, source_target_pairs={{1,0},{2,1},{3,2},{4,3},{5,4},{6,5},{7,6},{8,7},{9,8},{10,9},{11,1... | collective-permute-start | bytes 786440 | tf_op jit(solution)/shard_map/ppermute | solution.py:34
  173.9 10.3 %collective-permute-start.9 = (f32[1,128,512]{2,1,0:T(8,128)S(1)}, f32[1,128,512]{2,1,0:T(8,128)S(1)}, u32[]{:S(2)}, u32[]{:S(2)}) collective-permute-start(f32[1,128,512]{2,1,0:T(8,128)S(1)} %get-tuple-element.73), channel_id=1, source_target_pairs={{0,1},{1,2},{2,3},{3,4},{4,5},{5,6},{6,7},{7,8},{8,9},{9,10},{10,1... | collective-permute-start | bytes 786440 | tf_op jit(solution)/shard_map/ppermute | solution.py:31
  177.5 12.5 %collective-permute-start.8 = (f32[1,128,512]{2,1,0:T(8,128)S(1)}, f32[1,128,512]{2,1,0:T(8,128)S(1)}, u32[]{:S(2)}, u32[]{:S(2)}) collective-permute-start(f32[1,128,512]{2,1,0:T(8,128)S(1)} %get-tuple-element.74), channel_id=1, source_target_pairs={{1,0},{2,1},{3,2},{4,3},{5,4},{6,5},{7,6},{8,7},{9,8},{10,9},{11,1... | collective-permute-start | bytes 786440 | tf_op jit(solution)/shard_map/ppermute | solution.py:34
  191.8 11.3 %collective-permute-start.11 = (f32[1,128,512]{2,1,0:T(8,128)S(1)}, f32[1,128,512]{2,1,0:T(8,128)S(1)}, u32[]{:S(2)}, u32[]{:S(2)}) collective-permute-start(f32[1,128,512]{2,1,0:T(8,128)S(1)} %get-tuple-element.71), channel_id=1, source_target_pairs={{0,1},{1,2},{2,3},{3,4},{4,5},{5,6},{6,7},{7,8},{8,9},{9,10},{10,1... | collective-permute-start | bytes 786440 | tf_op jit(solution)/shard_map/ppermute | solution.py:31
  194.4 13.3 %collective-permute-start.10 = (f32[1,128,512]{2,1,0:T(8,128)S(1)}, f32[1,128,512]{2,1,0:T(8,128)S(1)}, u32[]{:S(2)}, u32[]{:S(2)}) collective-permute-start(f32[1,128,512]{2,1,0:T(8,128)S(1)} %get-tuple-element.72), channel_id=1, source_target_pairs={{1,0},{2,1},{3,2},{4,3},{5,4},{6,5},{7,6},{8,7},{9,8},{10,9},{11,1... | collective-permute-start | bytes 786440 | tf_op jit(solution)/shard_map/ppermute | solution.py:34
  209.5 12.6 %collective-permute-start.13 = (f32[1,128,512]{2,1,0:T(8,128)S(1)}, f32[1,128,512]{2,1,0:T(8,128)S(1)}, u32[]{:S(2)}, u32[]{:S(2)}) collective-permute-start(f32[1,128,512]{2,1,0:T(8,128)S(1)} %get-tuple-element.69), channel_id=1, source_target_pairs={{0,1},{1,2},{2,3},{3,4},{4,5},{5,6},{6,7},{7,8},{8,9},{9,10},{10,1... | collective-permute-start | bytes 786440 | tf_op jit(solution)/shard_map/ppermute | solution.py:31
  213.1 15.1 %collective-permute-start.12 = (f32[1,128,512]{2,1,0:T(8,128)S(1)}, f32[1,128,512]{2,1,0:T(8,128)S(1)}, u32[]{:S(2)}, u32[]{:S(2)}) collective-permute-start(f32[1,128,512]{2,1,0:T(8,128)S(1)} %get-tuple-element.70), channel_id=1, source_target_pairs={{1,0},{2,1},{3,2},{4,3},{5,4},{6,5},{7,6},{8,7},{9,8},{10,9},{11,1... | collective-permute-start | bytes 786440 | tf_op jit(solution)/shard_map/ppermute | solution.py:34
  230.6 140.5 %copy-start = (f32[64,32,128]{2,1,0:T(8,128)S(1)}, f32[64,32,128]{2,1,0:T(8,128)}, u32[]{:S(2)}) copy-start(f32[64,32,128]{2,1,0:T(8,128)} %param.5) | copy-start | bytes 3145732
where the time goes:
time: 381 us; the launch traced here: 374 us
  blocking collectives  164 us (43%)
  other arithmetic  83.1 us (22%)
  waiting for transfers between devices  54.6 us (14%)
  starting transfers between devices  44.7 us (12%)
  local copies, waits for them, and re-layouts  25.9 us (7%)
    psum x1, blocking collectives, body(): total = lax.psum(jnp.sum(jnp.abs(filtered)), ('gx', 'gy', 'gz'))  102 us
    mul x1, other arithmetic, cell_source(): return -3.0 * density * density * density * share * energy  38 us
    all_to_all x1, blocking collectives, body(): lax.all_to_all(outgoing, ('gy', 'gz'), split_axis=0, concat_axis=0, tiled...  37 us
    ppermute x7, starting transfers between devices, with_halo(): lax.ppermute(lax.slice_in_dim(block, block.shape[dim] - width, None, axis...  32.3 us
    ppermute x7, waiting for transfers between devices, with_halo(): lax.ppermute(lax.slice_in_dim(block, 0, width, axis=dim), axis, backward)  31.1 us
    add x12, other arithmetic, spline_pass(): total + weights[2] * lax.slice_in_dim(field, 2, length + 2, axis=axis)  27 us
    all_to_all x1, blocking collectives, body(): lax.all_to_all(pieces, ('gy', 'gz'), split_axis=0, concat_axis=0, tiled=T...  24.6 us
    ppermute x7, waiting for transfers between devices, with_halo(): lax.ppermute(lax.slice_in_dim(block, block.shape[dim] - width, None, axis...  23.5 us
  transfers between devices with their start and end apart: 14, of which 12 were waited for; matrix products, arithmetic and copies ran while one was open for 3% of the time, Pallas kernels for 0%

commit v1 on v0

v1 whole, which is shorter than its diff:
```python
import functools
import math

import jax
import jax.numpy as jnp
from jax import lax
from jax.experimental import pallas as pl
from jax.experimental.pallas import tpu as pltpu
from jax.sharding import PartitionSpec as P

LAMBDA = 0.3 / 0.52
SHEAR_MODULUS = 1.0 / 2.6
SPREAD_MID = 5.5
SPREAD_HALF = 4.5
STEP_SIZE = 0.3
SHARPNESS = 8.0
THRESHOLD = 0.5

AXES = ("gx", "gy", "gz")
LANES = 128
REACH = 4
WIDE = REACH + 1

SIGMA = SPREAD_MID / SPREAD_HALF
CHEB = 16.0 * SIGMA**5 - 20.0 * SIGMA**3 + 5.0 * SIGMA
POLY = [
    (16.0 * SIGMA**4 - 20.0 * SIGMA**2 + 5.0) / (SPREAD_HALF * CHEB),
    (16.0 * SIGMA**3 - 20.0 * SIGMA) / 6.0 / (SPREAD_HALF * CHEB),
    (16.0 * SIGMA**2 - 20.0) / 36.0 / (SPREAD_HALF * CHEB),
    16.0 * SIGMA / 216.0 / (SPREAD_HALF * CHEB),
    16.0 / 1296.0 / (SPREAD_HALF * CHEB),
]

F32 = jnp.float32
VMEM = pl.BlockSpec(memory_space=pltpu.VMEM)
PARAMS = dict(vmem_limit_bytes=56 * 1024 * 1024)


def swap(first, second, axis):
    count = lax.axis_size(axis)
    even = [(i, i ^ 1) for i in range(count)]
    odd = [(i, i + 1 if i % 2 else i - 1) for i in range(1, count - 1)]
    got_first = lax.ppermute(first, axis, even)
    got_second = lax.ppermute(second, axis, odd) if odd else jnp.zeros_like(second)
    return got_first, got_second


def is_odd(axis):
    return lax.rem(lax.axis_index(axis), 2) == 1


def cell_coef(density, cell_flags, trim_level):
    trimmed = (1.0 + trim_level.astype(F32)) * 0.2
    share = jnp.where(cell_flags == 1, 1.0, jnp.where(cell_flags == 2, trimmed, 0.001))
    return -3.0 * density * density * density * share


def lane_ids():
    return lax.broadcasted_iota(jnp.int32, (8, LANES), 1)


def row_ids():
    return lax.broadcasted_iota(jnp.int32, (8, LANES), 0)


def half_turn(tile):
    return pltpu.roll(tile, 4, 0)


def rim_tile(first, second, index, odd):
    one = jnp.broadcast_to(first[pl.ds(index, 1), :], (8, LANES))
    two = jnp.broadcast_to(second[pl.ds(index, 1), :], (8, LANES))
    at_top = row_ids() == 0
    return jnp.where(jnp.logical_xor(at_top, odd), one, two)


def ends_kernel(disp, xr1, xr2, yr1, yr2, zs1, zs2):
    _, bx, by, _ = disp.shape
    planes = bx + 2 * WIDE
    odd_y, odd_z = is_odd("gy"), is_odd("gz")
    lane = lane_ids()

    def gather(tile_of, c, row):
        low = jnp.zeros((8, LANES), F32)
        high = jnp.zeros((8, LANES), F32)
        for x in range(planes):
            tile = tile_of(x)
            here = lane == x
            low = jnp.where(here, pltpu.roll(tile, x, 1) if x else tile, low)
            high = jnp.where(here, pltpu.roll(tile, x + 1, 1), high)
        zs1[c, pl.ds(row, 8), :] = jnp.where(odd_z, low, high)
        zs2[c, pl.ds(row, 8), :] = jnp.where(odd_z, high, low)

    for c in range(3):

        def rows(t, carry, c=c):
            row = pl.multiple_of(8 * t, 8)

            def tile_of(x):
                if x < WIDE:
                    return xr1[c * WIDE + x, pl.ds(row, 8), :]
                if x < WIDE + bx:
                    return disp[c, x - WIDE, pl.ds(row, 8), :]
                return xr2[c * WIDE + x - WIDE - bx, pl.ds(row, 8), :]

            gather(tile_of, c, row)
            return carry

        lax.fori_loop(0, by // 8, rows, 0)
        gather(lambda x, c=c: rim_tile(yr1, yr2, c * planes + x, odd_y), c, by)


def triple(a, b, c):
    ends = a + c
    curve = ends - 2.0 * b
    return 4.0 * b + (2.0 / 3.0) * curve, c - a, curve


def pair(a, b, c):
    return (2.0 / 3.0) * (a + c) + (8.0 / 3.0) * b, c - a


def energy_of(fields):
    grads = []
    for c in range(3):
        g = {}
        for key, planes in fields[c].items():
            if key == "MM":
                a, b, n = planes
                g["DMM"], g["SMM"] = n - a, (a + n) - 2.0 * b
            elif key in ("MD", "DM", "DD"):
                g["M" + key], g["D" + key], g["S" + key] = triple(*planes)
            else:
                g["M" + key], g["D" + key] = pair(*planes)
        grads.append(g)
    names = "MD", "DS"

    def part(c, e, p):
        return grads[c]["".join(names[1 if d == e else 0][p[d]] for d in range(3))]

    traces = normals = shears = None
    for order in (3, 2, 1, 0):
        if traces is not None:
            traces, normals, shears = (v * (1.0 / 3.0) for v in (traces, normals, shears))
        for bits in range(8):
            p = (bits >> 2) & 1, (bits >> 1) & 1, bits & 1
            if sum(p) != order:
                continue
            xx, yy, zz = (part(c, c, p) for c in range(3))
            xy = part(0, 1, p) + part(1, 0, p)
            xz = part(0, 2, p) + part(2, 0, p)
            yz = part(1, 2, p) + part(2, 1, p)
            trace = xx + yy + zz
            trace = trace * trace
            normal = xx * xx + yy * yy + zz * zz
            shear = xy * xy + xz * xz + yz * yz
            if traces is None:
                traces, normals, shears = trace, normal, shear
            else:
                traces, normals, shears = traces + trace, normals + normal, shears + shear
    scale = 1.0 / 1024.0
    return (
        (LAMBDA * scale) * traces
        + (2.0 * SHEAR_MODULUS * scale) * normals
        + (SHEAR_MODULUS * scale) * shears
    )


YZ = ("MM", "MD", "MS", "DM", "DD", "DS", "SM", "SD")


def source_kernel(
    disp, density, flags, trim, xr1, xr2, yr1, yr2, zr1, zr2,
    source, ys1, ys2, packed,
    field, coef, zlow, zhigh, along, ring,
):
    _, bx, by, _ = disp.shape
    planes = bx + 2 * WIDE
    cells = bx + 2 * REACH
    odd_x, odd_y, odd_z = is_odd("gx"), is_odd("gy"), is_odd("gz")
    lane, row = lane_ids(), row_ids()

    for k in range(WIDE):
        for c in range(3):
            field[c, jnp.where(odd_x, 0, bx + WIDE) + k, 0:by, :] = xr1[c * WIDE + k]
            field[c, jnp.where(odd_x, bx + WIDE, 0) + k, 0:by, :] = xr2[c * WIDE + k]
    for k in range(REACH):
        coef[jnp.where(odd_x, 0, bx + REACH) + k] = xr1[3 * WIDE + k]
        coef[jnp.where(odd_x, bx + REACH, 0) + k] = xr2[3 * WIDE + k]

    def fill(x, carry):
        for c in range(3):
            field[c, x + WIDE, 0:by, :] = disp[c, x]
        coef[x + REACH] = cell_coef(density[x], flags[x], trim[x])
        return carry

    lax.fori_loop(0, bx, fill, 0)

    def place(x):
        low = jnp.where(x < WIDE, x + bx + WIDE, x)
        swapped = jnp.where(x >= bx + WIDE, x - bx - WIDE, low)
        return jnp.where(odd_x, x, swapped)

    def rim(x, carry):
        for c in range(3):
            field[c, x, by : by + 8, :] = rim_tile(yr1, yr2, c * planes + place(x), odd_y)
        return carry

    lax.fori_loop(0, planes, rim, 0)
    zlow[...] = jnp.where(odd_z, zr1[...], zr2[...])
    zhigh[...] = jnp.where(odd_z, zr2[...], zr1[...])

    def plane(x, slot):
        spot = place(x)
        to_first = lax.rem(LANES - spot, LANES)
        to_last = LANES - 1 - spot
        for c in range(3):
            for t in range(by // 8 + 1):
                rows = slice(8 * t, 8 * t + 8)
                mid = field[c, x, rows, :]
                low = pltpu.roll(zlow[c, rows, :], to_first, 1)
                high = pltpu.roll(zhigh[c, rows, :], to_last, 1)
                low = jnp.where(lane == 0, low, pltpu.roll(mid, 1, 1))
                high = jnp.where(lane == LANES - 1, high, pltpu.roll(mid, LANES - 1, 1))
                for k, v in enumerate(triple(low, mid, high)):
                    along[3 * c + k, 8 * t + 8 : 8 * t + 16, :] = v
                    if t == by // 8:
                        along[3 * c + k, 0:8, :] = v
        at = jnp.maximum(x - 2, 0)
        for t in range(by // 8):
            rows = slice(8 * t, 8 * t + 8)
            fields = []
            for c in range(3):
                now = {}
                for k, z in enumerate("MDS"):
                    three = [along[3 * c + k, 8 * t + 7 + o : 8 * t + 15 + o, :] for o in range(3)]
                    if z == "S":
                        now["MS"], now["DS"] = pair(*three)
                    else:
                        now["M" + z], now["D" + z], now["S" + z] = triple(*three)
                held = {}
                for k, key in enumerate(YZ):
                    f = 8 * c + k
                    held[key] = ring[slot, f, rows, :], ring[1 - slot, f, rows, :], now[key]
                for k, key in enumerate(YZ):
                    ring[slot, 8 * c + k, rows, :] = now[key]
                fields.append(held)
            source[at, rows, :] = coef[at, rows, :] * energy_of(fields)

    def planes_two(k, carry):
        plane(2 * k, 0)
        plane(2 * k + 1, 1)
        return carry

    lax.fori_loop(0, planes // 2, planes_two, 0)

    def rows_out(q, carry):
        top = row < 4
        first, second = source[2 * q, 0:8, :], source[2 * q + 1, 0:8, :]
        low = jnp.where(top, first, half_turn(second))
        first, second = source[2 * q, by - 8 : by, :], source[2 * q + 1, by - 8 : by, :]
        high = jnp.where(top, half_turn(first), second)
        ys1[q] = jnp.where(odd_y, low, high)
        ys2[q] = jnp.where(odd_y, high, low)
        return carry

    lax.fori_loop(0, cells // 2, rows_out, 0)
    pack_columns(source, packed, by)


def pack_columns(source, packed, count):
    cells = source.shape[0]
    row = row_ids()
    for y in range(count):
        tall = jnp.concatenate([source[:, y, :], jnp.zeros((LANES - cells, LANES), F32)], axis=0)
        flat = tall.T
        packed[y] = jnp.where(row < 4, flat[0:8], flat[LANES - 8 : LANES])


def corner_kernel(yr1, yr2, packed, rim, rim_packed, zs1, zs2):
    by = packed.shape[0]
    odd_y, odd_z = is_odd("gy"), is_odd("gz")
    top = row_ids() < 4

    def unpack(q, carry):
        high = jnp.where(odd_y, yr2[q], yr1[q])
        low = jnp.where(odd_y, yr1[q], yr2[q])
        rim[2 * q] = jnp.where(top, high, half_turn(low))
        rim[2 * q + 1] = jnp.where(top, half_turn(high), low)
        return carry

    lax.fori_loop(0, yr1.shape[0], unpack, 0)
    pack_columns(rim, rim_packed, 8)

    def send(m, first, second):
        low = jnp.where(top, first, half_turn(second))
        high = jnp.where(top, half_turn(first), second)
        zs1[m] = jnp.where(odd_z, low, high)
        zs2[m] = jnp.where(odd_z, high, low)

    for m in range(by // 2):
        send(m, packed[2 * m], packed[2 * m + 1])
    for m in range(4):
        send(by // 2 + m, rim_packed[2 * m], rim_packed[2 * m + 1])


def filter_kernel(
    source, rim, packed, rim_packed, zr1, zr2, filtered, partial,
    work, low_strip, high_strip, strips, ends,
):
    cells, by, _ = source.shape
    bx = cells - 2 * REACH
    tall = by + 8
    odd_z = is_odd("gz")
    lane, row = lane_ids(), row_ids()
    top = row < 4
    first_x, last_x = lax.axis_index("gx") == 0, lax.axis_index("gx") == lax.axis_size("gx") - 1
    first_y, last_y = lax.axis_index("gy") == 0, lax.axis_index("gy") == lax.axis_size("gy") - 1
    first_z, last_z = lax.axis_index("gz") == 0, lax.axis_index("gz") == lax.axis_size("gz") - 1

    for m in range(tall // 2):
        low = jnp.where(odd_z, zr1[m], zr2[m])
        high = jnp.where(odd_z, zr2[m], zr1[m])
        for part in range(2):
            y = 2 * m + part
            own = half_turn(packed[y] if y < by else rim_packed[y - by])
            low_strip[y] = jnp.where(top, half_turn(low) if part else low, own)
            high_strip[y] = jnp.where(top, own, high if part else half_turn(high))

    inside_x = jnp.logical_not(
        jnp.logical_or(
            jnp.logical_and(first_x, lane < REACH),
            jnp.logical_and(last_x, lane >= bx + REACH),
        )
    )
    inside_low = jnp.logical_and(inside_x, jnp.logical_not(jnp.logical_and(first_z, top)))
    inside_high = jnp.logical_and(
        inside_x, jnp.logical_not(jnp.logical_and(last_z, jnp.logical_not(top)))
    )
    for side, strip, edge_row, inside in (
        (0, low_strip, 3, inside_low),
        (1, high_strip, 4, inside_high),
    ):
        strips[0] = POLY[4] * strip[...]
        for k in range(4):
            now, later = k % 2, (k + 1) % 2
            for t in range(tall // 8):
                ends[k, side, 8 * t : 8 * t + 8, :] = strips[now, 8 * t : 8 * t + 8, edge_row, :]
            if k == 3:
                break
            for y in range(tall):
                mid = strips[now, y]
                total = strips[now, (y + 1) % tall] + strips[now, (y - 1) % tall]
                total = total + (pltpu.roll(mid, 1, 1) + pltpu.roll(mid, LANES - 1, 1))
                total = total + (pltpu.roll(mid, 1, 0) + pltpu.roll(mid, 7, 0))
                total = total + POLY[3 - k] * strip[y]
                outside = first_y if y >= by + 4 else last_y
                keep = inside
                if y >= by:
                    keep = jnp.logical_and(inside, jnp.logical_not(outside))
                strips[later, y] = jnp.where(keep, total, 0.0)

    def put(slot, x, t, value):
        work[slot, x, 8 * t + 8 : 8 * t + 16, :] = value
        if t == by // 8:
            work[slot, x, 0:8, :] = value
        if t == 0:
            work[slot, x, by + 16 : by + 24, :] = value

    def begin(x, carry):
        for t in range(by // 8):
            put(0, x, t, POLY[4] * source[x, 8 * t : 8 * t + 8, :])
        put(0, x, by // 8, POLY[4] * rim[x])
        return carry

    lax.fori_loop(0, cells, begin, 0)
    rim_keep = jnp.logical_not(
        jnp.logical_or(
            jnp.logical_and(last_y, top), jnp.logical_and(first_y, jnp.logical_not(top))
        )
    )
    tiles = by // 8
    for k in range(4):
        now, later = k % 2, (k + 1) % 2

        def sweep(x, total, k=k, now=now, later=later):
            to_first = lax.rem(LANES - x, LANES)
            to_last = LANES - 1 - x
            for t in range(tiles + (k < 3)):
                at = 8 * t + 8
                mid = work[now, x, at : at + 8, :]
                value = work[now, x - 1, at : at + 8, :] + work[now, x + 1, at : at + 8, :]
                value = value + (
                    work[now, x, at - 1 : at + 7, :] + work[now, x, at + 1 : at + 9, :]
                )
                low = pltpu.roll(ends[k, 0, 8 * t : 8 * t + 8, :], to_first, 1)
                high = pltpu.roll(ends[k, 1, 8 * t : 8 * t + 8, :], to_last, 1)
                low = jnp.where(lane == 0, low, pltpu.roll(mid, 1, 1))
                high = jnp.where(lane == LANES - 1, high, pltpu.roll(mid, LANES - 1, 1))
                value = value + (low + high)
                own = source[x, 8 * t : 8 * t + 8, :] if t < tiles else rim[x]
                value = value + POLY[3 - k] * own
                if k == 3:
                    filtered[x - REACH, 8 * t : 8 * t + 8, :] = value
                    total = total + jnp.abs(value)
                else:
                    if t == tiles:
                        value = jnp.where(rim_keep, value, 0.0)
                    put(later, x, t, value)
            return total

        total = lax.fori_loop(k + 1, cells - 1 - k, sweep, jnp.zeros((8, LANES), F32))
        if k < 3:

            @pl.when(first_x)
            def _(later=later):
                work[later, 0:REACH] = jnp.zeros((REACH,) + work.shape[2:], F32)

            @pl.when(last_x)
            def _(later=later):
                work[later, bx + REACH : cells] = jnp.zeros((REACH,) + work.shape[2:], F32)

    partial[...] = jnp.broadcast_to(jnp.sum(total, axis=0, keepdims=True), partial.shape)


def project_kernel(count, density, filtered, sums, projected):
    scale = jnp.sum(sums[...]) / count + 1e-06
    inverse = jnp.full((8, LANES), 1.0, F32) / scale
    lower = math.tanh(SHARPNESS * THRESHOLD)
    bottom = lower + math.tanh(SHARPNESS * (1.0 - THRESHOLD))

    def one(x, carry):
        for t in range(density.shape[1] // 8):
            rows = slice(8 * t, 8 * t + 8)
            trial = density[x, rows, :] - STEP_SIZE * (filtered[x, rows, :] * inverse + 1.0)
            level = lower + jnp.tanh(SHARPNESS * (trial - THRESHOLD))
            projected[x, rows, :] = level * (1.0 / bottom)
        return carry

    lax.fori_loop(0, density.shape[0], one, 0)


def call(kernel, outs, scratch=()):
    return pl.pallas_call(
        kernel,
        out_shape=[jax.ShapeDtypeStruct(s, F32) for s in outs],
        out_specs=[VMEM] * len(outs),
        scratch_shapes=[pltpu.VMEM(s, F32) for s in scratch],
        compiler_params=pltpu.CompilerParams(**PARAMS),
    )


def body(displacement, density, cell_flags, trim_level):
    bx, by, bz = density.shape
    assert bz == LANES and bx + 2 * WIDE <= LANES
    planes, cells, tall = bx + 2 * WIDE, bx + 2 * REACH, by + 8

    odd_x, odd_y = is_odd("gx"), is_odd("gy")

    def x_face(at_low):
        start = jnp.where(at_low, 0, bx - WIDE)
        near = lax.dynamic_slice_in_dim(displacement, start, WIDE, 1)
        start = jnp.where(at_low, 0, bx - REACH)
        near_coef = cell_coef(
            *(lax.dynamic_slice_in_dim(v, start, REACH, 0) for v in (density, cell_flags, trim_level))
        )
        return jnp.concatenate([near.reshape(3 * WIDE, by, bz), near_coef], axis=0)

    xr1, xr2 = swap(x_face(odd_x), x_face(jnp.logical_not(odd_x)), "gx")

    def y_face(at_low):
        start = jnp.where(at_low, 0, by - 1)
        parts = [xr1[: 3 * WIDE].reshape(3, WIDE, by, bz), displacement]
        parts.append(xr2[: 3 * WIDE].reshape(3, WIDE, by, bz))
        parts = [lax.dynamic_slice_in_dim(p, start, 1, 2)[:, :, 0, :] for p in parts]
        return jnp.concatenate(parts, axis=1).reshape(3 * planes, bz)

    yr1, yr2 = swap(y_face(odd_y), y_face(jnp.logical_not(odd_y)), "gy")
    zs1, zs2 = call(ends_kernel, [(3, tall, LANES)] * 2)(displacement, xr1, xr2, yr1, yr2)
    zr1, zr2 = swap(zs1, zs2, "gz")
    source, ys1, ys2, packed = call(
        source_kernel,
        [(cells, by, LANES), (cells // 2, 8, LANES), (cells // 2, 8, LANES), (by, 8, LANES)],
        [
            (3, planes, tall, LANES),
            (cells, by, LANES),
            (3, tall, LANES),
            (3, tall, LANES),
            (9, by + 16, LANES),
            (2, 24, by, LANES),
        ],
    )(displacement, density, cell_flags, trim_level, xr1, xr2, yr1, yr2, zr1, zr2)
    yr1, yr2 = swap(ys1, ys2, "gy")
    rim, rim_packed, zs1, zs2 = call(
        corner_kernel,
        [(cells, 8, LANES), (8, 8, LANES), (tall // 2, 8, LANES), (tall // 2, 8, LANES)],
    )(yr1, yr2, packed)
    zr1, zr2 = swap(zs1, zs2, "gz")
    devices = lax.axis_size(AXES)
    filtered, partial = call(
        filter_kernel,
        [(bx, by, LANES), (devices, LANES)],
        [
            (2, cells, by + 24, LANES),
            (tall, 8, LANES),
            (tall, 8, LANES),
            (2, tall, 8, LANES),
            (4, 2, tall, LANES),
        ],
    )(source, rim, packed, rim_packed, zr1, zr2)
    sums = lax.all_to_all(partial, AXES, split_axis=0, concat_axis=0, tiled=True)
    count = float(filtered.size * devices)
    (projected,) = call(functools.partial(project_kernel, count), [(bx, by, LANES)])(
        density, filtered, sums
    )
    return projected, filtered


def solution(mesh):
    return jax.shard_map(
        body,
        mesh=mesh,
        in_specs=(P(None, *AXES), P(*AXES), P(*AXES), P(*AXES)),
        out_specs=(P(*AXES), P(*AXES)),
        check_vma=False,
    )
```

time: 381 us -> 153 us (0.40); the launches traced: 374 us -> 153 us
  blocking collectives: 164 us -> 32.1 us
  other arithmetic: 83.1 us -> 1.14 us
  Pallas kernels: 0 us -> 70.6 us
  waiting for transfers between devices: 54.6 us -> 12.2 us
  local copies, waits for them, and re-layouts: 25.9 us -> 5.39 us
  starting transfers between devices: 44.7 us -> 30.6 us
    psum x1 -> x0, blocking collectives: 102 us -> none  [body(): total = lax.psum(jnp.sum(jnp.abs(filtered)), ('gx', 'gy', 'gz'))]
    pallas_call x0 -> x5, Pallas kernels: none -> 70.6 us  [the longest x1 31.2 us: body(): call(filter_kernel, [(bx, by, LANES), (devices, LANES)], [(2, cells, by +...]
    ppermute x14 -> x10, waiting for transfers between devices: 54.6 us -> 12.2 us  [the longest x5 7.82 us: swap(): got_first = lax.ppermute(first, axis, even)]
    mul x1, other arithmetic: 38 us -> 1.06 us  [cell_coef(): return -3.0 * density * density * density * share]
    add x16 -> x0, other arithmetic: 31.4 us -> none  [the longest x12 27 us: spline_pass(): total + weights[2] * lax.slice_in_dim(field, 2, length + 2, axis=axis)]
    all_to_all x2 -> x1, blocking collectives: 61.6 us -> 32.1 us  [body(): lax.all_to_all(partial, AXES, split_axis=0, concat_axis=0, tiled=True)]
    ppermute x14 -> x10, starting transfers between devices: 44.7 us -> 30.6 us  [the longest x5 19.1 us: swap(): lax.ppermute(second, axis, odd)]
    slice x9 -> x2, local copies, waits for them, and re-layouts: 13.2 us -> 0.03 us  [the longest x1 0.02 us: y_face(): parts.append(xr2[:3 * WIDE].reshape(3, WIDE, by, bz))]
  transfers between devices with their start and end apart: 14 -> 10, of which waited for: 12 -> 5; matrix products, arithmetic and copies ran while one was open for 3% -> 1% of each run, Pallas kernels for 0% -> 0%
where the time goes in v1:
time: 153 us
  Pallas kernels  70.6 us (46%)
  blocking collectives  32.1 us (21%)
  starting transfers between devices  30.6 us (20%)
  waiting for transfers between devices  12.2 us (8%)
  local copies, waits for them, and re-layouts  5.39 us (4%)
    all_to_all x1, blocking collectives, body(): lax.all_to_all(partial, AXES, split_axis=0, concat_axis=0, tiled=True)  32.1 us
    pallas_call x1, Pallas kernels, body(): call(filter_kernel, [(bx, by, LANES), (devices, LANES)], [(2, cells, by +...  31.2 us
    pallas_call x1, Pallas kernels, body(): call(source_kernel, [(cells, by, LANES), (cells // 2, 8, LANES), (cells /...  27.4 us
    ppermute x5, starting transfers between devices, swap(): lax.ppermute(second, axis, odd)  19.1 us
    ppermute x5, starting transfers between devices, swap(): got_first = lax.ppermute(first, axis, even)  11.5 us
    ppermute x5, waiting for transfers between devices, swap(): got_first = lax.ppermute(first, axis, even)  7.82 us
    pallas_call x1, Pallas kernels, body(): call(ends_kernel, [(3, tall, LANES)] * 2)(displacement, xr1, xr2, yr1, yr2)  6.08 us
    ppermute x5, waiting for transfers between devices, swap(): lax.ppermute(second, axis, odd)  4.39 us
  transfers between devices with their start and end apart: 10, of which 5 were waited for; matrix products, arithmetic and copies ran while one was open for 1% of the time, Pallas kernels for 0%

profile of v1, /device:TPU:1, one launch (start us, length us, event | category | flops | bytes accessed | tf_op | source)
XLA Modules:
  0.0 152.9 jit_solution(1255983883093126712)
XLA Ops:
  0.6 1.1 constant_dynamic-slice_fusion.5
  1.8 1.1 fusion.1
  2.8 2.2 %collective-permute-start = (f32[19,32,128]{2,1,0:T(8,128)S(1)}, f32[19,32,128]{2,1,0:T(8,128)S(1)}, u32[]{:S(2)}, u32[]{:S(2)}) collective-permute-start(f32[19,32,128]{2,1,0:T(8,128)S(1)} %pad_maximum_fusion), channel_id=1, source_target_pairs={{0,16},{16,0},{32,48},{48,32},{64,80},{80,64},{96,112},{112,96},{1... | collective-permute-start | bytes 933896 | tf_op jit(solution)/shard_map/ppermute | solution.py:43
  5.1 0.7 collective-permute-start.1
  5.8 1.5 %constant_dynamic-slice_fusion.6 = (f32[3,64,1,128]{3,2,1,0:T(1,128)S(1)}, f32[3,64,1,128]{3,2,1,0:T(1,128)S(1)}) fusion(f32[3,64,32,128]{3,2,1,0:T(8,128)} %disp.3, s32[]{:T(128)S(6)} %select_n.56, s32[]{:T(128)S(6)} %select_n.55), kind=kLoop, calls=%fused_computation.18 | loop fusion | bytes 393224 | tf_op jit(solution)/shard_map/dynamic_slice | solution.py:475
  7.3 3.6 %collective-permute-done.xr1 = f32[19,32,128]{2,1,0:T(8,128)S(1)} collective-permute-done((f32[19,32,128]{2,1,0:T(8,128)S(1)}, f32[19,32,128]{2,1,0:T(8,128)S(1)}, u32[]{:S(2)}, u32[]{:S(2)}) %collective-permute-start) | collective-permute-done | bytes 311328 | tf_op jit(solution)/shard_map/ppermute | solution.py:43
  10.9 0.0 collective-permute-done.1.xr2
  10.9 0.0 copy-start.1
  11.2 0.7 collective-permute-start.3
  11.9 4.8 %collective-permute-start.2 = (f32[222,128]{1,0:T(8,128)S(1)}, f32[222,128]{1,0:T(8,128)S(1)}, u32[]{:S(2)}, u32[]{:S(2)}) collective-permute-start(f32[222,128]{1,0:T(8,128)S(1)} %reshape.30), channel_id=1, source_target_pairs={{0,4},{4,0},{8,12},{12,8},{1,5},{5,1},{9,13},{13,9},{2,6},{6,2},{1... | collective-permute-start | bytes 341000 | tf_op jit(solution)/shard_map/ppermute | solution.py:43
  16.7 0.0 collective-permute-done.3.yr2
  16.7 2.2 %collective-permute-done.2.yr1 = f32[222,128]{1,0:T(8,128)S(1)} collective-permute-done((f32[222,128]{1,0:T(8,128)S(1)}, f32[222,128]{1,0:T(8,128)S(1)}, u32[]{:S(2)}, u32[]{:S(2)}) %collective-permute-start.2) | collective-permute-done | bytes 113696 | tf_op jit(solution)/shard_map/ppermute | solution.py:43
  18.9 0.6 copy-done.3
  19.6 6.1 %shard_map.59 = (f32[3,40,128]{2,1,0:T(8,128)}, f32[3,40,128]{2,1,0:T(8,128)}) custom-call(f32[3,64,32,128]{3,2,1,0:T(8,128)} %disp.3, f32[19,32,128]{2,1,0:T(8,128)} %copy-done, f32[19,32,128]{2,1,0:T(8,128)} %copy-done.1, f32[222,128]{1,0:T(8,128)} %copy-done.3, f32[222,128]{1,0:T(8,128)} %copy-done.2), custom_call_target="tpu_custom_call" | custom-call | tf_op jit(solution)/shard_map/pallas_call | solution.py:479
  25.6 2.7 %collective-permute-start.4 = (f32[3,40,128]{2,1,0:T(8,128)}, f32[3,40,128]{2,1,0:T(8,128)S(1)}, u32[]{:S(2)}, u32[]{:S(2)}) collective-permute-start(f32[3,40,128]{2,1,0:T(8,128)} %get-tuple-element.14), channel_id=1, source_target_pairs={{0,1},{1,0},{2,3},{3,2},{4,5},{5,4},{6,7},{7,6},{8,9},{9,8},{10,11... | collective-permute-start | bytes 184328 | tf_op jit(solution)/shard_map/ppermute | solution.py:43
  28.3 8.7 %collective-permute-start.5 = (f32[3,40,128]{2,1,0:T(8,128)}, f32[3,40,128]{2,1,0:T(8,128)S(1)}, u32[]{:S(2)}, u32[]{:S(2)}) collective-permute-start(f32[3,40,128]{2,1,0:T(8,128)} %get-tuple-element.15), channel_id=1, source_target_pairs={{1,2},{2,1},{5,6},{6,5},{9,10},{10,9},{13,14},{14,13},{17,18},{18,... | collective-permute-start | bytes 184328 | tf_op jit(solution)/shard_map/ppermute | solution.py:44
  37.1 2.1 %collective-permute-done.5.zr2 = f32[3,40,128]{2,1,0:T(8,128)S(1)} collective-permute-done((f32[3,40,128]{2,1,0:T(8,128)}, f32[3,40,128]{2,1,0:T(8,128)S(1)}, u32[]{:S(2)}, u32[]{:S(2)}) %collective-permute-start.5) | collective-permute-done | bytes 61472 | tf_op jit(solution)/shard_map/ppermute | solution.py:44
  39.1 0.6 copy-done.9
  39.8 27.4 %shard_map.60 = (f32[72,32,128]{2,1,0:T(8,128)}, f32[36,8,128]{2,1,0:T(8,128)}, f32[36,8,128]{2,1,0:T(8,128)}, f32[32,8,128]{2,1,0:T(8,128)}) custom-call(f32[3,64,32,128]{3,2,1,0:T(8,128)} %disp.3, f32[64,32,128]{2,1,0:T(8,128)} %density.3, s32[64,32,128]{2,1,0:T(8,128)} %flags.1, s32[64,32,128]{2,1,0:T(8,128)} %trim.1, f32[19,32,128]{2,1,0:T(8,128)} %copy-done, ...), custom_call_target="tpu_custom_call" | custom-call | tf_op jit(solution)/shard_map/pallas_call | solution.py:481
  67.2 1.7 %collective-permute-start.6 = (f32[36,8,128]{2,1,0:T(8,128)}, f32[36,8,128]{2,1,0:T(8,128)S(1)}, u32[]{:S(2)}, u32[]{:S(2)}) collective-permute-start(f32[36,8,128]{2,1,0:T(8,128)} %get-tuple-element.17), channel_id=1, source_target_pairs={{0,4},{4,0},{8,12},{12,8},{1,5},{5,1},{9,13},{13,9},{2,6},{6,2},{1... | collective-permute-start | bytes 442376 | tf_op jit(solution)/shard_map/ppermute | solution.py:43
  68.9 0.7 collective-permute-start.7
  69.6 2.1 %collective-permute-done.6.yr1 = f32[36,8,128]{2,1,0:T(8,128)S(1)} collective-permute-done((f32[36,8,128]{2,1,0:T(8,128)}, f32[36,8,128]{2,1,0:T(8,128)S(1)}, u32[]{:S(2)}, u32[]{:S(2)}) %collective-permute-start.6) | collective-permute-done | bytes 147488 | tf_op jit(solution)/shard_map/ppermute | solution.py:43
  71.7 0.7 copy-done.4
  72.3 0.1 copy-done.5
  72.4 2.2 %shard_map.61 = (f32[72,8,128]{2,1,0:T(8,128)}, f32[8,8,128]{2,1,0:T(8,128)}, f32[20,8,128]{2,1,0:T(8,128)}, f32[20,8,128]{2,1,0:T(8,128)}) custom-call(f32[36,8,128]{2,1,0:T(8,128)} %copy-done.4, f32[36,8,128]{2,1,0:T(8,128)} %copy-done.5, f32[32,8,128]{2,1,0:T(8,128)} %get-tuple-element.19.packed), custom_call_target="tpu_custom_call" | custom-call | tf_op jit(solution)/shard_map/pallas_call | solution.py:494
  74.6 0.0 collective-permute-start.8
  74.6 8.4 %collective-permute-start.9 = (f32[20,8,128]{2,1,0:T(8,128)}, f32[20,8,128]{2,1,0:T(8,128)S(1)}, u32[]{:S(2)}, u32[]{:S(2)}) collective-permute-start(f32[20,8,128]{2,1,0:T(8,128)} %get-tuple-element.23), channel_id=1, source_target_pairs={{1,2},{2,1},{5,6},{6,5},{9,10},{10,9},{13,14},{14,13},{17,18},{18,... | collective-permute-start | bytes 245768 | tf_op jit(solution)/shard_map/ppermute | solution.py:44
  83.0 2.3 %collective-permute-done.9.zr2 = f32[20,8,128]{2,1,0:T(8,128)S(1)} collective-permute-done((f32[20,8,128]{2,1,0:T(8,128)}, f32[20,8,128]{2,1,0:T(8,128)S(1)}, u32[]{:S(2)}, u32[]{:S(2)}) %collective-permute-start.9) | collective-permute-done | bytes 81952 | tf_op jit(solution)/shard_map/ppermute | solution.py:44
  85.3 0.6 copy-done.7
  85.9 31.2 %shard_map.62 = (f32[64,32,128]{2,1,0:T(8,128)}, f32[256,128]{1,0:T(8,128)}) custom-call(f32[72,32,128]{2,1,0:T(8,128)} %get-tuple-element.16.source, f32[72,8,128]{2,1,0:T(8,128)} %get-tuple-element.20.rim, f32[32,8,128]{2,1,0:T(8,128)} %get-tuple-element.19.packed, f32[8,8,128]{2,1,0:T(8,128)} %get-tuple-element.21.rim_packed, f32[20,8,128]{2,1,0:T(8,128)} %copy-done.6, ...), custom_call_target="tpu_custom_call" | custom-call | tf_op jit(solution)/shard_map/pallas_call | solution.py:500
  117.1 32.1 %all_to_all.11 = f32[256,1,128]{2,1,0:T(1,128)} all-to-all(f32[256,1,128]{2,1,0:T(1,128)} %bitcast.29), channel_id=1, replica_groups=mesh['gx'=16,'gy'=4,'gz'=4] {'gx','gy','gz'}, dimensions={0} | all-to-all | bytes 262144 | tf_op jit(solution)/shard_map/all_to_all | solution.py:511
  149.1 3.7 %shard_map.63 = f32[64,32,128]{2,1,0:T(8,128)} custom-call(f32[64,32,128]{2,1,0:T(8,128)} %density.3, f32[64,32,128]{2,1,0:T(8,128)} %get-tuple-element.13.filtered, f32[256,128]{1,0:T(8,128)} %bitcast.24), custom_call_target="tpu_custom_call" | custom-call | tf_op jit(solution)/shard_map/pallas_call | solution.py:513
  (34 shorter events, 0.2 us)
Async XLA Ops:
  2.8 8.0 %collective-permute-start = (f32[19,32,128]{2,1,0:T(8,128)S(1)}, f32[19,32,128]{2,1,0:T(8,128)S(1)}, u32[]{:S(2)}, u32[]{:S(2)}) collective-permute-start(f32[19,32,128]{2,1,0:T(8,128)S(1)} %pad_maximum_fusion), channel_id=1, source_target_pairs={{0,16},{16,0},{32,48},{48,32},{64,80},{80,64},{96,112},{112,96},{1... | collective-permute-start | bytes 933896 | tf_op jit(solution)/shard_map/ppermute | solution.py:43
  5.1 5.8 %collective-permute-start.1 = (f32[19,32,128]{2,1,0:T(8,128)S(1)}, f32[19,32,128]{2,1,0:T(8,128)S(1)}, u32[]{:S(2)}, u32[]{:S(2)}) collective-permute-start(f32[19,32,128]{2,1,0:T(8,128)S(1)} %pad_maximum_fusion.1), channel_id=1, source_target_pairs={{16,32},{32,16},{48,64},{64,48},{80,96},{96,80},{112,128},{128,112... | collective-permute-start | bytes 933896 | tf_op jit(solution)/shard_map/ppermute | solution.py:44
  10.9 8.0 %copy-start = (f32[19,32,128]{2,1,0:T(8,128)}, f32[19,32,128]{2,1,0:T(8,128)S(1)}, u32[]{:S(2)}) copy-start(f32[19,32,128]{2,1,0:T(8,128)S(1)} %collective-permute-done.xr1) | copy-start | bytes 933892
  10.9 8.0 %copy-start.1 = (f32[19,32,128]{2,1,0:T(8,128)}, f32[19,32,128]{2,1,0:T(8,128)S(1)}, u32[]{:S(2)}) copy-start(f32[19,32,128]{2,1,0:T(8,128)S(1)} %collective-permute-done.1.xr2) | copy-start | bytes 933892
  11.2 5.5 %collective-permute-start.3 = (f32[222,128]{1,0:T(8,128)S(1)}, f32[222,128]{1,0:T(8,128)S(1)}, u32[]{:S(2)}, u32[]{:S(2)}) collective-permute-start(f32[222,128]{1,0:T(8,128)S(1)} %reshape.31), channel_id=1, source_target_pairs={{4,8},{8,4},{5,9},{9,5},{6,10},{10,6},{7,11},{11,7},{20,24},{24,20... | collective-permute-start | bytes 341000 | tf_op jit(solution)/shard_map/ppermute | solution.py:44
  11.9 7.0 %collective-permute-start.2 = (f32[222,128]{1,0:T(8,128)S(1)}, f32[222,128]{1,0:T(8,128)S(1)}, u32[]{:S(2)}, u32[]{:S(2)}) collective-permute-start(f32[222,128]{1,0:T(8,128)S(1)} %reshape.30), channel_id=1, source_target_pairs={{0,4},{4,0},{8,12},{12,8},{1,5},{5,1},{9,13},{13,9},{2,6},{6,2},{1... | collective-permute-start | bytes 341000 | tf_op jit(solution)/shard_map/ppermute | solution.py:43
  16.7 2.2 %copy-start.2 = (f32[222,128]{1,0:T(8,128)}, f32[222,128]{1,0:T(8,128)S(1)}, u32[]{:S(2)}) copy-start(f32[222,128]{1,0:T(8,128)S(1)} %collective-permute-done.3.yr2) | copy-start | bytes 340996
  18.9 0.7 copy-start.3
  25.6 11.4 %collective-permute-start.4 = (f32[3,40,128]{2,1,0:T(8,128)}, f32[3,40,128]{2,1,0:T(8,128)S(1)}, u32[]{:S(2)}, u32[]{:S(2)}) collective-permute-start(f32[3,40,128]{2,1,0:T(8,128)} %get-tuple-element.14), channel_id=1, source_target_pairs={{0,1},{1,0},{2,3},{3,2},{4,5},{5,4},{6,7},{7,6},{8,9},{9,8},{10,11... | collective-permute-start | bytes 184328 | tf_op jit(solution)/shard_map/ppermute | solution.py:43
  28.3 10.8 %collective-permute-start.5 = (f32[3,40,128]{2,1,0:T(8,128)}, f32[3,40,128]{2,1,0:T(8,128)S(1)}, u32[]{:S(2)}, u32[]{:S(2)}) collective-permute-start(f32[3,40,128]{2,1,0:T(8,128)} %get-tuple-element.15), channel_id=1, source_target_pairs={{1,2},{2,1},{5,6},{6,5},{9,10},{10,9},{13,14},{14,13},{17,18},{18,... | collective-permute-start | bytes 184328 | tf_op jit(solution)/shard_map/ppermute | solution.py:44
  37.1 2.1 %copy-start.8 = (f32[3,40,128]{2,1,0:T(8,128)}, f32[3,40,128]{2,1,0:T(8,128)S(1)}, u32[]{:S(2)}) copy-start(f32[3,40,128]{2,1,0:T(8,128)S(1)} %collective-permute-done.4.zr1) | copy-start | bytes 184324
  39.1 0.6 copy-start.9
  67.2 4.5 %collective-permute-start.6 = (f32[36,8,128]{2,1,0:T(8,128)}, f32[36,8,128]{2,1,0:T(8,128)S(1)}, u32[]{:S(2)}, u32[]{:S(2)}) collective-permute-start(f32[36,8,128]{2,1,0:T(8,128)} %get-tuple-element.17), channel_id=1, source_target_pairs={{0,4},{4,0},{8,12},{12,8},{1,5},{5,1},{9,13},{13,9},{2,6},{6,2},{1... | collective-permute-start | bytes 442376 | tf_op jit(solution)/shard_map/ppermute | solution.py:43
  68.9 2.7 %collective-permute-start.7 = (f32[36,8,128]{2,1,0:T(8,128)}, f32[36,8,128]{2,1,0:T(8,128)S(1)}, u32[]{:S(2)}, u32[]{:S(2)}) collective-permute-start(f32[36,8,128]{2,1,0:T(8,128)} %get-tuple-element.18), channel_id=1, source_target_pairs={{4,8},{8,4},{5,9},{9,5},{6,10},{10,6},{7,11},{11,7},{20,24},{24,20... | collective-permute-start | bytes 442376 | tf_op jit(solution)/shard_map/ppermute | solution.py:44
  71.7 0.7 copy-start.4
  71.7 0.7 copy-start.5
  74.6 8.4 %collective-permute-start.8 = (f32[20,8,128]{2,1,0:T(8,128)}, f32[20,8,128]{2,1,0:T(8,128)S(1)}, u32[]{:S(2)}, u32[]{:S(2)}) collective-permute-start(f32[20,8,128]{2,1,0:T(8,128)} %get-tuple-element.22), channel_id=1, source_target_pairs={{0,1},{1,0},{2,3},{3,2},{4,5},{5,4},{6,7},{7,6},{8,9},{9,8},{10,11... | collective-permute-start | bytes 245768 | tf_op jit(solution)/shard_map/ppermute | solution.py:43
  74.6 10.7 %collective-permute-start.9 = (f32[20,8,128]{2,1,0:T(8,128)}, f32[20,8,128]{2,1,0:T(8,128)S(1)}, u32[]{:S(2)}, u32[]{:S(2)}) collective-permute-start(f32[20,8,128]{2,1,0:T(8,128)} %get-tuple-element.23), channel_id=1, source_target_pairs={{1,2},{2,1},{5,6},{6,5},{9,10},{10,9},{13,14},{14,13},{17,18},{18,... | collective-permute-start | bytes 245768 | tf_op jit(solution)/shard_map/ppermute | solution.py:44
  83.0 2.3 %copy-start.6 = (f32[20,8,128]{2,1,0:T(8,128)}, f32[20,8,128]{2,1,0:T(8,128)S(1)}, u32[]{:S(2)}) copy-start(f32[20,8,128]{2,1,0:T(8,128)S(1)} %collective-permute-done.8.zr1) | copy-start | bytes 245764
  85.3 0.6 copy-start.7

commit v2 on v1

--- a/solution.py
+++ b/solution.py
@@ -18,6 +18,7 @@
 
 AXES = ("gx", "gy", "gz")
 LANES = 128
+HALF = 64
 REACH = 4
 WIDE = REACH + 1
 
@@ -33,7 +34,7 @@
 
 F32 = jnp.float32
 VMEM = pl.BlockSpec(memory_space=pltpu.VMEM)
-PARAMS = dict(vmem_limit_bytes=56 * 1024 * 1024)
+PARAMS = dict(vmem_limit_bytes=20 * 1024 * 1024)
 
 
 def swap(first, second, axis):
@@ -74,40 +75,82 @@
     return jnp.where(jnp.logical_xor(at_top, odd), one, two)
 
 
-def ends_kernel(disp, xr1, xr2, yr1, yr2, zs1, zs2):
+def two_halves(first, second):
+    spare = HALF - first.shape[0]
+    if spare:
+        zero = jnp.zeros((spare, LANES), F32)
+        first = jnp.concatenate([first, zero], axis=0)
+        second = jnp.concatenate([second, zero], axis=0)
+    return jnp.concatenate([first, second], axis=0).T
+
+
+def faces_kernel(disp, low, high):
+    _, _, by, _ = disp.shape
+    n = by // 16
+    for c in range(3):
+        for y in range(by // 2):
+            turned = two_halves(disp[c, :, y, :], disp[c, :, y + by // 2, :])
+            low[c * n + y // 8, y % 8 : y % 8 + 1, :] = turned[0:1]
+            high[c * n + y // 8, y % 8 : y % 8 + 1, :] = turned[LANES - 1 : LANES]
+
+
+def ends_kernel(low, high, yr1, yr2, zs1, zs2):
+    odd_z = is_odd("gz")
+    n, bx = low.shape[0], yr1.shape[0] // 3
+    zs1[0:n] = jnp.where(odd_z, low[...], high[...])
+    zs2[0:n] = jnp.where(odd_z, high[...], low[...])
+    zs1[n] = jnp.zeros((8, LANES), F32)
+    zs2[n] = jnp.zeros((8, LANES), F32)
+    for c in range(3):
+        rows = slice(c * bx, c * bx + bx)
+        turned = two_halves(yr1[rows, :], yr2[rows, :])
+        near, far = turned[0:1], turned[LANES - 1 : LANES]
+        zs1[n, c : c + 1, :] = jnp.where(odd_z, near, far)
+        zs2[n, c : c + 1, :] = jnp.where(odd_z, far, near)
+
+
+def x_rows(by):
+    tall = by + 8
+    planes = 3 * WIDE * tall
+    coefs = planes + REACH * by
+    return planes, coefs, coefs + 2 * 3 * (by // 16 + 1) * 8
+
+
+def ends_tiles(by):
+    return 3 * (by // 16 + 1)
+
+
+def outward_kernel(disp, density, flags, trim, yr1, yr2, zr1, zr2, xs1, xs2, rims):
     _, bx, by, _ = disp.shape
-    planes = bx + 2 * WIDE
-    odd_y, odd_z = is_odd("gy"), is_odd("gz")
-    lane = lane_ids()
-
-    def gather(tile_of, c, row):
-        low = jnp.zeros((8, LANES), F32)
-        high = jnp.zeros((8, LANES), F32)
-        for x in range(planes):
-            tile = tile_of(x)
-            here = lane == x
-            low = jnp.where(here, pltpu.roll(tile, x, 1) if x else tile, low)
-            high = jnp.where(here, pltpu.roll(tile, x + 1, 1), high)
-        zs1[c, pl.ds(row, 8), :] = jnp.where(odd_z, low, high)
-        zs2[c, pl.ds(row, 8), :] = jnp.where(odd_z, high, low)
-
-    for c in range(3):
-
-        def rows(t, carry, c=c):
-            row = pl.multiple_of(8 * t, 8)
-
-            def tile_of(x):
-                if x < WIDE:
-                    return xr1[c * WIDE + x, pl.ds(row, 8), :]
-                if x < WIDE + bx:
-                    return disp[c, x - WIDE, pl.ds(row, 8), :]
-                return xr2[c * WIDE + x - WIDE - bx, pl.ds(row, 8), :]
-
-            gather(tile_of, c, row)
-            return carry
-
-        lax.fori_loop(0, by // 8, rows, 0)
-        gather(lambda x, c=c: rim_tile(yr1, yr2, c * planes + x, odd_y), c, by)
+    tall, n = by + 8, by // 16
+    odd_x, odd_y, odd_z = is_odd("gx"), is_odd("gy"), is_odd("gz")
+    top_row, left = row_ids() == 0, lane_ids() < HALF
+    for side in range(2):
+        def pick(*at, side=side):
+            one, two = zr1[at], zr2[at]
+            return jnp.where(odd_z, two, one) if side else jnp.where(odd_z, one, two)
+
+        for c in range(3):
+            base = side * ends_tiles(by) + c * (n + 1)
+            for t in range(n):
+                rims[base + t] = pick(c * n + t)
+            both = jnp.broadcast_to(pick(3 * n, slice(c, c + 1), slice(None)), (8, LANES))
+            other = pltpu.roll(both, HALF, 1)
+            rims[base + n] = jnp.where(jnp.logical_xor(top_row, odd_y), both, other)
+    planes, coefs, _ = x_rows(by)
+    for out, at_low in ((xs1, odd_x), (xs2, jnp.logical_not(odd_x))):
+        start = jnp.where(at_low, 0, bx - WIDE)
+        for c in range(3):
+            for k in range(WIDE):
+                at = (c * WIDE + k) * tall
+                out[at : at + by, :] = disp[c, start + k]
+                out[at + by : at + tall, :] = rim_tile(yr1, yr2, c * bx + start + k, odd_y)
+        start = jnp.where(at_low, 0, bx - REACH)
+        for k in range(REACH):
+            x = start + k
+            out[planes + k * by : planes + (k + 1) * by, :] = cell_coef(density[x], flags[x], trim[x])
+        for j in range(2 * ends_tiles(by)):
+            out[coefs + 8 * j : coefs + 8 * j + 8, :] = rims[j]
 
 
 def triple(a, b, c):
@@ -169,90 +212,168 @@
 YZ = ("MM", "MD", "MS", "DM", "DD", "DS", "SM", "SD")
 
 
-def source_kernel(
-    disp, density, flags, trim, xr1, xr2, yr1, yr2, zr1, zr2,
+def z_pass(tile_of, low_of, high_of, along):
+    lane = lane_ids()
+    tiles = along.shape[1] // 8 - 1
+    for c in range(3):
+        for t in range(tiles):
+            mid = tile_of(c, t)
+            low = jnp.where(lane == 0, low_of(c, t), pltpu.roll(mid, 1, 1))
+            high = jnp.where(lane == LANES - 1, high_of(c, t), pltpu.roll(mid, LANES - 1, 1))
+            for k, v in enumerate(triple(low, mid, high)):
+                along[3 * c + k, 8 * t + 8 : 8 * t + 16, :] = v
+                if t == tiles - 1:
+                    along[3 * c + k, 0:8, :] = v
+
+
+def rim_shifts(by, t, spot, to_lane):
+    n = by // 16
+    if t == 2 * n:
+        return n, lax.rem(to_lane + LANES - spot, LANES)
+    return t % n, lax.rem(to_lane + 2 * LANES - spot - HALF * (t // n), LANES)
+
+
+def xy_pass(along, ring, slot, emit):
+    for t in range(along.shape[1] // 8 - 2):
+        rows = slice(8 * t, 8 * t + 8)
+        fields = []
+        for c in range(3):
+            now = {}
+            for k, z in enumerate("MDS"):
+                three = [along[3 * c + k, 8 * t + 7 + o : 8 * t + 15 + o, :] for o in range(3)]
+                if z == "S":
+                    now["MS"], now["DS"] = pair(*three)
+                else:
+                    now["M" + z], now["D" + z], now["S" + z] = triple(*three)
+            held = {}
+            for k, key in enumerate(YZ):
+                f = 8 * c + k
+                if emit is not None:
+                    held[key] = ring[slot, f, rows, :], ring[1 - slot, f, rows, :], now[key]
+                ring[slot, f, rows, :] = now[key]
+            fields.append(held)
+        if emit is not None:
+            emit(t, energy_of(fields))
+
+
+def inner_kernel(disp, density, flags, trim, yr1, yr2, rims, inner, along0, along1, ring):
+    _, bx, by, _ = disp.shape
+    odd_y = is_odd("gy")
+    tiles = by // 8
+
+    def along_z(x, along):
+        def tile_of(c, t):
+            if t < tiles:
+                return disp[c, x, 8 * t : 8 * t + 8, :]
+            return rim_tile(yr1, yr2, c * bx + x, odd_y)
+
+        def rim(side, to_lane):
+            def of(c, t):
+                tile, turn = rim_shifts(by, t, x, to_lane)
+                return pltpu.roll(rims[side * ends_tiles(by) + c * (by // 16 + 1) + tile], turn, 1)
+
+            return of
+
+        z_pass(tile_of, rim(0, 0), rim(1, LANES - 1), along)
+
+    def across(x, along, slot):
+        def emit(t, energy):
+            rows = slice(8 * t, 8 * t + 8)
+            at = jnp.maximum(x - 1, 0)
+            coef = cell_coef(density[at, rows, :], flags[at, rows, :], trim[at, rows, :])
+            inner[jnp.maximum(x - 2, 0), rows, :] = coef * energy
+
+        xy_pass(along, ring, slot, emit)
+
+    along_z(0, along0)
+
+    def planes_two(k, carry):
+        along_z(2 * k + 1, along1)
+        across(2 * k, along0, 0)
+        along_z(jnp.minimum(2 * k + 2, bx - 1), along0)
+        across(2 * k + 1, along1, 1)
+        return carry
+
+    lax.fori_loop(0, bx // 2, planes_two, 0)
+
+
+def outer_kernel(
+    disp, density, flags, trim, yr1, yr2, rims, xr1, xr2, inner,
     source, ys1, ys2, packed,
-    field, coef, zlow, zhigh, along, ring,
+    field, coef, ends, along0, along1, ring,
 ):
     _, bx, by, _ = disp.shape
-    planes = bx + 2 * WIDE
-    cells = bx + 2 * REACH
-    odd_x, odd_y, odd_z = is_odd("gx"), is_odd("gy"), is_odd("gz")
-    lane, row = lane_ids(), row_ids()
-
-    for k in range(WIDE):
+    cells, tall = bx + 2 * REACH, by + 8
+    planes, coefs, _ = x_rows(by)
+    count = WIDE + 2
+    odd_x, odd_y = is_odd("gx"), is_odd("gy")
+    row = row_ids()
+    for side in range(2):
+        def pick(at, size, side=side):
+            one, two = xr1[at : at + size, :], xr2[at : at + size, :]
+            return jnp.where(odd_x, two, one) if side else jnp.where(odd_x, one, two)
+
         for c in range(3):
-            field[c, jnp.where(odd_x, 0, bx + WIDE) + k, 0:by, :] = xr1[c * WIDE + k]
-            field[c, jnp.where(odd_x, bx + WIDE, 0) + k, 0:by, :] = xr2[c * WIDE + k]
-    for k in range(REACH):
-        coef[jnp.where(odd_x, 0, bx + REACH) + k] = xr1[3 * WIDE + k]
-        coef[jnp.where(odd_x, bx + REACH, 0) + k] = xr2[3 * WIDE + k]
-
-    def fill(x, carry):
-        for c in range(3):
-            field[c, x + WIDE, 0:by, :] = disp[c, x]
-        coef[x + REACH] = cell_coef(density[x], flags[x], trim[x])
+            for k in range(WIDE):
+                field[side, c, k + 2 * side] = pick((c * WIDE + k) * tall, tall)
+            for k in range(2):
+                x = bx - 2 + k if side else k
+                at = k if side else WIDE + k
+                field[side, c, at, 0:by, :] = disp[c, x]
+                field[side, c, at, by:tall, :] = rim_tile(yr1, yr2, c * bx + x, odd_y)
+        for k in range(REACH):
+            coef[side, k + side] = pick(planes + k * by, by)
+        x = bx - 1 if side else 0
+        coef[side, 0 if side else REACH] = cell_coef(density[x], flags[x], trim[x])
+        for j in range(2 * ends_tiles(by)):
+            ends[side, j] = pick(coefs + 8 * j, 8)
+    for j in range(2 * ends_tiles(by)):
+        ends[2, j] = rims[j]
+
+    def one_side(side, carry):
+        high_side = side == 1
+
+        def along_z(i, along):
+            low_whose = 2 if i >= WIDE else 0
+            low_spot = i - WIDE if i >= WIDE else bx - WIDE + i
+            high_whose = 2 if i < 2 else 1
+            high_spot = bx - 2 + i if i < 2 else i - 2
+            whose = jnp.where(high_side, high_whose, low_whose)
+            spot = jnp.where(high_side, high_spot, low_spot)
+
+            def rim(z_side, to_lane):
+                def of(c, t):
+                    tile, turn = rim_shifts(by, t, spot, to_lane)
+                    at = z_side * ends_tiles(by) + c * (by // 16 + 1) + tile
+                    return pltpu.roll(ends[whose, at], turn, 1)
+
+                return of
+
+            z_pass(
+                lambda c, t: field[side, c, i, 8 * t : 8 * t + 8, :],
+                rim(0, 0), rim(1, LANES - 1), along,
+            )
+
+        alongs = along0, along1
+        along_z(0, along0)
+        for i in range(count):
+            if i + 1 < count:
+                along_z(i + 1, alongs[(i + 1) % 2])
+
+            def emit(t, energy, i=i):
+                rows = slice(8 * t, 8 * t + 8)
+                source[side * (cells - WIDE) + i - 2, rows, :] = coef[side, i - 2, rows, :] * energy
+
+            xy_pass(alongs[i % 2], ring, i % 2, emit if i >= 2 else None)
         return carry
 
-    lax.fori_loop(0, bx, fill, 0)
-
-    def place(x):
-        low = jnp.where(x < WIDE, x + bx + WIDE, x)
-        swapped = jnp.where(x >= bx + WIDE, x - bx - WIDE, low)
-        return jnp.where(odd_x, x, swapped)
-
-    def rim(x, carry):
-        for c in range(3):
-            field[c, x, by : by + 8, :] = rim_tile(yr1, yr2, c * planes + place(x), odd_y)
+    lax.fori_loop(0, 2, one_side, 0)
+
+    def copy(x, carry):
+        source[x + WIDE] = inner[x]
         return carry
 
-    lax.fori_loop(0, planes, rim, 0)
-    zlow[...] = jnp.where(odd_z, zr1[...], zr2[...])
-    zhigh[...] = jnp.where(odd_z, zr2[...], zr1[...])
-
-    def plane(x, slot):
-        spot = place(x)
-        to_first = lax.rem(LANES - spot, LANES)
-        to_last = LANES - 1 - spot
-        for c in range(3):
-            for t in range(by // 8 + 1):
-                rows = slice(8 * t, 8 * t + 8)
-                mid = field[c, x, rows, :]
-                low = pltpu.roll(zlow[c, rows, :], to_first, 1)
-                high = pltpu.roll(zhigh[c, rows, :], to_last, 1)
-                low = jnp.where(lane == 0, low, pltpu.roll(mid, 1, 1))
-                high = jnp.where(lane == LANES - 1, high, pltpu.roll(mid, LANES - 1, 1))
-                for k, v in enumerate(triple(low, mid, high)):
-                    along[3 * c + k, 8 * t + 8 : 8 * t + 16, :] = v
-                    if t == by // 8:
-                        along[3 * c + k, 0:8, :] = v
-        at = jnp.maximum(x - 2, 0)
-        for t in range(by // 8):
-            rows = slice(8 * t, 8 * t + 8)
-            fields = []
-            for c in range(3):
-                now = {}
-                for k, z in enumerate("MDS"):
-                    three = [along[3 * c + k, 8 * t + 7 + o : 8 * t + 15 + o, :] for o in range(3)]
-                    if z == "S":
-                        now["MS"], now["DS"] = pair(*three)
-                    else:
-                        now["M" + z], now["D" + z], now["S" + z] = triple(*three)
-                held = {}
-                for k, key in enumerate(YZ):
-                    f = 8 * c + k
-                    held[key] = ring[slot, f, rows, :], ring[1 - slot, f, rows, :], now[key]
-                for k, key in enumerate(YZ):
-                    ring[slot, 8 * c + k, rows, :] = now[key]
-                fields.append(held)
-            source[at, rows, :] = coef[at, rows, :] * energy_of(fields)
-
-    def planes_two(k, carry):
-        plane(2 * k, 0)
-        plane(2 * k + 1, 1)
-        return carry
-
-    lax.fori_loop(0, planes // 2, planes_two, 0)
+    lax.fori_loop(0, bx - 2, copy, 0, unroll=4)
 
     def rows_out(q, carry):
         top = row < 4
@@ -264,7 +385,7 @@
         ys2[q] = jnp.where(odd_y, high, low)
         return carry
 
-    lax.fori_loop(0, cells // 2, rows_out, 0)
+    lax.fori_loop(0, cells // 2, rows_out, 0, unroll=6)
     pack_columns(source, packed, by)
 
 
@@ -289,7 +410,7 @@
         rim[2 * q + 1] = jnp.where(top, half_turn(high), low)
         return carry
 
-    lax.fori_loop(0, yr1.shape[0], unpack, 0)
+    lax.fori_loop(0, yr1.shape[0], unpack, 0, unroll=6)
     pack_columns(rim, rim_packed, 8)
 
     def send(m, first, second):
@@ -306,7 +427,7 @@
 
 def filter_kernel(
     source, rim, packed, rim_packed, zr1, zr2, filtered, partial,
-    work, low_strip, high_strip, strips, ends,
+    work0, work1, low_strip, high_strip, strips, ends, joint,
 ):
     cells, by, _ = source.shape
     bx = cells - 2 * REACH
@@ -360,43 +481,49 @@
                     keep = jnp.logical_and(inside, jnp.logical_not(outside))
                 strips[later, y] = jnp.where(keep, total, 0.0)
 
-    def put(slot, x, t, value):
-        work[slot, x, 8 * t + 8 : 8 * t + 16, :] = value
+    for k in range(4):
+        for t in range(tall // 8):
+            low = ends[k, 0, 8 * t : 8 * t + 8, :]
+            high = pltpu.roll(ends[k, 1, 8 * t : 8 * t + 8, :], LANES - 1, 1)
+            even = lax.rem(lane, 2) == 0
+            joint[k, 0, 8 * t : 8 * t + 8, :] = jnp.where(even, low, high)
+            joint[k, 1, 8 * t : 8 * t + 8, :] = jnp.where(even, high, low)
+
+    def put(ref, x, t, value):
+        ref[x, 8 * t + 8 : 8 * t + 16, :] = value
         if t == by // 8:
-            work[slot, x, 0:8, :] = value
+            ref[x, 0:8, :] = value
         if t == 0:
-            work[slot, x, by + 16 : by + 24, :] = value
+            ref[x, by + 16 : by + 24, :] = value
 
     def begin(x, carry):
         for t in range(by // 8):
-            put(0, x, t, POLY[4] * source[x, 8 * t : 8 * t + 8, :])
-        put(0, x, by // 8, POLY[4] * rim[x])
+            put(work0, x, t, POLY[4] * source[x, 8 * t : 8 * t + 8, :])
+        put(work0, x, by // 8, POLY[4] * rim[x])
         return carry
 
-    lax.fori_loop(0, cells, begin, 0)
+    lax.fori_loop(0, cells, begin, 0, unroll=4)
     rim_keep = jnp.logical_not(
         jnp.logical_or(
             jnp.logical_and(last_y, top), jnp.logical_and(first_y, jnp.logical_not(top))
         )
     )
     tiles = by // 8
+    total = jnp.zeros((8, LANES), F32)
     for k in range(4):
-        now, later = k % 2, (k + 1) % 2
-
-        def sweep(x, total, k=k, now=now, later=later):
+        now, later = (work0, work1)[k % 2], (work0, work1)[(k + 1) % 2]
+
+        def sweep(x, parity, k=k, now=now, later=later):
             to_first = lax.rem(LANES - x, LANES)
-            to_last = LANES - 1 - x
+            total = 0.0
             for t in range(tiles + (k < 3)):
                 at = 8 * t + 8
-                mid = work[now, x, at : at + 8, :]
-                value = work[now, x - 1, at : at + 8, :] + work[now, x + 1, at : at + 8, :]
-                value = value + (
-                    work[now, x, at - 1 : at + 7, :] + work[now, x, at + 1 : at + 9, :]
-                )
-                low = pltpu.roll(ends[k, 0, 8 * t : 8 * t + 8, :], to_first, 1)
-                high = pltpu.roll(ends[k, 1, 8 * t : 8 * t + 8, :], to_last, 1)
-                low = jnp.where(lane == 0, low, pltpu.roll(mid, 1, 1))
-                high = jnp.where(lane == LANES - 1, high, pltpu.roll(mid, LANES - 1, 1))
+                mid = now[x, at : at + 8, :]
+                value = now[x - 1, at : at + 8, :] + now[x + 1, at : at + 8, :]
+                value = value + (now[x, at - 1 : at + 7, :] + now[x, at + 1 : at + 9, :])
+                ends_here = pltpu.roll(joint[k, parity, 8 * t : 8 * t + 8, :], to_first, 1)
+                low = jnp.where(lane == 0, ends_here, pltpu.roll(mid, 1, 1))
+                high = jnp.where(lane == LANES - 1, ends_here, pltpu.roll(mid, LANES - 1, 1))
                 value = value + (low + high)
                 own = source[x, 8 * t : 8 * t + 8, :] if t < tiles else rim[x]
                 value = value + POLY[3 - k] * own
@@ -409,16 +536,25 @@
                     put(later, x, t, value)
             return total
 
-        total = lax.fori_loop(k + 1, cells - 1 - k, sweep, jnp.zeros((8, LANES), F32))
+        first, left = (1, cells - 2) if k < 3 else (REACH, bx)
+        group = max(g for g in range(2, 19, 2) if left % g == 0)
+
+        def sweeps(j, total, first=first, group=group, sweep=sweep, k=k):
+            for g in range(group):
+                more = sweep(first + j * group + g, (first + g) % 2)
+                total = total + more if k == 3 else total
+            return total
+
+        total = lax.fori_loop(0, left // group, sweeps, total)
         if k < 3:
 
             @pl.when(first_x)
             def _(later=later):
-                work[later, 0:REACH] = jnp.zeros((REACH,) + work.shape[2:], F32)
+                later[0:REACH] = jnp.zeros((REACH,) + later.shape[1:], F32)
 
             @pl.when(last_x)
             def _(later=later):
-                work[later, bx + REACH : cells] = jnp.zeros((REACH,) + work.shape[2:], F32)
+                later[bx + REACH : cells] = jnp.zeros((REACH,) + later.shape[1:], F32)
 
     partial[...] = jnp.broadcast_to(jnp.sum(total, axis=0, keepdims=True), partial.shape)
 
@@ -437,74 +573,75 @@
             projected[x, rows, :] = level * (1.0 / bottom)
         return carry
 
-    lax.fori_loop(0, density.shape[0], one, 0)
-
-
-def call(kernel, outs, scratch=()):
+    lax.fori_loop(0, density.shape[0], one, 0, unroll=8)
+
+
+def call(kernel, outs, scratch=(), cost=0):
     return pl.pallas_call(
         kernel,
         out_shape=[jax.ShapeDtypeStruct(s, F32) for s in outs],
         out_specs=[VMEM] * len(outs),
         scratch_shapes=[pltpu.VMEM(s, F32) for s in scratch],
         compiler_params=pltpu.CompilerParams(**PARAMS),
+        cost_estimate=pl.CostEstimate(flops=cost, bytes_accessed=cost, transcendentals=0),
     )
 
 
 def body(displacement, density, cell_flags, trim_level):
     bx, by, bz = density.shape
-    assert bz == LANES and bx + 2 * WIDE <= LANES
-    planes, cells, tall = bx + 2 * WIDE, bx + 2 * REACH, by + 8
-
-    odd_x, odd_y = is_odd("gx"), is_odd("gy")
-
-    def x_face(at_low):
-        start = jnp.where(at_low, 0, bx - WIDE)
-        near = lax.dynamic_slice_in_dim(displacement, start, WIDE, 1)
-        start = jnp.where(at_low, 0, bx - REACH)
-        near_coef = cell_coef(
-            *(lax.dynamic_slice_in_dim(v, start, REACH, 0) for v in (density, cell_flags, trim_level))
-        )
-        return jnp.concatenate([near.reshape(3 * WIDE, by, bz), near_coef], axis=0)
-
-    xr1, xr2 = swap(x_face(odd_x), x_face(jnp.logical_not(odd_x)), "gx")
+    assert bz == LANES and bx <= HALF and bx % 2 == 0 and by % 16 == 0
+    cells, tall = bx + 2 * REACH, by + 8
+    devices = lax.axis_size(AXES)
+    odd_y = is_odd("gy")
+    given = displacement, density, cell_flags, trim_level
 
     def y_face(at_low):
         start = jnp.where(at_low, 0, by - 1)
-        parts = [xr1[: 3 * WIDE].reshape(3, WIDE, by, bz), displacement]
-        parts.append(xr2[: 3 * WIDE].reshape(3, WIDE, by, bz))
-        parts = [lax.dynamic_slice_in_dim(p, start, 1, 2)[:, :, 0, :] for p in parts]
-        return jnp.concatenate(parts, axis=1).reshape(3 * planes, bz)
+        return lax.dynamic_slice_in_dim(displacement, start, 1, 2).reshape(3 * bx, bz)
 
     yr1, yr2 = swap(y_face(odd_y), y_face(jnp.logical_not(odd_y)), "gy")
-    zs1, zs2 = call(ends_kernel, [(3, tall, LANES)] * 2)(displacement, xr1, xr2, yr1, yr2)
+    n = 3 * (by // 16)
+    low, high = call(faces_kernel, [(n, 8, LANES)] * 2, cost=6_000_000)(displacement)
+    zs1, zs2 = call(ends_kernel, [(n + 1, 8, LANES)] * 2)(low, high, yr1, yr2)
     zr1, zr2 = swap(zs1, zs2, "gz")
+    rows = x_rows(by)[2]
+    xs1, xs2, rims = call(
+        outward_kernel, [(rows, LANES), (rows, LANES), (2 * ends_tiles(by), 8, LANES)]
+    )(*given, yr1, yr2, zr1, zr2)
+    xr1, xr2 = swap(xs1, xs2, "gx")
+    along = (9, by + 16, LANES)
+    ring = (2, 24, by, LANES)
+    (inner,) = call(
+        inner_kernel, [(bx - 2, by, LANES)], [along, along, ring], cost=60_000_000
+    )(*given, yr1, yr2, rims)
     source, ys1, ys2, packed = call(
-        source_kernel,
+        outer_kernel,
         [(cells, by, LANES), (cells // 2, 8, LANES), (cells // 2, 8, LANES), (by, 8, LANES)],
         [
-            (3, planes, tall, LANES),
-            (cells, by, LANES),
-            (3, tall, LANES),
-            (3, tall, LANES),
-            (9, by + 16, LANES),
-            (2, 24, by, LANES),
+            (2, 3, WIDE + 2, tall, LANES),
+            (2, REACH + 1, by, LANES),
+            (3, 2 * ends_tiles(by), 8, LANES),
+            along,
+            along,
+            ring,
         ],
-    )(displacement, density, cell_flags, trim_level, xr1, xr2, yr1, yr2, zr1, zr2)
+    )(*given, yr1, yr2, rims, xr1, xr2, inner)
     yr1, yr2 = swap(ys1, ys2, "gy")
     rim, rim_packed, zs1, zs2 = call(
         corner_kernel,
         [(cells, 8, LANES), (8, 8, LANES), (tall // 2, 8, LANES), (tall // 2, 8, LANES)],
     )(yr1, yr2, packed)
     zr1, zr2 = swap(zs1, zs2, "gz")
-    devices = lax.axis_size(AXES)
     filtered, partial = call(
         filter_kernel,
         [(bx, by, LANES), (devices, LANES)],
         [
-            (2, cells, by + 24, LANES),
+            (cells, by + 24, LANES),
+            (cells, by + 24, LANES),
             (tall, 8, LANES),
             (tall, 8, LANES),
             (2, tall, 8, LANES),
+            (4, 2, tall, LANES),
             (4, 2, tall, LANES),
         ],
     )(source, rim, packed, rim_packed, zr1, zr2)

time: 153 us -> 104 us (0.68)
  Pallas kernels: 70.6 us -> 32.3 us
  waiting for transfers between devices: 12.2 us -> 5.55 us
  local copies, waits for them, and re-layouts: 5.39 us -> 8.31 us
  blocking collectives: 32.1 us -> 29.2 us
  starting transfers between devices: 30.6 us -> 27.8 us
    pallas_call x3 -> x6, Pallas kernels: 64.7 us -> 30.5 us  [the longest x1 17.3 us: body(): call(inner_kernel, [(bx - 2, by, LANES)], [along, along, ring], cost=6000...]
    ppermute x5, waiting for transfers between devices: 7.82 us -> 1.88 us  [swap(): got_first = lax.ppermute(first, axis, even)]
    unnamed x24 -> x12, local copies, waits for them, and re-layouts: 2.62 us -> 6.79 us
    all_to_all x1, blocking collectives: 32.1 us -> 29.2 us  [body(): lax.all_to_all(partial, AXES, split_axis=0, concat_axis=0, tiled=True)]
    ppermute x5, starting transfers between devices: 11.5 us -> 8.96 us  [swap(): got_first = lax.ppermute(first, axis, even)]
    pallas_call x1, Pallas kernels: 3.74 us -> 1.5 us  [body(): call(functools.partial(project_kernel, count), [(bx, by, LANES)])]
    pallas_call x1, Pallas kernels: 2.2 us -> 0.3 us  [body(): call(corner_kernel, [(cells, 8, LANES), (8, 8, LANES), (tall // 2, 8, LAN...]
  transfers between devices with their start and end apart: 10 -> 10, of which waited for: 5 -> 3; matrix products, arithmetic and copies ran while one was open for 1% -> 0% of each run, Pallas kernels for 0% -> 18%
where the time goes in v2:
time: 104 us
  Pallas kernels  32.3 us (31%)
  blocking collectives  29.2 us (28%)
  starting transfers between devices  27.8 us (27%)
  local copies, waits for them, and re-layouts  8.31 us (8%)
  waiting for transfers between devices  5.55 us (5%)
    all_to_all x1, blocking collectives, body(): lax.all_to_all(partial, AXES, split_axis=0, concat_axis=0, tiled=True)  29.2 us
    ppermute x5, starting transfers between devices, swap(): lax.ppermute(second, axis, odd)  18.9 us
    pallas_call x1, Pallas kernels, body(): call(inner_kernel, [(bx - 2, by, LANES)], [along, along, ring], cost=6000...  17.3 us
    ppermute x5, starting transfers between devices, swap(): got_first = lax.ppermute(first, axis, even)  8.96 us
    pallas_call x1, Pallas kernels, body(): call(filter_kernel, [(bx, by, LANES), (devices, LANES)], [(cells, by + 24...  7.48 us
    unnamed x12, local copies, waits for them, and re-layouts  6.79 us
    pallas_call x1, Pallas kernels, body(): call(outer_kernel, [(cells, by, LANES), (cells // 2, 8, LANES), (cells //...  3.81 us
    ppermute x5, waiting for transfers between devices, swap(): lax.ppermute(second, axis, odd)  3.67 us
  transfers between devices with their start and end apart: 10, of which 3 were waited for; matrix products, arithmetic and copies ran while one was open for 0% of the time, Pallas kernels for 18%

profile of v2, /device:TPU:1, one launch (start us, length us, event | category | flops | bytes accessed | tf_op | source)
XLA Modules:
  0.0 104.0 jit_solution(15819339545376418479)
XLA Ops:
  0.6 1.5 %constant_dynamic-slice_fusion = (f32[3,64,1,128]{3,2,1,0:T(1,128)S(1)}, f32[3,64,1,128]{3,2,1,0:T(1,128)S(1)}) fusion(f32[3,64,32,128]{3,2,1,0:T(8,128)} %disp.7, s32[]{:T(128)S(6)} %select_n.10, s32[]{:T(128)S(6)} %select_n.9), kind=kLoop, calls=%fused_computation | loop fusion | bytes 393224 | tf_op jit(solution)/shard_map/dynamic_slice | solution.py:600
  2.2 2.1 %collective-permute-start = (f32[192,128]{1,0:T(8,128)S(1)}, f32[192,128]{1,0:T(8,128)S(1)}, u32[]{:S(2)}, u32[]{:S(2)}) collective-permute-start(f32[192,128]{1,0:T(8,128)S(1)} %bitcast.9), channel_id=1, source_target_pairs={{0,4},{4,0},{8,12},{12,8},{1,5},{5,1},{9,13},{13,9},{2,6},{6,2},{1... | collective-permute-start | bytes 294920 | tf_op jit(solution)/shard_map/ppermute | solution.py:44
  4.3 0.7 collective-permute-start.1
  5.0 0.0 copy-start
  5.0 1.9 %copy-done = f32[3,64,32,128]{3,2,1,0:T(8,128)S(1)} copy-done((f32[3,64,32,128]{3,2,1,0:T(8,128)S(1)}, f32[3,64,32,128]{3,2,1,0:T(8,128)}, u32[]{:S(2)}) %copy-start) | copy-done | bytes 3145752
  6.9 1.7 %shard_map.59 = (f32[6,8,128]{2,1,0:T(8,128)S(1)}, f32[6,8,128]{2,1,0:T(8,128)S(1)}) custom-call(f32[3,64,32,128]{3,2,1,0:T(8,128)S(1)} %copy-done), custom_call_target="tpu_custom_call" | custom-call | flops 6000000 | bytes 6000000 | tf_op jit(solution)/shard_map/pallas_call | solution.py:604
  8.6 0.0 collective-permute-done.yr1
  8.6 0.0 collective-permute-done.1.yr2
  8.6 0.1 shard_map.60
  8.7 1.6 %collective-permute-start.2 = (f32[7,8,128]{2,1,0:T(8,128)S(1)}, f32[7,8,128]{2,1,0:T(8,128)S(1)}, u32[]{:S(2)}, u32[]{:S(2)}) collective-permute-start(f32[7,8,128]{2,1,0:T(8,128)S(1)} %get-tuple-element.21), channel_id=1, source_target_pairs={{0,1},{1,0},{2,3},{3,2},{4,5},{5,4},{6,7},{7,6},{8,9},{9,8},{10,11... | collective-permute-start | bytes 86024 | tf_op jit(solution)/shard_map/ppermute | solution.py:44
  10.3 8.1 %collective-permute-start.3 = (f32[7,8,128]{2,1,0:T(8,128)S(1)}, f32[7,8,128]{2,1,0:T(8,128)S(1)}, u32[]{:S(2)}, u32[]{:S(2)}) collective-permute-start(f32[7,8,128]{2,1,0:T(8,128)S(1)} %get-tuple-element.22), channel_id=1, source_target_pairs={{1,2},{2,1},{5,6},{6,5},{9,10},{10,9},{13,14},{14,13},{17,18},{18,... | collective-permute-start | bytes 86024 | tf_op jit(solution)/shard_map/ppermute | solution.py:45
  18.5 1.6 %collective-permute-done.3.zr2 = f32[7,8,128]{2,1,0:T(8,128)S(1)} collective-permute-done((f32[7,8,128]{2,1,0:T(8,128)S(1)}, f32[7,8,128]{2,1,0:T(8,128)S(1)}, u32[]{:S(2)}, u32[]{:S(2)}) %collective-permute-start.3) | collective-permute-done | bytes 28704 | tf_op jit(solution)/shard_map/ppermute | solution.py:45
  20.0 1.2 %copy-done.2 = f32[64,32,128]{2,1,0:T(8,128)S(1)} copy-done((f32[64,32,128]{2,1,0:T(8,128)S(1)}, f32[64,32,128]{2,1,0:T(8,128)}, u32[]{:S(2)}) %copy-start.2) | copy-done | bytes 1048600
  21.3 1.2 %copy-done.3 = s32[64,32,128]{2,1,0:T(8,128)S(1)} copy-done((s32[64,32,128]{2,1,0:T(8,128)S(1)}, s32[64,32,128]{2,1,0:T(8,128)}, u32[]{:S(2)}) %copy-start.3) | copy-done | bytes 1048600
  22.5 1.2 %copy-done.4 = s32[64,32,128]{2,1,0:T(8,128)S(1)} copy-done((s32[64,32,128]{2,1,0:T(8,128)S(1)}, s32[64,32,128]{2,1,0:T(8,128)}, u32[]{:S(2)}) %copy-start.4) | copy-done | bytes 1048600
  23.7 0.1 shard_map.61
  23.8 1.4 %collective-permute-start.4 = (f32[872,128]{1,0:T(8,128)S(1)}, f32[872,128]{1,0:T(8,128)S(1)}, u32[]{:S(2)}, u32[]{:S(2)}) collective-permute-start(f32[872,128]{1,0:T(8,128)S(1)} %get-tuple-element.24), channel_id=1, source_target_pairs={{0,16},{16,0},{32,48},{48,32},{64,80},{80,64},{96,112},{112,96},{1... | collective-permute-start | bytes 1339400 | tf_op jit(solution)/shard_map/ppermute | solution.py:44
  25.2 0.7 collective-permute-start.5
  25.9 17.3 %shard_map.62.inner = f32[62,32,128]{2,1,0:T(8,128)S(1)} custom-call(f32[3,64,32,128]{3,2,1,0:T(8,128)S(1)} %copy-done.1, f32[64,32,128]{2,1,0:T(8,128)S(1)} %copy-done.2, s32[64,32,128]{2,1,0:T(8,128)S(1)} %copy-done.3, s32[64,32,128]{2,1,0:T(8,128)S(1)} %copy-done.4, f32[192,128]{1,0:T(8,128)S(1)} %collective-permute-done.yr1, ...), custom_call_target="tpu_custom_call" | custom-call | flops 60000000 | bytes 60000000 | tf_op jit(solution)/shard_map/pallas_call | solution.py:614
  43.2 0.0 collective-permute-done.4.xr1
  43.2 3.8 %shard_map.63 = (f32[72,32,128]{2,1,0:T(8,128)S(1)}, f32[36,8,128]{2,1,0:T(8,128)S(1)}, f32[36,8,128]{2,1,0:T(8,128)S(1)}, f32[32,8,128]{2,1,0:T(8,128)S(1)}) custom-call(f32[3,64,32,128]{3,2,1,0:T(8,128)S(1)} %copy-done.1, f32[64,32,128]{2,1,0:T(8,128)S(1)} %copy-done.2, s32[64,32,128]{2,1,0:T(8,128)S(1)} %copy-done.3, s32[64,32,128]{2,1,0:T(8,128)S(1)} %copy-done.4, ...), custom_call_target="tpu_custom_call" | custom-call | tf_op jit(solution)/shard_map/pallas_call | solution.py:617
  47.1 3.7 %collective-permute-start.6 = (f32[36,8,128]{2,1,0:T(8,128)S(1)}, f32[36,8,128]{2,1,0:T(8,128)S(1)}, u32[]{:S(2)}, u32[]{:S(2)}) collective-permute-start(f32[36,8,128]{2,1,0:T(8,128)S(1)} %get-tuple-element.27), channel_id=1, source_target_pairs={{0,4},{4,0},{8,12},{12,8},{1,5},{5,1},{9,13},{13,9},{2,6},{6,2},{1... | collective-permute-start | bytes 442376 | tf_op jit(solution)/shard_map/ppermute | solution.py:44
  50.8 0.7 collective-permute-start.7
  51.5 1.9 %collective-permute-done.6.yr1 = f32[36,8,128]{2,1,0:T(8,128)S(1)} collective-permute-done((f32[36,8,128]{2,1,0:T(8,128)S(1)}, f32[36,8,128]{2,1,0:T(8,128)S(1)}, u32[]{:S(2)}, u32[]{:S(2)}) %collective-permute-start.6) | collective-permute-done | bytes 147488 | tf_op jit(solution)/shard_map/ppermute | solution.py:44
  53.3 0.3 shard_map.64
  53.6 0.1 collective-permute-start.8
  53.7 8.7 %collective-permute-start.9 = (f32[20,8,128]{2,1,0:T(8,128)S(1)}, f32[20,8,128]{2,1,0:T(8,128)S(1)}, u32[]{:S(2)}, u32[]{:S(2)}) collective-permute-start(f32[20,8,128]{2,1,0:T(8,128)S(1)} %get-tuple-element.33), channel_id=1, source_target_pairs={{1,2},{2,1},{5,6},{6,5},{9,10},{10,9},{13,14},{14,13},{17,18},{18,... | collective-permute-start | bytes 245768 | tf_op jit(solution)/shard_map/ppermute | solution.py:45
  62.5 2.1 %collective-permute-done.9.zr2 = f32[20,8,128]{2,1,0:T(8,128)S(1)} collective-permute-done((f32[20,8,128]{2,1,0:T(8,128)S(1)}, f32[20,8,128]{2,1,0:T(8,128)S(1)}, u32[]{:S(2)}, u32[]{:S(2)}) %collective-permute-start.9) | collective-permute-done | bytes 81952 | tf_op jit(solution)/shard_map/ppermute | solution.py:45
  64.6 7.5 %shard_map.65 = (f32[64,32,128]{2,1,0:T(8,128)}, f32[256,128]{1,0:T(8,128)S(1)}) custom-call(f32[72,32,128]{2,1,0:T(8,128)S(1)} %get-tuple-element.26.source, f32[72,8,128]{2,1,0:T(8,128)S(1)} %get-tuple-element.30.rim, f32[32,8,128]{2,1,0:T(8,128)S(1)} %get-tuple-element.29.packed, f32[8,8,128]{2,1,0:T(8,128)S(1)} %get-tuple-element.31.rim_packed, ...), custom_call_target="tpu_custom_call" | custom-call | tf_op jit(solution)/shard_map/pallas_call | solution.py:635
  72.1 29.2 %all_to_all.11 = f32[256,1,128]{2,1,0:T(1,128)S(1)} all-to-all(f32[256,1,128]{2,1,0:T(1,128)S(1)} %bitcast.7), channel_id=1, replica_groups=mesh['gx'=16,'gy'=4,'gz'=4] {'gx','gy','gz'}, dimensions={0} | all-to-all | bytes 262144 | tf_op jit(solution)/shard_map/all_to_all | solution.py:648
  101.3 1.2 %copy-done.5 = f32[64,32,128]{2,1,0:T(8,128)S(1)} copy-done((f32[64,32,128]{2,1,0:T(8,128)S(1)}, f32[64,32,128]{2,1,0:T(8,128)}, u32[]{:S(2)}) %copy-start.5) | copy-done | bytes 1048600
  102.5 1.5 %shard_map.66 = f32[64,32,128]{2,1,0:T(8,128)} custom-call(f32[64,32,128]{2,1,0:T(8,128)S(1)} %copy-done.2, f32[64,32,128]{2,1,0:T(8,128)S(1)} %copy-done.5, f32[256,128]{1,0:T(8,128)S(1)} %bitcast.6), custom_call_target="tpu_custom_call" | custom-call | tf_op jit(solution)/shard_map/pallas_call | solution.py:650
  (10 shorter events, 0.0 us)
Async XLA Ops:
  2.2 6.4 %collective-permute-start = (f32[192,128]{1,0:T(8,128)S(1)}, f32[192,128]{1,0:T(8,128)S(1)}, u32[]{:S(2)}, u32[]{:S(2)}) collective-permute-start(f32[192,128]{1,0:T(8,128)S(1)} %bitcast.9), channel_id=1, source_target_pairs={{0,4},{4,0},{8,12},{12,8},{1,5},{5,1},{9,13},{13,9},{2,6},{6,2},{1... | collective-permute-start | bytes 294920 | tf_op jit(solution)/shard_map/ppermute | solution.py:44
  4.3 4.3 %collective-permute-start.1 = (f32[192,128]{1,0:T(8,128)S(1)}, f32[192,128]{1,0:T(8,128)S(1)}, u32[]{:S(2)}, u32[]{:S(2)}) collective-permute-start(f32[192,128]{1,0:T(8,128)S(1)} %bitcast.8), channel_id=1, source_target_pairs={{4,8},{8,4},{5,9},{9,5},{6,10},{10,6},{7,11},{11,7},{20,24},{24,20... | collective-permute-start | bytes 294920 | tf_op jit(solution)/shard_map/ppermute | solution.py:45
  5.0 1.9 %copy-start = (f32[3,64,32,128]{3,2,1,0:T(8,128)S(1)}, f32[3,64,32,128]{3,2,1,0:T(8,128)}, u32[]{:S(2)}) copy-start(f32[3,64,32,128]{3,2,1,0:T(8,128)} %disp.7) | copy-start | bytes 9437188
  6.9 13.2 %copy-start.1 = (f32[3,64,32,128]{3,2,1,0:T(8,128)S(1)}, f32[3,64,32,128]{3,2,1,0:T(8,128)}, u32[]{:S(2)}) copy-start(f32[3,64,32,128]{3,2,1,0:T(8,128)} %disp.7) | copy-start | bytes 9437188
  8.7 9.8 %collective-permute-start.2 = (f32[7,8,128]{2,1,0:T(8,128)S(1)}, f32[7,8,128]{2,1,0:T(8,128)S(1)}, u32[]{:S(2)}, u32[]{:S(2)}) collective-permute-start(f32[7,8,128]{2,1,0:T(8,128)S(1)} %get-tuple-element.21), channel_id=1, source_target_pairs={{0,1},{1,0},{2,3},{3,2},{4,5},{5,4},{6,7},{7,6},{8,9},{9,8},{10,11... | collective-permute-start | bytes 86024 | tf_op jit(solution)/shard_map/ppermute | solution.py:44
  10.3 9.7 %collective-permute-start.3 = (f32[7,8,128]{2,1,0:T(8,128)S(1)}, f32[7,8,128]{2,1,0:T(8,128)S(1)}, u32[]{:S(2)}, u32[]{:S(2)}) collective-permute-start(f32[7,8,128]{2,1,0:T(8,128)S(1)} %get-tuple-element.22), channel_id=1, source_target_pairs={{1,2},{2,1},{5,6},{6,5},{9,10},{10,9},{13,14},{14,13},{17,18},{18,... | collective-permute-start | bytes 86024 | tf_op jit(solution)/shard_map/ppermute | solution.py:45
  20.0 1.2 %copy-start.2 = (f32[64,32,128]{2,1,0:T(8,128)S(1)}, f32[64,32,128]{2,1,0:T(8,128)}, u32[]{:S(2)}) copy-start(f32[64,32,128]{2,1,0:T(8,128)} %density.7) | copy-start | bytes 3145732
  21.3 1.2 %copy-start.3 = (s32[64,32,128]{2,1,0:T(8,128)S(1)}, s32[64,32,128]{2,1,0:T(8,128)}, u32[]{:S(2)}) copy-start(s32[64,32,128]{2,1,0:T(8,128)} %flags.5) | copy-start | bytes 3145732
  22.5 1.2 %copy-start.4 = (s32[64,32,128]{2,1,0:T(8,128)S(1)}, s32[64,32,128]{2,1,0:T(8,128)}, u32[]{:S(2)}) copy-start(s32[64,32,128]{2,1,0:T(8,128)} %trim.5) | copy-start | bytes 3145732
  23.8 19.4 %collective-permute-start.4 = (f32[872,128]{1,0:T(8,128)S(1)}, f32[872,128]{1,0:T(8,128)S(1)}, u32[]{:S(2)}, u32[]{:S(2)}) collective-permute-start(f32[872,128]{1,0:T(8,128)S(1)} %get-tuple-element.24), channel_id=1, source_target_pairs={{0,16},{16,0},{32,48},{48,32},{64,80},{80,64},{96,112},{112,96},{1... | collective-permute-start | bytes 1339400 | tf_op jit(solution)/shard_map/ppermute | solution.py:44
  25.2 18.0 %collective-permute-start.5 = (f32[872,128]{1,0:T(8,128)S(1)}, f32[872,128]{1,0:T(8,128)S(1)}, u32[]{:S(2)}, u32[]{:S(2)}) collective-permute-start(f32[872,128]{1,0:T(8,128)S(1)} %get-tuple-element.25), channel_id=1, source_target_pairs={{16,32},{32,16},{48,64},{64,48},{80,96},{96,80},{112,128},{128,112... | collective-permute-start | bytes 1339400 | tf_op jit(solution)/shard_map/ppermute | solution.py:45
  47.1 6.3 %collective-permute-start.6 = (f32[36,8,128]{2,1,0:T(8,128)S(1)}, f32[36,8,128]{2,1,0:T(8,128)S(1)}, u32[]{:S(2)}, u32[]{:S(2)}) collective-permute-start(f32[36,8,128]{2,1,0:T(8,128)S(1)} %get-tuple-element.27), channel_id=1, source_target_pairs={{0,4},{4,0},{8,12},{12,8},{1,5},{5,1},{9,13},{13,9},{2,6},{6,2},{1... | collective-permute-start | bytes 442376 | tf_op jit(solution)/shard_map/ppermute | solution.py:44
  50.8 2.5 %collective-permute-start.7 = (f32[36,8,128]{2,1,0:T(8,128)S(1)}, f32[36,8,128]{2,1,0:T(8,128)S(1)}, u32[]{:S(2)}, u32[]{:S(2)}) collective-permute-start(f32[36,8,128]{2,1,0:T(8,128)S(1)} %get-tuple-element.28), channel_id=1, source_target_pairs={{4,8},{8,4},{5,9},{9,5},{6,10},{10,6},{7,11},{11,7},{20,24},{24,20... | collective-permute-start | bytes 442376 | tf_op jit(solution)/shard_map/ppermute | solution.py:45
  53.6 8.8 %collective-permute-start.8 = (f32[20,8,128]{2,1,0:T(8,128)S(1)}, f32[20,8,128]{2,1,0:T(8,128)S(1)}, u32[]{:S(2)}, u32[]{:S(2)}) collective-permute-start(f32[20,8,128]{2,1,0:T(8,128)S(1)} %get-tuple-element.32), channel_id=1, source_target_pairs={{0,1},{1,0},{2,3},{3,2},{4,5},{5,4},{6,7},{7,6},{8,9},{9,8},{10,11... | collective-permute-start | bytes 245768 | tf_op jit(solution)/shard_map/ppermute | solution.py:44
  53.7 10.8 %collective-permute-start.9 = (f32[20,8,128]{2,1,0:T(8,128)S(1)}, f32[20,8,128]{2,1,0:T(8,128)S(1)}, u32[]{:S(2)}, u32[]{:S(2)}) collective-permute-start(f32[20,8,128]{2,1,0:T(8,128)S(1)} %get-tuple-element.33), channel_id=1, source_target_pairs={{1,2},{2,1},{5,6},{6,5},{9,10},{10,9},{13,14},{14,13},{17,18},{18,... | collective-permute-start | bytes 245768 | tf_op jit(solution)/shard_map/ppermute | solution.py:45
  101.3 1.2 %copy-start.5 = (f32[64,32,128]{2,1,0:T(8,128)S(1)}, f32[64,32,128]{2,1,0:T(8,128)}, u32[]{:S(2)}) copy-start(f32[64,32,128]{2,1,0:T(8,128)} %get-tuple-element.18.filtered) | copy-start | bytes 3145732

commit v3 on v2

--- a/solution.py
+++ b/solution.py
@@ -3,6 +3,7 @@
 
 import jax
 import jax.numpy as jnp
+import numpy as np
 from jax import lax
 from jax.experimental import pallas as pl
 from jax.experimental.pallas import tpu as pltpu
@@ -32,18 +33,55 @@
     16.0 / 1296.0 / (SPREAD_HALF * CHEB),
 ]
 
+
+def reach_weights():
+    power = np.ones((5 + REACH,) * 3)
+    total = POLY[0] * power
+    for m in range(1, REACH + 1):
+        wide = np.pad(np.pad(power, ((0, 1),) * 3, mode="edge"), ((1, 0),) * 3)
+        power = sum(
+            np.roll(wide, step, dim)[1:-1, 1:-1, 1:-1] for dim in range(3) for step in (1, -1)
+        )
+        total = total + POLY[m] * power
+    return total[:5, :5, :5]
+
+
 F32 = jnp.float32
 VMEM = pl.BlockSpec(memory_space=pltpu.VMEM)
 PARAMS = dict(vmem_limit_bytes=20 * 1024 * 1024)
 
 
+def partners(axis, sizes):
+    dim = AXES.index(axis)
+    count, near = sizes[dim], 1 if axis == "gz" else 2
+    first, second = [], []
+    for at in np.ndindex(*sizes):
+        for pairs, other in (
+            (first, at[dim] ^ 1),
+            (second, at[dim] + 1 if at[dim] % 2 else at[dim] - 1),
+        ):
+            to = list(at)
+            if 0 <= other < count:
+                to[dim] = other
+            elif sizes[near] > 1:
+                to[near] ^= 1
+            pairs.append(tuple(int(np.ravel_multi_index(v, sizes)) for v in (at, to)))
+    return first, second
+
+
 def swap(first, second, axis):
-    count = lax.axis_size(axis)
-    even = [(i, i ^ 1) for i in range(count)]
-    odd = [(i, i + 1 if i % 2 else i - 1) for i in range(1, count - 1)]
-    got_first = lax.ppermute(first, axis, even)
-    got_second = lax.ppermute(second, axis, odd) if odd else jnp.zeros_like(second)
-    return got_first, got_second
+    sizes = tuple(lax.axis_size(a) for a in AXES)
+    near, far_ones = partners(axis, sizes)
+    return lax.ppermute(first, AXES, near), lax.ppermute(second, AXES, far_ones)
+
+
+def at_end(axis):
+    at = lax.axis_index(axis)
+    return jnp.logical_or(at == 0, at == lax.axis_size(axis) - 1)
+
+
+def cleared(axis, value):
+    return jnp.where(at_end(axis), 0.0, value)
 
 
 def is_odd(axis):
@@ -82,6 +120,16 @@
         first = jnp.concatenate([first, zero], axis=0)
         second = jnp.concatenate([second, zero], axis=0)
     return jnp.concatenate([first, second], axis=0).T
+
+
+def sides_kernel(disp, ys1, ys2):
+    _, bx, by, _ = disp.shape
+    odd_y = is_odd("gy")
+    for c in range(3):
+        rows = slice(c * bx, c * bx + bx)
+        low, high = disp[c, :, 0, :], disp[c, :, by - 1, :]
+        ys1[rows, :] = jnp.where(odd_y, low, high)
+        ys2[rows, :] = jnp.where(odd_y, high, low)
 
 
 def faces_kernel(disp, low, high):
@@ -94,9 +142,10 @@
             high[c * n + y // 8, y % 8 : y % 8 + 1, :] = turned[LANES - 1 : LANES]
 
 
-def ends_kernel(low, high, yr1, yr2, zs1, zs2):
+def ends_kernel(low, high, yr1, yr2_raw, zs1, zs2, yr2):
     odd_z = is_odd("gz")
     n, bx = low.shape[0], yr1.shape[0] // 3
+    yr2[...] = cleared("gy", yr2_raw[...])
     zs1[0:n] = jnp.where(odd_z, low[...], high[...])
     zs2[0:n] = jnp.where(odd_z, high[...], low[...])
     zs1[n] = jnp.zeros((8, LANES), F32)
@@ -120,14 +169,14 @@
     return 3 * (by // 16 + 1)
 
 
-def outward_kernel(disp, density, flags, trim, yr1, yr2, zr1, zr2, xs1, xs2, rims):
+def outward_kernel(disp, coef, yr1, yr2, zr1, zr2, xs1, xs2, rims):
     _, bx, by, _ = disp.shape
     tall, n = by + 8, by // 16
     odd_x, odd_y, odd_z = is_odd("gx"), is_odd("gy"), is_odd("gz")
     top_row, left = row_ids() == 0, lane_ids() < HALF
     for side in range(2):
         def pick(*at, side=side):
-            one, two = zr1[at], zr2[at]
+            one, two = zr1[at], cleared("gz", zr2[at])
             return jnp.where(odd_z, two, one) if side else jnp.where(odd_z, one, two)
 
         for c in range(3):
@@ -147,8 +196,7 @@
                 out[at + by : at + tall, :] = rim_tile(yr1, yr2, c * bx + start + k, odd_y)
         start = jnp.where(at_low, 0, bx - REACH)
         for k in range(REACH):
-            x = start + k
-            out[planes + k * by : planes + (k + 1) * by, :] = cell_coef(density[x], flags[x], trim[x])
+            out[planes + k * by : planes + (k + 1) * by, :] = coef[start + k]
         for j in range(2 * ends_tiles(by)):
             out[coefs + 8 * j : coefs + 8 * j + 8, :] = rims[j]
 
@@ -163,28 +211,37 @@
     return (2.0 / 3.0) * (a + c) + (8.0 / 3.0) * b, c - a
 
 
+FIELDS = (
+    [(0, key) for key in ("MM", "MD", "MS", "DM", "DD", "DS", "SM", "SD")]
+    + [(1, key) for key in ("MM", "MD", "DM", "DD", "SM", "SD")]
+    + [(2, key) for key in ("MM", "MD", "DM", "DD", "MS", "DS")]
+    + [(3, key) for key in ("00", "01", "10", "11")]
+)
+ALL_THREE = {(0, "MD"), (0, "DM"), (0, "DD"), (1, "DM"), (1, "DD"), (2, "MD"), (2, "DD")}
+NO_VALUE = {(0, "MM"), (1, "MM"), (1, "MD"), (2, "MM"), (2, "DM")}
+
+
 def energy_of(fields):
-    grads = []
-    for c in range(3):
-        g = {}
-        for key, planes in fields[c].items():
-            if key == "MM":
-                a, b, n = planes
-                g["DMM"], g["SMM"] = n - a, (a + n) - 2.0 * b
-            elif key in ("MD", "DM", "DD"):
-                g["M" + key], g["D" + key], g["S" + key] = triple(*planes)
-            else:
-                g["M" + key], g["D" + key] = pair(*planes)
-        grads.append(g)
+    grads = {}
+    for name, planes in fields.items():
+        if name in NO_VALUE:
+            a, b, n = planes
+            grads[name + ("D",)], grads[name + ("S",)] = n - a, (a + n) - 2.0 * b
+        elif name in ALL_THREE:
+            three = triple(*planes)
+            grads.update({name + (x,): v for x, v in zip("MDS", three)})
+        else:
+            grads.update({name + (x,): v for x, v in zip("MD", pair(*planes))})
     names = "MD", "DS"
 
     def part(c, e, p):
-        return grads[c]["".join(names[1 if d == e else 0][p[d]] for d in range(3))]
-
-    traces = normals = shears = None
+        ops = [names[1 if d == e else 0][p[d]] for d in range(3)]
+        return grads[(c, ops[1] + ops[2], ops[0])]
+
+    traces = mixed = shears = None
     for order in (3, 2, 1, 0):
         if traces is not None:
-            traces, normals, shears = (v * (1.0 / 3.0) for v in (traces, normals, shears))
+            traces, mixed, shears = (v * (1.0 / 3.0) for v in (traces, mixed, shears))
         for bits in range(8):
             p = (bits >> 2) & 1, (bits >> 1) & 1, bits & 1
             if sum(p) != order:
@@ -192,24 +249,22 @@
             xx, yy, zz = (part(c, c, p) for c in range(3))
             xy = part(0, 1, p) + part(1, 0, p)
             xz = part(0, 2, p) + part(2, 0, p)
-            yz = part(1, 2, p) + part(2, 1, p)
-            trace = xx + yy + zz
+            yz = grads[(3, "%d%d" % p[1:], "MD"[p[0]])]
+            both = xx + yy
+            trace = both + zz
             trace = trace * trace
-            normal = xx * xx + yy * yy + zz * zz
+            mix = xx * yy + both * zz
             shear = xy * xy + xz * xz + yz * yz
             if traces is None:
-                traces, normals, shears = trace, normal, shear
+                traces, mixed, shears = trace, mix, shear
             else:
-                traces, normals, shears = traces + trace, normals + normal, shears + shear
+                traces, mixed, shears = traces + trace, mixed + mix, shears + shear
     scale = 1.0 / 1024.0
     return (
-        (LAMBDA * scale) * traces
-        + (2.0 * SHEAR_MODULUS * scale) * normals
+        ((LAMBDA + 2.0 * SHEAR_MODULUS) * scale) * traces
+        - (4.0 * SHEAR_MODULUS * scale) * mixed
         + (SHEAR_MODULUS * scale) * shears
     )
-
-
-YZ = ("MM", "MD", "MS", "DM", "DD", "DS", "SM", "SD")
 
 
 def z_pass(tile_of, low_of, high_of, along):
@@ -236,30 +291,51 @@
 def xy_pass(along, ring, slot, emit):
     for t in range(along.shape[1] // 8 - 2):
         rows = slice(8 * t, 8 * t + 8)
-        fields = []
+        now = {}
         for c in range(3):
-            now = {}
             for k, z in enumerate("MDS"):
                 three = [along[3 * c + k, 8 * t + 7 + o : 8 * t + 15 + o, :] for o in range(3)]
-                if z == "S":
-                    now["MS"], now["DS"] = pair(*three)
-                else:
-                    now["M" + z], now["D" + z], now["S" + z] = triple(*three)
-            held = {}
-            for k, key in enumerate(YZ):
-                f = 8 * c + k
-                if emit is not None:
-                    held[key] = ring[slot, f, rows, :], ring[1 - slot, f, rows, :], now[key]
-                ring[slot, f, rows, :] = now[key]
-            fields.append(held)
+                values = pair(*three) if z == "S" else triple(*three)
+                now.update({(c, y + z): v for y, v in zip("MDS", values)})
+        now[(3, "00")] = now[(2, "DM")] + now[(1, "MD")]
+        now[(3, "01")] = now[(2, "DD")] + now[(1, "MS")]
+        now[(3, "10")] = now[(2, "SM")] + now[(1, "DD")]
+        now[(3, "11")] = now[(2, "SD")] + now[(1, "DS")]
+        fields = {}
+        for f, name in enumerate(FIELDS):
+            if emit is not None:
+                fields[name] = ring[slot, f, rows, :], ring[1 - slot, f, rows, :], now[name]
+            ring[slot, f, rows, :] = now[name]
         if emit is not None:
             emit(t, energy_of(fields))
 
 
-def inner_kernel(disp, density, flags, trim, yr1, yr2, rims, inner, along0, along1, ring):
+def far(axis, index, size):
+    at = lax.axis_index(axis) * size + index
+    return jnp.minimum(jnp.minimum(at, lax.axis_size(axis) * size - 1 - at), REACH)
+
+
+def fill_weights(weights):
+    table = reach_weights()
+    by = weights.shape[1]
+    far_z = far("gz", lane_ids(), LANES)
+    for d in range(REACH + 1):
+        for t in range(by // 8):
+            far_y = far("gy", row_ids() + 8 * t, by)
+            value = None
+            for j in range(REACH, -1, -1):
+                line = jnp.full((8, LANES), table[d, j, REACH], F32)
+                for k in range(REACH):
+                    line = jnp.where(far_z == k, F32(table[d, j, k]), line)
+                value = line if value is None else jnp.where(far_y == j, line, value)
+            weights[d, 8 * t : 8 * t + 8, :] = value
+
+
+def inner_kernel(disp, coef, yr1, yr2, rims, inner, partial, weights, along0, along1, ring):
     _, bx, by, _ = disp.shape
     odd_y = is_odd("gy")
     tiles = by // 8
+    fill_weights(weights)
 
     def along_z(x, along):
         def tile_of(c, t):
@@ -276,31 +352,37 @@
 
         z_pass(tile_of, rim(0, 0), rim(1, LANES - 1), along)
 
-    def across(x, along, slot):
+    def across(x, along, slot, total):
+        totals = [total]
+
         def emit(t, energy):
             rows = slice(8 * t, 8 * t + 8)
-            at = jnp.maximum(x - 1, 0)
-            coef = cell_coef(density[at, rows, :], flags[at, rows, :], trim[at, rows, :])
-            inner[jnp.maximum(x - 2, 0), rows, :] = coef * energy
-
-        xy_pass(along, ring, slot, emit)
+            value = coef[x - 1, rows, :] * energy
+            inner[x - 2, rows, :] = value
+            totals.append(totals[-1] + weights[far("gx", x - 1, bx), rows, :] * value)
+
+        xy_pass(along, ring, slot, emit if total is not None else None)
+        return totals[-1]
 
     along_z(0, along0)
-
-    def planes_two(k, carry):
+    along_z(1, along1)
+    across(0, along0, 0, None)
+    along_z(2, along0)
+    across(1, along1, 1, None)
+
+    def planes_two(k, total):
         along_z(2 * k + 1, along1)
-        across(2 * k, along0, 0)
+        total = across(2 * k, along0, 0, total)
         along_z(jnp.minimum(2 * k + 2, bx - 1), along0)
-        across(2 * k + 1, along1, 1)
-        return carry
-
-    lax.fori_loop(0, bx // 2, planes_two, 0)
+        return across(2 * k + 1, along1, 1, total)
+
+    partial[...] = lax.fori_loop(1, bx // 2, planes_two, jnp.zeros((8, LANES), F32))
 
 
 def outer_kernel(
-    disp, density, flags, trim, yr1, yr2, rims, xr1, xr2, inner,
-    source, ys1, ys2, packed,
-    field, coef, ends, along0, along1, ring,
+    disp, coef, yr1, yr2, rims, xr1, xr2, inner, partial, weights,
+    source, ys1, ys2, total,
+    field, rim_coef, ends, along0, along1, ring,
 ):
     _, bx, by, _ = disp.shape
     cells, tall = bx + 2 * REACH, by + 8
@@ -310,7 +392,7 @@
     row = row_ids()
     for side in range(2):
         def pick(at, size, side=side):
-            one, two = xr1[at : at + size, :], xr2[at : at + size, :]
+            one, two = xr1[at : at + size, :], cleared("gx", xr2[at : at + size, :])
             return jnp.where(odd_x, two, one) if side else jnp.where(odd_x, one, two)
 
         for c in range(3):
@@ -322,13 +404,13 @@
                 field[side, c, at, 0:by, :] = disp[c, x]
                 field[side, c, at, by:tall, :] = rim_tile(yr1, yr2, c * bx + x, odd_y)
         for k in range(REACH):
-            coef[side, k + side] = pick(planes + k * by, by)
-        x = bx - 1 if side else 0
-        coef[side, 0 if side else REACH] = cell_coef(density[x], flags[x], trim[x])
+            rim_coef[side, k + side] = pick(planes + k * by, by)
+        rim_coef[side, 0 if side else REACH] = coef[bx - 1 if side else 0]
         for j in range(2 * ends_tiles(by)):
             ends[side, j] = pick(coefs + 8 * j, 8)
     for j in range(2 * ends_tiles(by)):
         ends[2, j] = rims[j]
+    total[...] = partial[...]
 
     def one_side(side, carry):
         high_side = side == 1
@@ -362,13 +444,17 @@
 
             def emit(t, energy, i=i):
                 rows = slice(8 * t, 8 * t + 8)
-                source[side * (cells - WIDE) + i - 2, rows, :] = coef[side, i - 2, rows, :] * energy
+                value = rim_coef[side, i - 2, rows, :] * energy
+                source[side * (cells - WIDE) + i - 2, rows, :] = value
+                if i in (2, count - 1):
+                    own = high_side if i == 2 else jnp.logical_not(high_side)
+                    weight = weights[far("gx", bx - 1 if i == 2 else 0, bx), rows, :]
+                    total[...] += jnp.where(own, weight * value, 0.0)
 
             xy_pass(alongs[i % 2], ring, i % 2, emit if i >= 2 else None)
         return carry
 
     lax.fori_loop(0, 2, one_side, 0)
-
     def copy(x, carry):
         source[x + WIDE] = inner[x]
         return carry
@@ -386,7 +472,6 @@
         return carry
 
     lax.fori_loop(0, cells // 2, rows_out, 0, unroll=6)
-    pack_columns(source, packed, by)
 
 
 def pack_columns(source, packed, count):
@@ -398,14 +483,20 @@
         packed[y] = jnp.where(row < 4, flat[0:8], flat[LANES - 8 : LANES])
 
 
+def pack_kernel(source, total, packed, sums):
+    pack_columns(source, packed, source.shape[1])
+    sums[...] = jnp.broadcast_to(jnp.sum(total[...], axis=0, keepdims=True), sums.shape)
+
+
 def corner_kernel(yr1, yr2, packed, rim, rim_packed, zs1, zs2):
     by = packed.shape[0]
     odd_y, odd_z = is_odd("gy"), is_odd("gz")
     top = row_ids() < 4
 
     def unpack(q, carry):
-        high = jnp.where(odd_y, yr2[q], yr1[q])
-        low = jnp.where(odd_y, yr1[q], yr2[q])
+        one, two = yr1[q], cleared("gy", yr2[q])
+        high = jnp.where(odd_y, two, one)
+        low = jnp.where(odd_y, one, two)
         rim[2 * q] = jnp.where(top, high, half_turn(low))
         rim[2 * q + 1] = jnp.where(top, half_turn(high), low)
         return carry
@@ -426,8 +517,8 @@
 
 
 def filter_kernel(
-    source, rim, packed, rim_packed, zr1, zr2, filtered, partial,
-    work0, work1, low_strip, high_strip, strips, ends, joint,
+    count, source, rim, packed, rim_packed, zr1, zr2, density, sums, projected_out, filtered_out,
+    work0, work1, low_strip, high_strip, strips, ends, joint, projected, filtered, sems,
 ):
     cells, by, _ = source.shape
     bx = cells - 2 * REACH
@@ -440,8 +531,9 @@
     first_z, last_z = lax.axis_index("gz") == 0, lax.axis_index("gz") == lax.axis_size("gz") - 1
 
     for m in range(tall // 2):
-        low = jnp.where(odd_z, zr1[m], zr2[m])
-        high = jnp.where(odd_z, zr2[m], zr1[m])
+        one, two = zr1[m], cleared("gz", zr2[m])
+        low = jnp.where(odd_z, one, two)
+        high = jnp.where(odd_z, two, one)
         for part in range(2):
             y = 2 * m + part
             own = half_turn(packed[y] if y < by else rim_packed[y - by])
@@ -509,13 +601,15 @@
         )
     )
     tiles = by // 8
-    total = jnp.zeros((8, LANES), F32)
+    scale = jnp.full((8, LANES), -jnp.sum(sums[...]) / count, F32) + 1e-06
+    inverse = 1.0 / scale
+    lower = math.tanh(SHARPNESS * THRESHOLD)
+    bottom = 1.0 / (lower + math.tanh(SHARPNESS * (1.0 - THRESHOLD)))
     for k in range(4):
         now, later = (work0, work1)[k % 2], (work0, work1)[(k + 1) % 2]
 
         def sweep(x, parity, k=k, now=now, later=later):
             to_first = lax.rem(LANES - x, LANES)
-            total = 0.0
             for t in range(tiles + (k < 3)):
                 at = 8 * t + 8
                 mid = now[x, at : at + 8, :]
@@ -528,24 +622,43 @@
                 own = source[x, 8 * t : 8 * t + 8, :] if t < tiles else rim[x]
                 value = value + POLY[3 - k] * own
                 if k == 3:
-                    filtered[x - REACH, 8 * t : 8 * t + 8, :] = value
-                    total = total + jnp.abs(value)
+                    rows = slice(8 * t, 8 * t + 8)
+                    filtered[x - REACH, rows, :] = value
+                    trial = density[x - REACH, rows, :] - STEP_SIZE * (value * inverse + 1.0)
+                    level = lower + jnp.tanh(SHARPNESS * (trial - THRESHOLD))
+                    projected[x - REACH, rows, :] = level * bottom
                 else:
                     if t == tiles:
                         value = jnp.where(rim_keep, value, 0.0)
                     put(later, x, t, value)
-            return total
 
         first, left = (1, cells - 2) if k < 3 else (REACH, bx)
         group = max(g for g in range(2, 19, 2) if left % g == 0)
 
-        def sweeps(j, total, first=first, group=group, sweep=sweep, k=k):
+        def sweeps(j, carry, first=first, group=group, sweep=sweep):
             for g in range(group):
-                more = sweep(first + j * group + g, (first + g) % 2)
-                total = total + more if k == 3 else total
-            return total
-
-        total = lax.fori_loop(0, left // group, sweeps, total)
+                sweep(first + j * group + g, (first + g) % 2)
+            return carry
+
+        def leave(j, group=group):
+            at = pl.ds(j * group, group)
+            return [
+                pltpu.make_async_copy(here.at[at], there.at[at], sems.at[i, j])
+                for i, (here, there) in enumerate(
+                    ((projected, projected_out), (filtered, filtered_out))
+                )
+            ]
+
+        if k < 3:
+            lax.fori_loop(0, left // group, sweeps, 0)
+        else:
+            for j in range(left // group):
+                sweeps(j, 0)
+                for copy in leave(j):
+                    copy.start()
+            for j in range(left // group):
+                for copy in leave(j):
+                    copy.wait()
         if k < 3:
 
             @pl.when(first_x)
@@ -556,32 +669,13 @@
             def _(later=later):
                 later[bx + REACH : cells] = jnp.zeros((REACH,) + later.shape[1:], F32)
 
-    partial[...] = jnp.broadcast_to(jnp.sum(total, axis=0, keepdims=True), partial.shape)
-
-
-def project_kernel(count, density, filtered, sums, projected):
-    scale = jnp.sum(sums[...]) / count + 1e-06
-    inverse = jnp.full((8, LANES), 1.0, F32) / scale
-    lower = math.tanh(SHARPNESS * THRESHOLD)
-    bottom = lower + math.tanh(SHARPNESS * (1.0 - THRESHOLD))
-
-    def one(x, carry):
-        for t in range(density.shape[1] // 8):
-            rows = slice(8 * t, 8 * t + 8)
-            trial = density[x, rows, :] - STEP_SIZE * (filtered[x, rows, :] * inverse + 1.0)
-            level = lower + jnp.tanh(SHARPNESS * (trial - THRESHOLD))
-            projected[x, rows, :] = level * (1.0 / bottom)
-        return carry
-
-    lax.fori_loop(0, density.shape[0], one, 0, unroll=8)
-
-
-def call(kernel, outs, scratch=(), cost=0):
+
+def call(kernel, outs, scratch=(), cost=0, out_place=VMEM):
     return pl.pallas_call(
         kernel,
         out_shape=[jax.ShapeDtypeStruct(s, F32) for s in outs],
-        out_specs=[VMEM] * len(outs),
-        scratch_shapes=[pltpu.VMEM(s, F32) for s in scratch],
+        out_specs=[out_place] * len(outs),
+        scratch_shapes=[pltpu.VMEM(s, F32) if isinstance(s, tuple) else s for s in scratch],
         compiler_params=pltpu.CompilerParams(**PARAMS),
         cost_estimate=pl.CostEstimate(flops=cost, bytes_accessed=cost, transcendentals=0),
     )
@@ -592,31 +686,38 @@
     assert bz == LANES and bx <= HALF and bx % 2 == 0 and by % 16 == 0
     cells, tall = bx + 2 * REACH, by + 8
     devices = lax.axis_size(AXES)
-    odd_y = is_odd("gy")
-    given = displacement, density, cell_flags, trim_level
-
-    def y_face(at_low):
-        start = jnp.where(at_low, 0, by - 1)
-        return lax.dynamic_slice_in_dim(displacement, start, 1, 2).reshape(3 * bx, bz)
-
-    yr1, yr2 = swap(y_face(odd_y), y_face(jnp.logical_not(odd_y)), "gy")
+    ys1, ys2 = call(sides_kernel, [(3 * bx, LANES)] * 2)(displacement)
+    yr1, yr2 = swap(ys1, ys2, "gy")
     n = 3 * (by // 16)
     low, high = call(faces_kernel, [(n, 8, LANES)] * 2, cost=6_000_000)(displacement)
-    zs1, zs2 = call(ends_kernel, [(n + 1, 8, LANES)] * 2)(low, high, yr1, yr2)
+    zs1, zs2, yr2 = call(ends_kernel, [(n + 1, 8, LANES)] * 2 + [(3 * bx, LANES)])(
+        low, high, yr1, yr2
+    )
     zr1, zr2 = swap(zs1, zs2, "gz")
+    flags_here, zs1 = lax.optimization_barrier((cell_flags, zs1))
+    coef = cell_coef(density, flags_here, trim_level)
+    brick = (bx, by, LANES)
     rows = x_rows(by)[2]
     xs1, xs2, rims = call(
         outward_kernel, [(rows, LANES), (rows, LANES), (2 * ends_tiles(by), 8, LANES)]
-    )(*given, yr1, yr2, zr1, zr2)
+    )(displacement, coef, yr1, yr2, zr1, zr2)
     xr1, xr2 = swap(xs1, xs2, "gx")
     along = (9, by + 16, LANES)
     ring = (2, 24, by, LANES)
-    (inner,) = call(
-        inner_kernel, [(bx - 2, by, LANES)], [along, along, ring], cost=60_000_000
-    )(*given, yr1, yr2, rims)
-    source, ys1, ys2, packed = call(
+    inner, partial, weights = call(
+        inner_kernel,
+        [(bx - 2, by, LANES), (8, LANES), (REACH + 1, by, LANES)],
+        [along, along, ring],
+        cost=60_000_000,
+    )(displacement, coef, yr1, yr2, rims)
+    source, ys1, ys2, total = call(
         outer_kernel,
-        [(cells, by, LANES), (cells // 2, 8, LANES), (cells // 2, 8, LANES), (by, 8, LANES)],
+        [
+            (cells, by, LANES),
+            (cells // 2, 8, LANES),
+            (cells // 2, 8, LANES),
+            (8, LANES),
+        ],
         [
             (2, 3, WIDE + 2, tall, LANES),
             (2, REACH + 1, by, LANES),
@@ -625,16 +726,18 @@
             along,
             ring,
         ],
-    )(*given, yr1, yr2, rims, xr1, xr2, inner)
+    )(displacement, coef, yr1, yr2, rims, xr1, xr2, inner, partial, weights)
     yr1, yr2 = swap(ys1, ys2, "gy")
+    packed, sums = call(pack_kernel, [(by, 8, LANES), (devices, LANES)])(source, total)
+    sums = lax.all_to_all(sums, AXES, split_axis=0, concat_axis=0, tiled=True)
     rim, rim_packed, zs1, zs2 = call(
         corner_kernel,
         [(cells, 8, LANES), (8, 8, LANES), (tall // 2, 8, LANES), (tall // 2, 8, LANES)],
     )(yr1, yr2, packed)
     zr1, zr2 = swap(zs1, zs2, "gz")
-    filtered, partial = call(
-        filter_kernel,
-        [(bx, by, LANES), (devices, LANES)],
+    return call(
+        functools.partial(filter_kernel, float(bx * by * bz * devices)),
+        [brick, brick],
         [
             (cells, by + 24, LANES),
             (cells, by + 24, LANES),
@@ -643,14 +746,12 @@
             (2, tall, 8, LANES),
             (4, 2, tall, LANES),
             (4, 2, tall, LANES),
+            brick,
+            brick,
+            pltpu.SemaphoreType.DMA((2, bx)),
         ],
-    )(source, rim, packed, rim_packed, zr1, zr2)
-    sums = lax.all_to_all(partial, AXES, split_axis=0, concat_axis=0, tiled=True)
-    count = float(filtered.size * devices)
-    (projected,) = call(functools.partial(project_kernel, count), [(bx, by, LANES)])(
-        density, filtered, sums
-    )
-    return projected, filtered
+        out_place=pl.BlockSpec(memory_space=pl.ANY),
+    )(source, rim, packed, rim_packed, zr1, zr2, density, sums)
 
 
 def solution(mesh):

time: 104 us -> 79.7 us (0.77)
  blocking collectives: 29.2 us -> 0 us
  starting transfers between devices: 27.8 us -> 38 us
  local copies, waits for them, and re-layouts: 8.31 us -> 1.9 us
  waiting for transfers between devices: 5.55 us -> 6.85 us
    all_to_all x1 -> x0, blocking collectives: 29.2 us -> none  [body(): lax.all_to_all(partial, AXES, split_axis=0, concat_axis=0, tiled=True)]
    all_to_all x0 -> x1, starting transfers between devices: none -> 15 us  [body(): sums = lax.all_to_all(sums, AXES, split_axis=0, concat_axis=0, tiled=True)]
    unnamed x12 -> x10, local copies, waits for them, and re-layouts: 6.79 us -> 1.9 us
    ppermute x10, starting transfers between devices: 27.8 us -> 23 us  [the longest x5 12.5 us: swap(): lax.ppermute(second, AXES, far_ones)]
    dynamic_slice x1 -> x0, local copies, waits for them, and re-layouts: 1.53 us -> none  [y_face(): lax.dynamic_slice_in_dim(displacement, start, 1, 2).reshape(3 * bx, bz)]
    ppermute x10, waiting for transfers between devices: 5.55 us -> 6.85 us  [the longest x5 4.35 us: swap(): lax.ppermute(second, AXES, far_ones)]
    pallas_call x4 -> x5, Pallas kernels: 26.4 us -> 26.4 us  [the longest x1 16.4 us: body(): call(inner_kernel, [(bx - 2, by, LANES), (8, LANES), (REACH + 1, by, LANE...]
  transfers between devices with their start and end apart: 10 -> 11, of which waited for: 3 -> 3; matrix products, arithmetic and copies ran while one was open for 0% -> 1% of each run, Pallas kernels for 18% -> 23%
where the time goes in v3:
time: 79.7 us; the launch traced here: 79.5 us
  starting transfers between devices  38 us (48%)
  Pallas kernels  31.5 us (40%)
  waiting for transfers between devices  6.85 us (9%)
  local copies, waits for them, and re-layouts  1.9 us (2%)
  between operations  0.9 us (1%)
    pallas_call x1, Pallas kernels, body(): call(inner_kernel, [(bx - 2, by, LANES), (8, LANES), (REACH + 1, by, LANE...  16.4 us
    all_to_all x1, starting transfers between devices, body(): sums = lax.all_to_all(sums, AXES, split_axis=0, concat_axis=0, tiled=True)  15 us
    ppermute x5, starting transfers between devices, swap(): lax.ppermute(second, AXES, far_ones)  12.5 us
    ppermute x5, starting transfers between devices, swap(): lax.ppermute(first, AXES, near)  10.5 us
    pallas_call x1, Pallas kernels, body(): call(functools.partial(filter_kernel, float(bx * by * bz * devices)), [br...  8.38 us
    ppermute x5, waiting for transfers between devices, swap(): lax.ppermute(second, AXES, far_ones)  4.35 us
    pallas_call x1, Pallas kernels, body(): call(outer_kernel, [(cells, by, LANES), (cells // 2, 8, LANES), (cells //...  2.96 us
    ppermute x5, waiting for transfers between devices, swap(): lax.ppermute(first, AXES, near)  2.5 us
  transfers between devices with their start and end apart: 11, of which 3 were waited for; matrix products, arithmetic and copies ran while one was open for 1% of the time, Pallas kernels for 23%

profile of v3, /device:TPU:1, one launch (start us, length us, event | category | flops | bytes accessed | tf_op | source)
XLA Modules:
  0.0 79.5 jit_solution(3038777337512275965)
XLA Ops:
  0.6 0.0 copy-start
  0.6 1.9 %copy-done = f32[3,64,32,128]{3,2,1,0:T(8,128)S(1)} copy-done((f32[3,64,32,128]{3,2,1,0:T(8,128)S(1)}, f32[3,64,32,128]{3,2,1,0:T(8,128)}, u32[]{:S(2)}) %copy-start) | copy-done | bytes 3145752
  2.5 0.2 shard_map.60
  2.7 2.1 %collective-permute-start = (f32[192,128]{1,0:T(8,128)S(1)}, f32[192,128]{1,0:T(8,128)S(1)}, u32[]{:S(2)}, u32[]{:S(2)}) collective-permute-start(f32[192,128]{1,0:T(8,128)S(1)} %get-tuple-element.28), channel_id=1, source_target_pairs={{0,4},{1,5},{2,6},{3,7},{4,0},{5,1},{6,2},{7,3},{8,12},{9,13},{10,... | collective-permute-start | bytes 294920 | tf_op jit(solution)/shard_map/ppermute | solution.py:75
  4.8 1.3 %collective-permute-start.1 = (f32[192,128]{1,0:T(8,128)S(1)}, f32[192,128]{1,0:T(8,128)S(1)}, u32[]{:S(2)}, u32[]{:S(2)}) collective-permute-start(f32[192,128]{1,0:T(8,128)S(1)} %get-tuple-element.29), channel_id=1, source_target_pairs={{0,1},{1,0},{2,3},{3,2},{4,8},{5,9},{6,10},{7,11},{8,4},{9,5},{10,... | collective-permute-start | bytes 294920 | tf_op jit(solution)/shard_map/ppermute | solution.py:75
  6.2 1.7 %shard_map.59 = (f32[6,8,128]{2,1,0:T(8,128)S(1)}, f32[6,8,128]{2,1,0:T(8,128)S(1)}) custom-call(f32[3,64,32,128]{3,2,1,0:T(8,128)S(1)} %copy-done), custom_call_target="tpu_custom_call" | custom-call | flops 6000000 | bytes 6000000 | tf_op jit(solution)/shard_map/pallas_call | solution.py:692
  7.9 0.0 collective-permute-done.yr1
  7.9 0.0 collective-permute-done.1.yr2_raw
  7.9 0.1 shard_map.61
  8.0 2.9 %collective-permute-start.2 = (f32[7,8,128]{2,1,0:T(8,128)S(1)}, f32[7,8,128]{2,1,0:T(8,128)S(1)}, u32[]{:S(2)}, u32[]{:S(2)}) collective-permute-start(f32[7,8,128]{2,1,0:T(8,128)S(1)} %get-tuple-element.30), channel_id=1, source_target_pairs={{0,1},{1,0},{2,3},{3,2},{4,5},{5,4},{6,7},{7,6},{8,9},{9,8},{10,11... | collective-permute-start | bytes 86024 | tf_op jit(solution)/shard_map/ppermute | solution.py:75
  10.9 5.2 %collective-permute-start.3 = (f32[7,8,128]{2,1,0:T(8,128)S(1)}, f32[7,8,128]{2,1,0:T(8,128)S(1)}, u32[]{:S(2)}, u32[]{:S(2)}) collective-permute-start(f32[7,8,128]{2,1,0:T(8,128)S(1)} %get-tuple-element.33), channel_id=1, source_target_pairs={{0,4},{1,2},{2,1},{3,7},{4,0},{5,6},{6,5},{7,3},{8,12},{9,10},{10,... | collective-permute-start | bytes 86024 | tf_op jit(solution)/shard_map/ppermute | solution.py:75
  16.0 0.4 fusion.coef
  16.4 1.6 %collective-permute-done.3.zr2 = f32[7,8,128]{2,1,0:T(8,128)S(1)} collective-permute-done((f32[7,8,128]{2,1,0:T(8,128)S(1)}, f32[7,8,128]{2,1,0:T(8,128)S(1)}, u32[]{:S(2)}, u32[]{:S(2)}) %collective-permute-start.3) | collective-permute-done | bytes 28704 | tf_op jit(solution)/shard_map/ppermute | solution.py:75
  18.1 0.0 collective-permute-done.2.zr1
  18.1 0.1 shard_map.62
  18.2 0.9 %collective-permute-start.4 = (f32[872,128]{1,0:T(8,128)S(1)}, f32[872,128]{1,0:T(8,128)S(1)}, u32[]{:S(2)}, u32[]{:S(2)}) collective-permute-start(f32[872,128]{1,0:T(8,128)S(1)} %get-tuple-element.35), channel_id=1, source_target_pairs={{0,16},{1,17},{2,18},{3,19},{4,20},{5,21},{6,22},{7,23},{8,24},{9,... | collective-permute-start | bytes 1339400 | tf_op jit(solution)/shard_map/ppermute | solution.py:75
  19.1 0.0 collective-permute-start.5
  19.1 16.4 %shard_map.63 = (f32[62,32,128]{2,1,0:T(8,128)S(1)}, f32[8,128]{1,0:T(8,128)S(1)}, f32[5,32,128]{2,1,0:T(8,128)S(1)}) custom-call(f32[3,64,32,128]{3,2,1,0:T(8,128)S(1)} %copy-done.1, f32[64,32,128]{2,1,0:T(8,128)S(1)} %fusion.coef, f32[192,128]{1,0:T(8,128)S(1)} %collective-permute-done.yr1, f32[192,128]{1,0:T(8,128)S(1)} %get-tuple-element.32.yr2, ...), custom_call_target="tpu_custom_call" | custom-call | flops 60000000 | bytes 60000000 | tf_op jit(solution)/shard_map/pallas_call | solution.py:707
  35.5 0.0 collective-permute-done.4.xr1
  35.5 3.0 %shard_map.64 = (f32[72,32,128]{2,1,0:T(8,128)S(1)}, f32[36,8,128]{2,1,0:T(8,128)S(1)}, f32[36,8,128]{2,1,0:T(8,128)S(1)}, f32[8,128]{1,0:T(8,128)S(1)}) custom-call(f32[3,64,32,128]{3,2,1,0:T(8,128)S(1)} %copy-done.1, f32[64,32,128]{2,1,0:T(8,128)S(1)} %fusion.coef, f32[192,128]{1,0:T(8,128)S(1)} %collective-permute-done.yr1, ...), custom_call_target="tpu_custom_call" | custom-call | tf_op jit(solution)/shard_map/pallas_call | solution.py:713
  38.5 1.3 %shard_map.65 = (f32[32,8,128]{2,1,0:T(8,128)S(1)}, f32[256,128]{1,0:T(8,128)}) custom-call(f32[72,32,128]{2,1,0:T(8,128)S(1)} %get-tuple-element.40.source, f32[8,128]{1,0:T(8,128)S(1)} %get-tuple-element.43.total), custom_call_target="tpu_custom_call" | custom-call | tf_op jit(solution)/shard_map/pallas_call | solution.py:731
  39.8 15.0 %all-to-all-start = ((f32[256,1,128]{2,1,0:T(1,128)}), f32[256,1,128]{2,1,0:T(1,128)S(1)}, u32[]{:S(2)}, u32[]{:S(2)}) async-start(f32[256,1,128]{2,1,0:T(1,128)} %bitcast.1), calls=%async_computation | async-start | bytes 262144 | tf_op jit(solution)/shard_map/all_to_all | solution.py:732
  54.8 1.5 %collective-permute-start.6 = (f32[36,8,128]{2,1,0:T(8,128)S(1)}, f32[36,8,128]{2,1,0:T(8,128)S(1)}, u32[]{:S(2)}, u32[]{:S(2)}) collective-permute-start(f32[36,8,128]{2,1,0:T(8,128)S(1)} %get-tuple-element.41), channel_id=1, source_target_pairs={{0,4},{1,5},{2,6},{3,7},{4,0},{5,1},{6,2},{7,3},{8,12},{9,13},{10,... | collective-permute-start | bytes 442376 | tf_op jit(solution)/shard_map/ppermute | solution.py:75
  56.3 0.9 %collective-permute-start.7 = (f32[36,8,128]{2,1,0:T(8,128)S(1)}, f32[36,8,128]{2,1,0:T(8,128)S(1)}, u32[]{:S(2)}, u32[]{:S(2)}) collective-permute-start(f32[36,8,128]{2,1,0:T(8,128)S(1)} %get-tuple-element.42), channel_id=1, source_target_pairs={{0,1},{1,0},{2,3},{3,2},{4,8},{5,9},{6,10},{7,11},{8,4},{9,5},{10,... | collective-permute-start | bytes 442376 | tf_op jit(solution)/shard_map/ppermute | solution.py:75
  57.1 2.5 %collective-permute-done.6.yr1 = f32[36,8,128]{2,1,0:T(8,128)S(1)} collective-permute-done((f32[36,8,128]{2,1,0:T(8,128)S(1)}, f32[36,8,128]{2,1,0:T(8,128)S(1)}, u32[]{:S(2)}, u32[]{:S(2)}) %collective-permute-start.6) | collective-permute-done | bytes 147488 | tf_op jit(solution)/shard_map/ppermute | solution.py:75
  59.6 0.0 collective-permute-done.7.yr2
  59.6 0.3 shard_map.66
  59.9 3.2 %collective-permute-start.8 = (f32[20,8,128]{2,1,0:T(8,128)S(1)}, f32[20,8,128]{2,1,0:T(8,128)S(1)}, u32[]{:S(2)}, u32[]{:S(2)}) collective-permute-start(f32[20,8,128]{2,1,0:T(8,128)S(1)} %get-tuple-element.47), channel_id=1, source_target_pairs={{0,1},{1,0},{2,3},{3,2},{4,5},{5,4},{6,7},{7,6},{8,9},{9,8},{10,11... | collective-permute-start | bytes 245768 | tf_op jit(solution)/shard_map/ppermute | solution.py:75
  63.1 5.2 %collective-permute-start.9 = (f32[20,8,128]{2,1,0:T(8,128)S(1)}, f32[20,8,128]{2,1,0:T(8,128)S(1)}, u32[]{:S(2)}, u32[]{:S(2)}) collective-permute-start(f32[20,8,128]{2,1,0:T(8,128)S(1)} %get-tuple-element.48), channel_id=1, source_target_pairs={{0,4},{1,2},{2,1},{3,7},{4,0},{5,6},{6,5},{7,3},{8,12},{9,10},{10,... | collective-permute-start | bytes 245768 | tf_op jit(solution)/shard_map/ppermute | solution.py:75
  68.2 2.7 %collective-permute-done.9.zr2 = f32[20,8,128]{2,1,0:T(8,128)S(1)} collective-permute-done((f32[20,8,128]{2,1,0:T(8,128)S(1)}, f32[20,8,128]{2,1,0:T(8,128)S(1)}, u32[]{:S(2)}, u32[]{:S(2)}) %collective-permute-start.9) | collective-permute-done | bytes 81952 | tf_op jit(solution)/shard_map/ppermute | solution.py:75
  71.0 0.0 all-to-all-done
  71.0 8.4 %shard_map.67 = (f32[64,32,128]{2,1,0:T(8,128)}, f32[64,32,128]{2,1,0:T(8,128)}) custom-call(f32[72,32,128]{2,1,0:T(8,128)S(1)} %get-tuple-element.40.source, f32[72,8,128]{2,1,0:T(8,128)S(1)} %get-tuple-element.45.rim, f32[32,8,128]{2,1,0:T(8,128)S(1)} %get-tuple-element.44.packed, f32[8,8,128]{2,1,0:T(8,128)S(1)} %get-tuple-element.46.rim_packed, ...), custom_call_target="tpu_custom_call" | custom-call | tf_op jit(solution)/shard_map/pallas_call | solution.py:738
  (10 shorter events, 0.0 us)
Async XLA Ops:
  0.6 1.9 %copy-start = (f32[3,64,32,128]{3,2,1,0:T(8,128)S(1)}, f32[3,64,32,128]{3,2,1,0:T(8,128)}, u32[]{:S(2)}) copy-start(f32[3,64,32,128]{3,2,1,0:T(8,128)} %disp.9) | copy-start | bytes 9437188
  2.5 13.5 %copy-start.2 = (f32[64,32,128]{2,1,0:T(8,128)S(1)}, f32[64,32,128]{2,1,0:T(8,128)}, u32[]{:S(2)}) copy-start(f32[64,32,128]{2,1,0:T(8,128)} %density.1) | copy-start | bytes 3145732
  2.5 13.5 %copy-start.3 = (s32[64,32,128]{2,1,0:T(8,128)S(1)}, s32[64,32,128]{2,1,0:T(8,128)}, u32[]{:S(2)}) copy-start(s32[64,32,128]{2,1,0:T(8,128)} %param.7) | copy-start | bytes 3145732
  2.5 13.5 %copy-start.4 = (s32[64,32,128]{2,1,0:T(8,128)S(1)}, s32[64,32,128]{2,1,0:T(8,128)}, u32[]{:S(2)}) copy-start(s32[64,32,128]{2,1,0:T(8,128)} %param.6) | copy-start | bytes 3145732
  2.7 5.1 %collective-permute-start = (f32[192,128]{1,0:T(8,128)S(1)}, f32[192,128]{1,0:T(8,128)S(1)}, u32[]{:S(2)}, u32[]{:S(2)}) collective-permute-start(f32[192,128]{1,0:T(8,128)S(1)} %get-tuple-element.28), channel_id=1, source_target_pairs={{0,4},{1,5},{2,6},{3,7},{4,0},{5,1},{6,2},{7,3},{8,12},{9,13},{10,... | collective-permute-start | bytes 294920 | tf_op jit(solution)/shard_map/ppermute | solution.py:75
  4.8 13.2 %copy-start.1 = (f32[3,64,32,128]{3,2,1,0:T(8,128)S(1)}, f32[3,64,32,128]{3,2,1,0:T(8,128)}, u32[]{:S(2)}) copy-start(f32[3,64,32,128]{3,2,1,0:T(8,128)} %disp.9) | copy-start | bytes 9437188
  4.8 3.0 %collective-permute-start.1 = (f32[192,128]{1,0:T(8,128)S(1)}, f32[192,128]{1,0:T(8,128)S(1)}, u32[]{:S(2)}, u32[]{:S(2)}) collective-permute-start(f32[192,128]{1,0:T(8,128)S(1)} %get-tuple-element.29), channel_id=1, source_target_pairs={{0,1},{1,0},{2,3},{3,2},{4,8},{5,9},{6,10},{7,11},{8,4},{9,5},{10,... | collective-permute-start | bytes 294920 | tf_op jit(solution)/shard_map/ppermute | solution.py:75
  8.0 10.1 %collective-permute-start.2 = (f32[7,8,128]{2,1,0:T(8,128)S(1)}, f32[7,8,128]{2,1,0:T(8,128)S(1)}, u32[]{:S(2)}, u32[]{:S(2)}) collective-permute-start(f32[7,8,128]{2,1,0:T(8,128)S(1)} %get-tuple-element.30), channel_id=1, source_target_pairs={{0,1},{1,0},{2,3},{3,2},{4,5},{5,4},{6,7},{7,6},{8,9},{9,8},{10,11... | collective-permute-start | bytes 86024 | tf_op jit(solution)/shard_map/ppermute | solution.py:75
  10.9 7.2 %collective-permute-start.3 = (f32[7,8,128]{2,1,0:T(8,128)S(1)}, f32[7,8,128]{2,1,0:T(8,128)S(1)}, u32[]{:S(2)}, u32[]{:S(2)}) collective-permute-start(f32[7,8,128]{2,1,0:T(8,128)S(1)} %get-tuple-element.33), channel_id=1, source_target_pairs={{0,4},{1,2},{2,1},{3,7},{4,0},{5,6},{6,5},{7,3},{8,12},{9,10},{10,... | collective-permute-start | bytes 86024 | tf_op jit(solution)/shard_map/ppermute | solution.py:75
  18.2 17.3 %collective-permute-start.4 = (f32[872,128]{1,0:T(8,128)S(1)}, f32[872,128]{1,0:T(8,128)S(1)}, u32[]{:S(2)}, u32[]{:S(2)}) collective-permute-start(f32[872,128]{1,0:T(8,128)S(1)} %get-tuple-element.35), channel_id=1, source_target_pairs={{0,16},{1,17},{2,18},{3,19},{4,20},{5,21},{6,22},{7,23},{8,24},{9,... | collective-permute-start | bytes 1339400 | tf_op jit(solution)/shard_map/ppermute | solution.py:75
  19.1 16.4 %collective-permute-start.5 = (f32[872,128]{1,0:T(8,128)S(1)}, f32[872,128]{1,0:T(8,128)S(1)}, u32[]{:S(2)}, u32[]{:S(2)}) collective-permute-start(f32[872,128]{1,0:T(8,128)S(1)} %get-tuple-element.36), channel_id=1, source_target_pairs={{0,1},{1,0},{2,3},{3,2},{4,5},{5,4},{6,7},{7,6},{8,9},{9,8},{10,11... | collective-permute-start | bytes 1339400 | tf_op jit(solution)/shard_map/ppermute | solution.py:75
  39.8 31.2 %all-to-all-start = ((f32[256,1,128]{2,1,0:T(1,128)}), f32[256,1,128]{2,1,0:T(1,128)S(1)}, u32[]{:S(2)}, u32[]{:S(2)}) async-start(f32[256,1,128]{2,1,0:T(1,128)} %bitcast.1), calls=%async_computation | async-start | bytes 262144 | tf_op jit(solution)/shard_map/all_to_all | solution.py:732
  54.8 4.8 %collective-permute-start.6 = (f32[36,8,128]{2,1,0:T(8,128)S(1)}, f32[36,8,128]{2,1,0:T(8,128)S(1)}, u32[]{:S(2)}, u32[]{:S(2)}) collective-permute-start(f32[36,8,128]{2,1,0:T(8,128)S(1)} %get-tuple-element.41), channel_id=1, source_target_pairs={{0,4},{1,5},{2,6},{3,7},{4,0},{5,1},{6,2},{7,3},{8,12},{9,13},{10,... | collective-permute-start | bytes 442376 | tf_op jit(solution)/shard_map/ppermute | solution.py:75
  56.3 3.4 %collective-permute-start.7 = (f32[36,8,128]{2,1,0:T(8,128)S(1)}, f32[36,8,128]{2,1,0:T(8,128)S(1)}, u32[]{:S(2)}, u32[]{:S(2)}) collective-permute-start(f32[36,8,128]{2,1,0:T(8,128)S(1)} %get-tuple-element.42), channel_id=1, source_target_pairs={{0,1},{1,0},{2,3},{3,2},{4,8},{5,9},{6,10},{7,11},{8,4},{9,5},{10,... | collective-permute-start | bytes 442376 | tf_op jit(solution)/shard_map/ppermute | solution.py:75
  59.9 8.3 %collective-permute-start.8 = (f32[20,8,128]{2,1,0:T(8,128)S(1)}, f32[20,8,128]{2,1,0:T(8,128)S(1)}, u32[]{:S(2)}, u32[]{:S(2)}) collective-permute-start(f32[20,8,128]{2,1,0:T(8,128)S(1)} %get-tuple-element.47), channel_id=1, source_target_pairs={{0,1},{1,0},{2,3},{3,2},{4,5},{5,4},{6,7},{7,6},{8,9},{9,8},{10,11... | collective-permute-start | bytes 245768 | tf_op jit(solution)/shard_map/ppermute | solution.py:75
  63.1 7.9 %collective-permute-start.9 = (f32[20,8,128]{2,1,0:T(8,128)S(1)}, f32[20,8,128]{2,1,0:T(8,128)S(1)}, u32[]{:S(2)}, u32[]{:S(2)}) collective-permute-start(f32[20,8,128]{2,1,0:T(8,128)S(1)} %get-tuple-element.48), channel_id=1, source_target_pairs={{0,4},{1,2},{2,1},{3,7},{4,0},{5,6},{6,5},{7,3},{8,12},{9,10},{10,... | collective-permute-start | bytes 245768 | tf_op jit(solution)/shard_map/ppermute | solution.py:75

commit v4 on v3

--- a/solution.py
+++ b/solution.py
@@ -48,6 +48,7 @@
 
 F32 = jnp.float32
 VMEM = pl.BlockSpec(memory_space=pltpu.VMEM)
+ANYWHERE = pl.BlockSpec(memory_space=pl.ANY)
 PARAMS = dict(vmem_limit_bytes=20 * 1024 * 1024)
 
 
@@ -224,12 +225,12 @@
 def energy_of(fields):
     grads = {}
     for name, planes in fields.items():
-        if name in NO_VALUE:
-            a, b, n = planes
-            grads[name + ("D",)], grads[name + ("S",)] = n - a, (a + n) - 2.0 * b
-        elif name in ALL_THREE:
-            three = triple(*planes)
-            grads.update({name + (x,): v for x, v in zip("MDS", three)})
+        if name in NO_VALUE or name in ALL_THREE:
+            mid, before, after = planes
+            curve = after - before
+            grads[name + ("D",)], grads[name + ("S",)] = before + after, curve
+            if name in ALL_THREE:
+                grads[name + ("M",)] = 4.0 * mid + (2.0 / 3.0) * curve
         else:
             grads.update({name + (x,): v for x, v in zip("MD", pair(*planes))})
     names = "MD", "DS"
@@ -303,6 +304,14 @@
         now[(3, "11")] = now[(2, "SD")] + now[(1, "DS")]
         fields = {}
         for f, name in enumerate(FIELDS):
+            if name in NO_VALUE or name in ALL_THREE:
+                mid = ring[0, f, rows, :]
+                after = now[name] - mid
+                if emit is not None:
+                    fields[name] = mid, ring[1, f, rows, :], after
+                ring[0, f, rows, :] = now[name]
+                ring[1, f, rows, :] = after
+                continue
             if emit is not None:
                 fields[name] = ring[slot, f, rows, :], ring[1 - slot, f, rows, :], now[name]
             ring[slot, f, rows, :] = now[name]
@@ -381,8 +390,8 @@
 
 def outer_kernel(
     disp, coef, yr1, yr2, rims, xr1, xr2, inner, partial, weights,
-    source, ys1, ys2, total,
-    field, rim_coef, ends, along0, along1, ring,
+    source, ys1, ys2, sums_out,
+    field, rim_coef, ends, total, sums, along0, along1, ring, sem,
 ):
     _, bx, by, _ = disp.shape
     cells, tall = bx + 2 * REACH, by + 8
@@ -455,6 +464,11 @@
         return carry
 
     lax.fori_loop(0, 2, one_side, 0)
+    sums[...] = jnp.broadcast_to(jnp.sum(total[...], axis=0, keepdims=True), sums.shape)
+    leave = pltpu.make_async_copy(sums, sums_out, sem)
+    leave.start()
+
+
     def copy(x, carry):
         source[x + WIDE] = inner[x]
         return carry
@@ -472,23 +486,26 @@
         return carry
 
     lax.fori_loop(0, cells // 2, rows_out, 0, unroll=6)
-
-
-def pack_columns(source, packed, count):
+    leave.wait()
+
+
+def pack_columns(source, packed, inside, count):
     cells = source.shape[0]
-    row = row_ids()
+    top = row_ids() < 4
     for y in range(count):
         tall = jnp.concatenate([source[:, y, :], jnp.zeros((LANES - cells, LANES), F32)], axis=0)
         flat = tall.T
-        packed[y] = jnp.where(row < 4, flat[0:8], flat[LANES - 8 : LANES])
-
-
-def pack_kernel(source, total, packed, sums):
-    pack_columns(source, packed, source.shape[1])
-    sums[...] = jnp.broadcast_to(jnp.sum(total[...], axis=0, keepdims=True), sums.shape)
-
-
-def corner_kernel(yr1, yr2, packed, rim, rim_packed, zs1, zs2):
+        first, last = flat[0:8], flat[LANES - 8 : LANES]
+        packed[y] = jnp.where(top, first, last)
+        inside[y] = half_turn(jnp.where(top, last, first))
+
+
+def pack_kernel(source, both):
+    pack_columns(source, both.at[0], both.at[1], source.shape[1])
+
+
+def corner_kernel(yr1, yr2, both, rim, rim_both, zs1, zs2):
+    packed, rim_packed, rim_inside = both.at[0], rim_both.at[0], rim_both.at[1]
     by = packed.shape[0]
     odd_y, odd_z = is_odd("gy"), is_odd("gz")
     top = row_ids() < 4
@@ -502,7 +519,7 @@
         return carry
 
     lax.fori_loop(0, yr1.shape[0], unpack, 0, unroll=6)
-    pack_columns(rim, rim_packed, 8)
+    pack_columns(rim, rim_packed, rim_inside, 8)
 
     def send(m, first, second):
         low = jnp.where(top, first, half_turn(second))
@@ -516,20 +533,77 @@
         send(by // 2 + m, rim_packed[2 * m], rim_packed[2 * m + 1])
 
 
-def filter_kernel(
-    count, source, rim, packed, rim_packed, zr1, zr2, density, sums, projected_out, filtered_out,
-    work0, work1, low_strip, high_strip, strips, ends, joint, projected, filtered, sems,
-):
+def sweeps_kernel(source, rim, filtered, work0, work1):
     cells, by, _ = source.shape
     bx = cells - 2 * REACH
-    tall = by + 8
-    odd_z = is_odd("gz")
-    lane, row = lane_ids(), row_ids()
-    top = row < 4
+    tiles = by // 8
+    top = row_ids() < 4
     first_x, last_x = lax.axis_index("gx") == 0, lax.axis_index("gx") == lax.axis_size("gx") - 1
     first_y, last_y = lax.axis_index("gy") == 0, lax.axis_index("gy") == lax.axis_size("gy") - 1
-    first_z, last_z = lax.axis_index("gz") == 0, lax.axis_index("gz") == lax.axis_size("gz") - 1
-
+
+    def put(ref, x, t, value):
+        ref[x, 8 * t + 8 : 8 * t + 16, :] = value
+        if t == tiles:
+            ref[x, 0:8, :] = value
+        if t == 0:
+            ref[x, by + 16 : by + 24, :] = value
+
+    def begin(x, carry):
+        for t in range(tiles):
+            put(work0, x, t, POLY[4] * source[x, 8 * t : 8 * t + 8, :])
+        put(work0, x, tiles, POLY[4] * rim[x])
+        return carry
+
+    lax.fori_loop(0, cells, begin, 0, unroll=8)
+    rim_keep = jnp.logical_not(
+        jnp.logical_or(
+            jnp.logical_and(last_y, top), jnp.logical_and(first_y, jnp.logical_not(top))
+        )
+    )
+    for k in range(4):
+        now, later = (work0, work1)[k % 2], (work0, work1)[(k + 1) % 2]
+
+        def sweep(x, k=k, now=now, later=later):
+            for t in range(tiles + (k < 3)):
+                at = 8 * t + 8
+                mid = now[x, at : at + 8, :]
+                value = now[x - 1, at : at + 8, :] + now[x + 1, at : at + 8, :]
+                value = value + (now[x, at - 1 : at + 7, :] + now[x, at + 1 : at + 9, :])
+                value = value + (pltpu.roll(mid, 1, 1) + pltpu.roll(mid, LANES - 1, 1))
+                own = source[x, 8 * t : 8 * t + 8, :] if t < tiles else rim[x]
+                value = value + POLY[3 - k] * own
+                if k == 3:
+                    filtered[x - REACH, 8 * t : 8 * t + 8, :] = value
+                else:
+                    if t == tiles:
+                        value = jnp.where(rim_keep, value, 0.0)
+                    put(later, x, t, value)
+
+        first, left = (1, cells - 2) if k < 3 else (REACH, bx)
+        group = max(g for g in range(2, 36) if left % g == 0)
+
+        def sweeps(j, carry, first=first, group=group, sweep=sweep):
+            for g in range(group):
+                sweep(first + j * group + g)
+            return carry
+
+        lax.fori_loop(0, left // group, sweeps, 0)
+        if k < 3:
+
+            @pl.when(first_x)
+            def _(later=later):
+                later[0:REACH] = jnp.zeros((REACH,) + later.shape[1:], F32)
+
+            @pl.when(last_x)
+            def _(later=later):
+                later[bx + REACH : cells] = jnp.zeros((REACH,) + later.shape[1:], F32)
+
+
+def strip_kernel(both, rim_both, zr1, zr2, strip):
+    by = both.shape[1]
+    tall = by + 8
+    packed, inside, rim_packed, rim_inside = both.at[0], both.at[1], rim_both.at[0], rim_both.at[1]
+    odd_z, top = is_odd("gz"), row_ids() < 4
     for m in range(tall // 2):
         one, two = zr1[m], cleared("gz", zr2[m])
         low = jnp.where(odd_z, one, two)
@@ -537,8 +611,22 @@
         for part in range(2):
             y = 2 * m + part
             own = half_turn(packed[y] if y < by else rim_packed[y - by])
-            low_strip[y] = jnp.where(top, half_turn(low) if part else low, own)
-            high_strip[y] = jnp.where(top, own, high if part else half_turn(high))
+            strip[y, 0] = jnp.where(top, half_turn(low) if part else low, own)
+            strip[y, 1] = jnp.where(top, own, high if part else half_turn(high))
+            strip[y, 2] = inside[y] if y < by else rim_inside[y - by]
+
+
+def finish_kernel(
+    count, inner, strip, density, sums,
+    projected_out, filtered_out, work0, work1, edges, projected, filtered, sems,
+):
+    bx, by, _ = density.shape
+    tall = by + 8
+    lane, row = lane_ids(), row_ids()
+    top = row < 4
+    first_x, last_x = lax.axis_index("gx") == 0, lax.axis_index("gx") == lax.axis_size("gx") - 1
+    first_y, last_y = lax.axis_index("gy") == 0, lax.axis_index("gy") == lax.axis_size("gy") - 1
+    first_z, last_z = lax.axis_index("gz") == 0, lax.axis_index("gz") == lax.axis_size("gz") - 1
 
     inside_x = jnp.logical_not(
         jnp.logical_or(
@@ -546,135 +634,89 @@
             jnp.logical_and(last_x, lane >= bx + REACH),
         )
     )
-    inside_low = jnp.logical_and(inside_x, jnp.logical_not(jnp.logical_and(first_z, top)))
-    inside_high = jnp.logical_and(
-        inside_x, jnp.logical_not(jnp.logical_and(last_z, jnp.logical_not(top)))
+    keeps = (
+        jnp.logical_and(inside_x, jnp.logical_not(jnp.logical_and(first_z, top))),
+        jnp.logical_and(
+            inside_x, jnp.logical_not(jnp.logical_and(last_z, jnp.logical_not(top)))
+        ),
+        inside_x,
     )
-    for side, strip, edge_row, inside in (
-        (0, low_strip, 3, inside_low),
-        (1, high_strip, 4, inside_high),
-    ):
-        strips[0] = POLY[4] * strip[...]
-        for k in range(4):
-            now, later = k % 2, (k + 1) % 2
-            for t in range(tall // 8):
-                ends[k, side, 8 * t : 8 * t + 8, :] = strips[now, 8 * t : 8 * t + 8, edge_row, :]
-            if k == 3:
-                break
-            for y in range(tall):
-                mid = strips[now, y]
-                total = strips[now, (y + 1) % tall] + strips[now, (y - 1) % tall]
-                total = total + (pltpu.roll(mid, 1, 1) + pltpu.roll(mid, LANES - 1, 1))
-                total = total + (pltpu.roll(mid, 1, 0) + pltpu.roll(mid, 7, 0))
-                total = total + POLY[3 - k] * strip[y]
-                outside = first_y if y >= by + 4 else last_y
-                keep = inside
+    work0[...] = POLY[4] * strip[...]
+    for k in range(4):
+        now, later = (work0, work1)[k % 2], (work0, work1)[(k + 1) % 2]
+        for y in range(tall if k < 3 else by):
+            low, high, mid = (now[y, part] for part in range(3))
+            ups = (
+                jnp.where(row == 7, pltpu.roll(mid, 7, 0), pltpu.roll(low, 7, 0)),
+                pltpu.roll(high, 7, 0),
+                jnp.where(row == 7, pltpu.roll(high, 7, 0), pltpu.roll(mid, 7, 0)),
+            )
+            downs = (
+                pltpu.roll(low, 1, 0),
+                jnp.where(row == 0, pltpu.roll(mid, 1, 0), pltpu.roll(high, 1, 0)),
+                jnp.where(row == 0, pltpu.roll(low, 1, 0), pltpu.roll(mid, 1, 0)),
+            )
+            for part in range(3 if k < 3 else 2):
+                tile = now[y, part]
+                value = now[(y + 1) % tall, part] + now[(y - 1) % tall, part]
+                value = value + (pltpu.roll(tile, 1, 1) + pltpu.roll(tile, LANES - 1, 1))
+                value = value + (ups[part] + downs[part])
+                value = value + POLY[3 - k] * strip[y, part]
+                keep = keeps[part]
                 if y >= by:
-                    keep = jnp.logical_and(inside, jnp.logical_not(outside))
-                strips[later, y] = jnp.where(keep, total, 0.0)
-
-    for k in range(4):
-        for t in range(tall // 8):
-            low = ends[k, 0, 8 * t : 8 * t + 8, :]
-            high = pltpu.roll(ends[k, 1, 8 * t : 8 * t + 8, :], LANES - 1, 1)
-            even = lax.rem(lane, 2) == 0
-            joint[k, 0, 8 * t : 8 * t + 8, :] = jnp.where(even, low, high)
-            joint[k, 1, 8 * t : 8 * t + 8, :] = jnp.where(even, high, low)
-
-    def put(ref, x, t, value):
-        ref[x, 8 * t + 8 : 8 * t + 16, :] = value
-        if t == by // 8:
-            ref[x, 0:8, :] = value
-        if t == 0:
-            ref[x, by + 16 : by + 24, :] = value
-
-    def begin(x, carry):
-        for t in range(by // 8):
-            put(work0, x, t, POLY[4] * source[x, 8 * t : 8 * t + 8, :])
-        put(work0, x, by // 8, POLY[4] * rim[x])
-        return carry
-
-    lax.fori_loop(0, cells, begin, 0, unroll=4)
-    rim_keep = jnp.logical_not(
-        jnp.logical_or(
-            jnp.logical_and(last_y, top), jnp.logical_and(first_y, jnp.logical_not(top))
-        )
-    )
-    tiles = by // 8
+                    outside = first_y if y >= by + 4 else last_y
+                    keep = jnp.logical_and(keep, jnp.logical_not(outside))
+                later[y, part] = jnp.where(keep, value, 0.0)
+
+    blank = jnp.zeros((LANES - 16, LANES), F32)
+    for y in range(by):
+        first = half_turn(work0[y, 0])
+        last = half_turn(work0[y, 1])
+        turned = jnp.concatenate([first, blank, last], axis=0).T
+        edges[:, y, :] = turned[0 : bx + 8, :]
+
     scale = jnp.full((8, LANES), -jnp.sum(sums[...]) / count, F32) + 1e-06
     inverse = 1.0 / scale
     lower = math.tanh(SHARPNESS * THRESHOLD)
     bottom = 1.0 / (lower + math.tanh(SHARPNESS * (1.0 - THRESHOLD)))
-    for k in range(4):
-        now, later = (work0, work1)[k % 2], (work0, work1)[(k + 1) % 2]
-
-        def sweep(x, parity, k=k, now=now, later=later):
-            to_first = lax.rem(LANES - x, LANES)
-            for t in range(tiles + (k < 3)):
-                at = 8 * t + 8
-                mid = now[x, at : at + 8, :]
-                value = now[x - 1, at : at + 8, :] + now[x + 1, at : at + 8, :]
-                value = value + (now[x, at - 1 : at + 7, :] + now[x, at + 1 : at + 9, :])
-                ends_here = pltpu.roll(joint[k, parity, 8 * t : 8 * t + 8, :], to_first, 1)
-                low = jnp.where(lane == 0, ends_here, pltpu.roll(mid, 1, 1))
-                high = jnp.where(lane == LANES - 1, ends_here, pltpu.roll(mid, LANES - 1, 1))
-                value = value + (low + high)
-                own = source[x, 8 * t : 8 * t + 8, :] if t < tiles else rim[x]
-                value = value + POLY[3 - k] * own
-                if k == 3:
-                    rows = slice(8 * t, 8 * t + 8)
-                    filtered[x - REACH, rows, :] = value
-                    trial = density[x - REACH, rows, :] - STEP_SIZE * (value * inverse + 1.0)
-                    level = lower + jnp.tanh(SHARPNESS * (trial - THRESHOLD))
-                    projected[x - REACH, rows, :] = level * bottom
-                else:
-                    if t == tiles:
-                        value = jnp.where(rim_keep, value, 0.0)
-                    put(later, x, t, value)
-
-        first, left = (1, cells - 2) if k < 3 else (REACH, bx)
-        group = max(g for g in range(2, 19, 2) if left % g == 0)
-
-        def sweeps(j, carry, first=first, group=group, sweep=sweep):
-            for g in range(group):
-                sweep(first + j * group + g, (first + g) % 2)
-            return carry
-
-        def leave(j, group=group):
-            at = pl.ds(j * group, group)
-            return [
-                pltpu.make_async_copy(here.at[at], there.at[at], sems.at[i, j])
-                for i, (here, there) in enumerate(
-                    ((projected, projected_out), (filtered, filtered_out))
-                )
-            ]
-
-        if k < 3:
-            lax.fori_loop(0, left // group, sweeps, 0)
-        else:
-            for j in range(left // group):
-                sweeps(j, 0)
-                for copy in leave(j):
-                    copy.start()
-            for j in range(left // group):
-                for copy in leave(j):
-                    copy.wait()
-        if k < 3:
-
-            @pl.when(first_x)
-            def _(later=later):
-                later[0:REACH] = jnp.zeros((REACH,) + later.shape[1:], F32)
-
-            @pl.when(last_x)
-            def _(later=later):
-                later[bx + REACH : cells] = jnp.zeros((REACH,) + later.shape[1:], F32)
-
-
-def call(kernel, outs, scratch=(), cost=0, out_place=VMEM):
+    at_face = jnp.logical_or(lane < REACH, lane >= LANES - REACH)
+
+    def project(x, carry):
+        for t in range(by // 8):
+            rows = slice(8 * t, 8 * t + 8)
+            value = jnp.where(at_face, edges[x + REACH, rows, :], inner[x, rows, :])
+            filtered[x, rows, :] = value
+            trial = density[x, rows, :] - STEP_SIZE * (value * inverse + 1.0)
+            level = lower + jnp.tanh(SHARPNESS * (trial - THRESHOLD))
+            projected[x, rows, :] = level * bottom
+        return carry
+
+    chunks = 4
+    size = bx // chunks
+
+    def leave(j):
+        at = pl.ds(j * size, size)
+        return [
+            pltpu.make_async_copy(here.at[at], there.at[at], sems.at[i, j])
+            for i, (here, there) in enumerate(
+                ((projected, projected_out), (filtered, filtered_out))
+            )
+        ]
+
+    for j in range(chunks):
+        lax.fori_loop(j * size, (j + 1) * size, project, 0, unroll=8)
+        for copy in leave(j):
+            copy.start()
+    for j in range(chunks):
+        for copy in leave(j):
+            copy.wait()
+
+
+def call(kernel, outs, scratch=(), cost=0, placed=None):
     return pl.pallas_call(
         kernel,
         out_shape=[jax.ShapeDtypeStruct(s, F32) for s in outs],
-        out_specs=[out_place] * len(outs),
+        out_specs=placed or [VMEM] * len(outs),
         scratch_shapes=[pltpu.VMEM(s, F32) if isinstance(s, tuple) else s for s in scratch],
         compiler_params=pltpu.CompilerParams(**PARAMS),
         cost_estimate=pl.CostEstimate(flops=cost, bytes_accessed=cost, transcendentals=0),
@@ -710,48 +752,58 @@
         [along, along, ring],
         cost=60_000_000,
     )(displacement, coef, yr1, yr2, rims)
-    source, ys1, ys2, total = call(
+    source, ys1, ys2, sums = call(
         outer_kernel,
         [
             (cells, by, LANES),
             (cells // 2, 8, LANES),
             (cells // 2, 8, LANES),
-            (8, LANES),
+            (devices, LANES),
         ],
         [
             (2, 3, WIDE + 2, tall, LANES),
             (2, REACH + 1, by, LANES),
             (3, 2 * ends_tiles(by), 8, LANES),
+            (8, LANES),
+            (devices, LANES),
             along,
             along,
             ring,
+            pltpu.SemaphoreType.DMA,
         ],
+        placed=[VMEM] * 3 + [ANYWHERE],
     )(displacement, coef, yr1, yr2, rims, xr1, xr2, inner, partial, weights)
     yr1, yr2 = swap(ys1, ys2, "gy")
-    packed, sums = call(pack_kernel, [(by, 8, LANES), (devices, LANES)])(source, total)
+    (both,) = call(pack_kernel, [(2, by, 8, LANES)], cost=6_000_000)(source)
     sums = lax.all_to_all(sums, AXES, split_axis=0, concat_axis=0, tiled=True)
-    rim, rim_packed, zs1, zs2 = call(
+    rim, rim_both, zs1, zs2 = call(
         corner_kernel,
-        [(cells, 8, LANES), (8, 8, LANES), (tall // 2, 8, LANES), (tall // 2, 8, LANES)],
-    )(yr1, yr2, packed)
+        [
+            (cells, 8, LANES),
+            (2, 8, 8, LANES),
+            (tall // 2, 8, LANES),
+            (tall // 2, 8, LANES),
+        ],
+    )(yr1, yr2, both)
     zr1, zr2 = swap(zs1, zs2, "gz")
+    (middle,) = call(
+        sweeps_kernel, [brick], [(cells, by + 24, LANES)] * 2, cost=20_000_000
+    )(source, rim)
+    strip_shape = (tall, 3, 8, LANES)
+    (strip,) = call(strip_kernel, [strip_shape])(both, rim_both, zr1, zr2)
     return call(
-        functools.partial(filter_kernel, float(bx * by * bz * devices)),
+        functools.partial(finish_kernel, float(bx * by * bz * devices)),
         [brick, brick],
         [
-            (cells, by + 24, LANES),
-            (cells, by + 24, LANES),
-            (tall, 8, LANES),
-            (tall, 8, LANES),
-            (2, tall, 8, LANES),
-            (4, 2, tall, LANES),
-            (4, 2, tall, LANES),
+            strip_shape,
+            strip_shape,
+            (bx + 8, by, LANES),
             brick,
             brick,
-            pltpu.SemaphoreType.DMA((2, bx)),
+            pltpu.SemaphoreType.DMA((2, 4)),
         ],
-        out_place=pl.BlockSpec(memory_space=pl.ANY),
-    )(source, rim, packed, rim_packed, zr1, zr2, density, sums)
+        placed=[ANYWHERE] * 2,
+    )(middle, strip, density, sums)
 
 
 def solution(mesh):

time: 79.7 us -> 74.2 us (0.931)
  waiting for transfers between devices: 6.85 us -> 3.42 us
  Pallas kernels: 31.5 us -> 29.4 us
    ppermute x5, waiting for transfers between devices: 4.35 us -> 1.64 us  [swap(): lax.ppermute(second, AXES, far_ones)]
    pallas_call x3 -> x5, Pallas kernels: 9.99 us -> 7.92 us  [the longest x1 3.58 us: body(): call(sweeps_kernel, [brick], [(cells, by + 24, LANES)] * 2, cost=20000000)]
  transfers between devices with their start and end apart: 11 -> 11, of which waited for: 3 -> 2; matrix products, arithmetic and copies ran while one was open for 1% -> 1% of each run, Pallas kernels for 23% -> 30%
where the time goes in v4:
time: 74.2 us; the launch traced here: 74.1 us
  starting transfers between devices  38 us (51%)
  Pallas kernels  29.4 us (40%)
  waiting for transfers between devices  3.42 us (5%)
  local copies, waits for them, and re-layouts  1.9 us (3%)
  between operations  0.95 us (1%)
    pallas_call x1, Pallas kernels, body(): call(inner_kernel, [(bx - 2, by, LANES), (8, LANES), (REACH + 1, by, LANE...  15.7 us
    all_to_all x1, starting transfers between devices, body(): sums = lax.all_to_all(sums, AXES, split_axis=0, concat_axis=0, tiled=True)  15 us
    ppermute x5, starting transfers between devices, swap(): lax.ppermute(second, AXES, far_ones)  12.3 us
    ppermute x5, starting transfers between devices, swap(): lax.ppermute(first, AXES, near)  10.7 us
    pallas_call x1, Pallas kernels, body(): call(outer_kernel, [(cells, by, LANES), (cells // 2, 8, LANES), (cells //...  3.71 us
    pallas_call x1, Pallas kernels, body(): call(sweeps_kernel, [brick], [(cells, by + 24, LANES)] * 2, cost=20000000)  3.58 us
    pallas_call x1, Pallas kernels, body(): call(functools.partial(finish_kernel, float(bx * by * bz * devices)), [br...  3.27 us
    unnamed x10, local copies, waits for them, and re-layouts  1.9 us
  transfers between devices with their start and end apart: 11, of which 2 were waited for; matrix products, arithmetic and copies ran while one was open for 1% of the time, Pallas kernels for 30%

profile of v4, /device:TPU:1, one launch (start us, length us, event | category | flops | bytes accessed | tf_op | source)
XLA Modules:
  0.0 74.1 jit_solution(16248182483761951882)
XLA Ops:
  0.6 0.0 copy-start
  0.6 1.9 %copy-done = f32[3,64,32,128]{3,2,1,0:T(8,128)S(1)} copy-done((f32[3,64,32,128]{3,2,1,0:T(8,128)S(1)}, f32[3,64,32,128]{3,2,1,0:T(8,128)}, u32[]{:S(2)}) %copy-start) | copy-done | bytes 3145752
  2.5 0.2 shard_map.60
  2.7 2.1 %collective-permute-start = (f32[192,128]{1,0:T(8,128)S(1)}, f32[192,128]{1,0:T(8,128)S(1)}, u32[]{:S(2)}, u32[]{:S(2)}) collective-permute-start(f32[192,128]{1,0:T(8,128)S(1)} %get-tuple-element.26), channel_id=1, source_target_pairs={{0,4},{1,5},{2,6},{3,7},{4,0},{5,1},{6,2},{7,3},{8,12},{9,13},{10,... | collective-permute-start | bytes 294920 | tf_op jit(solution)/shard_map/ppermute | solution.py:76
  4.8 1.3 %collective-permute-start.1 = (f32[192,128]{1,0:T(8,128)S(1)}, f32[192,128]{1,0:T(8,128)S(1)}, u32[]{:S(2)}, u32[]{:S(2)}) collective-permute-start(f32[192,128]{1,0:T(8,128)S(1)} %get-tuple-element.27), channel_id=1, source_target_pairs={{0,1},{1,0},{2,3},{3,2},{4,8},{5,9},{6,10},{7,11},{8,4},{9,5},{10,... | collective-permute-start | bytes 294920 | tf_op jit(solution)/shard_map/ppermute | solution.py:76
  6.2 1.7 %shard_map.59 = (f32[6,8,128]{2,1,0:T(8,128)S(1)}, f32[6,8,128]{2,1,0:T(8,128)S(1)}) custom-call(f32[3,64,32,128]{3,2,1,0:T(8,128)S(1)} %copy-done), custom_call_target="tpu_custom_call" | custom-call | flops 6000000 | bytes 6000000 | tf_op jit(solution)/shard_map/pallas_call | solution.py:734
  7.9 0.0 collective-permute-done.yr1
  7.9 0.0 collective-permute-done.1.yr2_raw
  7.9 0.1 shard_map.61
  8.0 2.9 %collective-permute-start.2 = (f32[7,8,128]{2,1,0:T(8,128)S(1)}, f32[7,8,128]{2,1,0:T(8,128)S(1)}, u32[]{:S(2)}, u32[]{:S(2)}) collective-permute-start(f32[7,8,128]{2,1,0:T(8,128)S(1)} %get-tuple-element.28), channel_id=1, source_target_pairs={{0,1},{1,0},{2,3},{3,2},{4,5},{5,4},{6,7},{7,6},{8,9},{9,8},{10,11... | collective-permute-start | bytes 86024 | tf_op jit(solution)/shard_map/ppermute | solution.py:76
  10.9 5.2 %collective-permute-start.3 = (f32[7,8,128]{2,1,0:T(8,128)S(1)}, f32[7,8,128]{2,1,0:T(8,128)S(1)}, u32[]{:S(2)}, u32[]{:S(2)}) collective-permute-start(f32[7,8,128]{2,1,0:T(8,128)S(1)} %get-tuple-element.31), channel_id=1, source_target_pairs={{0,4},{1,2},{2,1},{3,7},{4,0},{5,6},{6,5},{7,3},{8,12},{9,10},{10,... | collective-permute-start | bytes 86024 | tf_op jit(solution)/shard_map/ppermute | solution.py:76
  16.0 0.4 fusion.coef
  16.4 1.6 %collective-permute-done.3.zr2 = f32[7,8,128]{2,1,0:T(8,128)S(1)} collective-permute-done((f32[7,8,128]{2,1,0:T(8,128)S(1)}, f32[7,8,128]{2,1,0:T(8,128)S(1)}, u32[]{:S(2)}, u32[]{:S(2)}) %collective-permute-start.3) | collective-permute-done | bytes 28704 | tf_op jit(solution)/shard_map/ppermute | solution.py:76
  18.1 0.0 collective-permute-done.2.zr1
  18.1 0.1 shard_map.62
  18.2 0.9 %collective-permute-start.4 = (f32[872,128]{1,0:T(8,128)S(1)}, f32[872,128]{1,0:T(8,128)S(1)}, u32[]{:S(2)}, u32[]{:S(2)}) collective-permute-start(f32[872,128]{1,0:T(8,128)S(1)} %get-tuple-element.33), channel_id=1, source_target_pairs={{0,16},{1,17},{2,18},{3,19},{4,20},{5,21},{6,22},{7,23},{8,24},{9,... | collective-permute-start | bytes 1339400 | tf_op jit(solution)/shard_map/ppermute | solution.py:76
  19.1 0.0 collective-permute-start.5
  19.1 15.7 %shard_map.63 = (f32[62,32,128]{2,1,0:T(8,128)S(1)}, f32[8,128]{1,0:T(8,128)S(1)}, f32[5,32,128]{2,1,0:T(8,128)S(1)}) custom-call(f32[3,64,32,128]{3,2,1,0:T(8,128)S(1)} %copy-done.1, f32[64,32,128]{2,1,0:T(8,128)S(1)} %fusion.coef, f32[192,128]{1,0:T(8,128)S(1)} %collective-permute-done.yr1, f32[192,128]{1,0:T(8,128)S(1)} %get-tuple-element.30.yr2, ...), custom_call_target="tpu_custom_call" | custom-call | flops 60000000 | bytes 60000000 | tf_op jit(solution)/shard_map/pallas_call | solution.py:749
  34.8 0.0 collective-permute-done.5.xr2
  34.8 3.7 %shard_map.64 = (f32[72,32,128]{2,1,0:T(8,128)S(1)}, f32[36,8,128]{2,1,0:T(8,128)S(1)}, f32[36,8,128]{2,1,0:T(8,128)S(1)}, f32[256,128]{1,0:T(8,128)}) custom-call(f32[3,64,32,128]{3,2,1,0:T(8,128)S(1)} %copy-done.1, f32[64,32,128]{2,1,0:T(8,128)S(1)} %fusion.coef, f32[192,128]{1,0:T(8,128)S(1)} %collective-permute-done.yr1, ...), custom_call_target="tpu_custom_call" | custom-call | tf_op jit(solution)/shard_map/pallas_call | solution.py:755
  38.5 15.0 %all-to-all-start = ((f32[256,1,128]{2,1,0:T(1,128)}), f32[256,1,128]{2,1,0:T(1,128)S(1)}, u32[]{:S(2)}, u32[]{:S(2)}) async-start(f32[256,1,128]{2,1,0:T(1,128)} %bitcast.1), calls=%async_computation | async-start | bytes 262144 | tf_op jit(solution)/shard_map/all_to_all | solution.py:778
  53.5 1.5 %collective-permute-start.6 = (f32[36,8,128]{2,1,0:T(8,128)S(1)}, f32[36,8,128]{2,1,0:T(8,128)S(1)}, u32[]{:S(2)}, u32[]{:S(2)}) collective-permute-start(f32[36,8,128]{2,1,0:T(8,128)S(1)} %get-tuple-element.39), channel_id=1, source_target_pairs={{0,4},{1,5},{2,6},{3,7},{4,0},{5,1},{6,2},{7,3},{8,12},{9,13},{10,... | collective-permute-start | bytes 442376 | tf_op jit(solution)/shard_map/ppermute | solution.py:76
  55.0 0.9 %collective-permute-start.7 = (f32[36,8,128]{2,1,0:T(8,128)S(1)}, f32[36,8,128]{2,1,0:T(8,128)S(1)}, u32[]{:S(2)}, u32[]{:S(2)}) collective-permute-start(f32[36,8,128]{2,1,0:T(8,128)S(1)} %get-tuple-element.40), channel_id=1, source_target_pairs={{0,1},{1,0},{2,3},{3,2},{4,8},{5,9},{6,10},{7,11},{8,4},{9,5},{10,... | collective-permute-start | bytes 442376 | tf_op jit(solution)/shard_map/ppermute | solution.py:76
  55.9 0.7 shard_map.65.both
  56.6 1.8 %collective-permute-done.6.yr1 = f32[36,8,128]{2,1,0:T(8,128)S(1)} collective-permute-done((f32[36,8,128]{2,1,0:T(8,128)S(1)}, f32[36,8,128]{2,1,0:T(8,128)S(1)}, u32[]{:S(2)}, u32[]{:S(2)}) %collective-permute-start.6) | collective-permute-done | bytes 147488 | tf_op jit(solution)/shard_map/ppermute | solution.py:76
  58.4 0.3 shard_map.66
  58.7 3.3 %collective-permute-start.8 = (f32[20,8,128]{2,1,0:T(8,128)S(1)}, f32[20,8,128]{2,1,0:T(8,128)S(1)}, u32[]{:S(2)}, u32[]{:S(2)}) collective-permute-start(f32[20,8,128]{2,1,0:T(8,128)S(1)} %get-tuple-element.43), channel_id=1, source_target_pairs={{0,1},{1,0},{2,3},{3,2},{4,5},{5,4},{6,7},{7,6},{8,9},{9,8},{10,11... | collective-permute-start | bytes 245768 | tf_op jit(solution)/shard_map/ppermute | solution.py:76
  62.0 5.0 %collective-permute-start.9 = (f32[20,8,128]{2,1,0:T(8,128)S(1)}, f32[20,8,128]{2,1,0:T(8,128)S(1)}, u32[]{:S(2)}, u32[]{:S(2)}) collective-permute-start(f32[20,8,128]{2,1,0:T(8,128)S(1)} %get-tuple-element.44), channel_id=1, source_target_pairs={{0,4},{1,2},{2,1},{3,7},{4,0},{5,6},{6,5},{7,3},{8,12},{9,10},{10,... | collective-permute-start | bytes 245768 | tf_op jit(solution)/shard_map/ppermute | solution.py:76
  67.0 3.6 %shard_map.67.inner = f32[64,32,128]{2,1,0:T(8,128)S(1)} custom-call(f32[72,32,128]{2,1,0:T(8,128)S(1)} %get-tuple-element.38.source, f32[72,8,128]{2,1,0:T(8,128)S(1)} %get-tuple-element.41.rim), custom_call_target="tpu_custom_call" | custom-call | flops 20000000 | bytes 20000000 | tf_op jit(solution)/shard_map/pallas_call | solution.py:789
  70.6 0.0 collective-permute-done.8.zr1
  70.6 0.0 all-to-all-done
  70.6 3.3 %shard_map.69 = (f32[64,32,128]{2,1,0:T(8,128)}, f32[64,32,128]{2,1,0:T(8,128)}) custom-call(f32[64,32,128]{2,1,0:T(8,128)S(1)} %shard_map.67.inner, f32[40,3,8,128]{3,2,1,0:T(8,128)S(1)} %shard_map.68.strip, f32[64,32,128]{2,1,0:T(8,128)S(1)} %copy-done.2, f32[256,128]{1,0:T(8,128)S(1)} %bitcast.4), custom_call_target="tpu_custom_call" | custom-call | tf_op jit(solution)/shard_map/pallas_call | solution.py:794
  (12 shorter events, 0.1 us)
Async XLA Ops:
  0.6 1.9 %copy-start = (f32[3,64,32,128]{3,2,1,0:T(8,128)S(1)}, f32[3,64,32,128]{3,2,1,0:T(8,128)}, u32[]{:S(2)}) copy-start(f32[3,64,32,128]{3,2,1,0:T(8,128)} %disp.9) | copy-start | bytes 9437188
  2.5 13.5 %copy-start.2 = (f32[64,32,128]{2,1,0:T(8,128)S(1)}, f32[64,32,128]{2,1,0:T(8,128)}, u32[]{:S(2)}) copy-start(f32[64,32,128]{2,1,0:T(8,128)} %density.1) | copy-start | bytes 3145732
  2.5 13.5 %copy-start.3 = (s32[64,32,128]{2,1,0:T(8,128)S(1)}, s32[64,32,128]{2,1,0:T(8,128)}, u32[]{:S(2)}) copy-start(s32[64,32,128]{2,1,0:T(8,128)} %param.7) | copy-start | bytes 3145732
  2.5 13.5 %copy-start.4 = (s32[64,32,128]{2,1,0:T(8,128)S(1)}, s32[64,32,128]{2,1,0:T(8,128)}, u32[]{:S(2)}) copy-start(s32[64,32,128]{2,1,0:T(8,128)} %param.6) | copy-start | bytes 3145732
  2.7 5.1 %collective-permute-start = (f32[192,128]{1,0:T(8,128)S(1)}, f32[192,128]{1,0:T(8,128)S(1)}, u32[]{:S(2)}, u32[]{:S(2)}) collective-permute-start(f32[192,128]{1,0:T(8,128)S(1)} %get-tuple-element.26), channel_id=1, source_target_pairs={{0,4},{1,5},{2,6},{3,7},{4,0},{5,1},{6,2},{7,3},{8,12},{9,13},{10,... | collective-permute-start | bytes 294920 | tf_op jit(solution)/shard_map/ppermute | solution.py:76
  4.8 13.2 %copy-start.1 = (f32[3,64,32,128]{3,2,1,0:T(8,128)S(1)}, f32[3,64,32,128]{3,2,1,0:T(8,128)}, u32[]{:S(2)}) copy-start(f32[3,64,32,128]{3,2,1,0:T(8,128)} %disp.9) | copy-start | bytes 9437188
  4.8 3.0 %collective-permute-start.1 = (f32[192,128]{1,0:T(8,128)S(1)}, f32[192,128]{1,0:T(8,128)S(1)}, u32[]{:S(2)}, u32[]{:S(2)}) collective-permute-start(f32[192,128]{1,0:T(8,128)S(1)} %get-tuple-element.27), channel_id=1, source_target_pairs={{0,1},{1,0},{2,3},{3,2},{4,8},{5,9},{6,10},{7,11},{8,4},{9,5},{10,... | collective-permute-start | bytes 294920 | tf_op jit(solution)/shard_map/ppermute | solution.py:76
  8.0 10.1 %collective-permute-start.2 = (f32[7,8,128]{2,1,0:T(8,128)S(1)}, f32[7,8,128]{2,1,0:T(8,128)S(1)}, u32[]{:S(2)}, u32[]{:S(2)}) collective-permute-start(f32[7,8,128]{2,1,0:T(8,128)S(1)} %get-tuple-element.28), channel_id=1, source_target_pairs={{0,1},{1,0},{2,3},{3,2},{4,5},{5,4},{6,7},{7,6},{8,9},{9,8},{10,11... | collective-permute-start | bytes 86024 | tf_op jit(solution)/shard_map/ppermute | solution.py:76
  10.9 7.2 %collective-permute-start.3 = (f32[7,8,128]{2,1,0:T(8,128)S(1)}, f32[7,8,128]{2,1,0:T(8,128)S(1)}, u32[]{:S(2)}, u32[]{:S(2)}) collective-permute-start(f32[7,8,128]{2,1,0:T(8,128)S(1)} %get-tuple-element.31), channel_id=1, source_target_pairs={{0,4},{1,2},{2,1},{3,7},{4,0},{5,6},{6,5},{7,3},{8,12},{9,10},{10,... | collective-permute-start | bytes 86024 | tf_op jit(solution)/shard_map/ppermute | solution.py:76
  18.2 16.6 %collective-permute-start.4 = (f32[872,128]{1,0:T(8,128)S(1)}, f32[872,128]{1,0:T(8,128)S(1)}, u32[]{:S(2)}, u32[]{:S(2)}) collective-permute-start(f32[872,128]{1,0:T(8,128)S(1)} %get-tuple-element.33), channel_id=1, source_target_pairs={{0,16},{1,17},{2,18},{3,19},{4,20},{5,21},{6,22},{7,23},{8,24},{9,... | collective-permute-start | bytes 1339400 | tf_op jit(solution)/shard_map/ppermute | solution.py:76
  19.1 15.7 %collective-permute-start.5 = (f32[872,128]{1,0:T(8,128)S(1)}, f32[872,128]{1,0:T(8,128)S(1)}, u32[]{:S(2)}, u32[]{:S(2)}) collective-permute-start(f32[872,128]{1,0:T(8,128)S(1)} %get-tuple-element.34), channel_id=1, source_target_pairs={{0,1},{1,0},{2,3},{3,2},{4,5},{5,4},{6,7},{7,6},{8,9},{9,8},{10,11... | collective-permute-start | bytes 1339400 | tf_op jit(solution)/shard_map/ppermute | solution.py:76
  38.5 32.1 %all-to-all-start = ((f32[256,1,128]{2,1,0:T(1,128)}), f32[256,1,128]{2,1,0:T(1,128)S(1)}, u32[]{:S(2)}, u32[]{:S(2)}) async-start(f32[256,1,128]{2,1,0:T(1,128)} %bitcast.1), calls=%async_computation | async-start | bytes 262144 | tf_op jit(solution)/shard_map/all_to_all | solution.py:778
  53.5 4.8 %collective-permute-start.6 = (f32[36,8,128]{2,1,0:T(8,128)S(1)}, f32[36,8,128]{2,1,0:T(8,128)S(1)}, u32[]{:S(2)}, u32[]{:S(2)}) collective-permute-start(f32[36,8,128]{2,1,0:T(8,128)S(1)} %get-tuple-element.39), channel_id=1, source_target_pairs={{0,4},{1,5},{2,6},{3,7},{4,0},{5,1},{6,2},{7,3},{8,12},{9,13},{10,... | collective-permute-start | bytes 442376 | tf_op jit(solution)/shard_map/ppermute | solution.py:76
  55.0 3.4 %collective-permute-start.7 = (f32[36,8,128]{2,1,0:T(8,128)S(1)}, f32[36,8,128]{2,1,0:T(8,128)S(1)}, u32[]{:S(2)}, u32[]{:S(2)}) collective-permute-start(f32[36,8,128]{2,1,0:T(8,128)S(1)} %get-tuple-element.40), channel_id=1, source_target_pairs={{0,1},{1,0},{2,3},{3,2},{4,8},{5,9},{6,10},{7,11},{8,4},{9,5},{10,... | collective-permute-start | bytes 442376 | tf_op jit(solution)/shard_map/ppermute | solution.py:76
  58.7 11.9 %collective-permute-start.8 = (f32[20,8,128]{2,1,0:T(8,128)S(1)}, f32[20,8,128]{2,1,0:T(8,128)S(1)}, u32[]{:S(2)}, u32[]{:S(2)}) collective-permute-start(f32[20,8,128]{2,1,0:T(8,128)S(1)} %get-tuple-element.43), channel_id=1, source_target_pairs={{0,1},{1,0},{2,3},{3,2},{4,5},{5,4},{6,7},{7,6},{8,9},{9,8},{10,11... | collective-permute-start | bytes 245768 | tf_op jit(solution)/shard_map/ppermute | solution.py:76
  62.0 8.6 %collective-permute-start.9 = (f32[20,8,128]{2,1,0:T(8,128)S(1)}, f32[20,8,128]{2,1,0:T(8,128)S(1)}, u32[]{:S(2)}, u32[]{:S(2)}) collective-permute-start(f32[20,8,128]{2,1,0:T(8,128)S(1)} %get-tuple-element.44), channel_id=1, source_target_pairs={{0,4},{1,2},{2,1},{3,7},{4,0},{5,6},{6,5},{7,3},{8,12},{9,10},{10,... | collective-permute-start | bytes 245768 | tf_op jit(solution)/shard_map/ppermute | solution.py:76

commit v5 on v4

--- a/solution.py
+++ b/solution.py
@@ -289,7 +289,7 @@
     return t % n, lax.rem(to_lane + 2 * LANES - spot - HALF * (t // n), LANES)
 
 
-def xy_pass(along, ring, slot, emit):
+def xy_pass(along, ring, slot, emit, keep=True):
     for t in range(along.shape[1] // 8 - 2):
         rows = slice(8 * t, 8 * t + 8)
         now = {}
@@ -304,7 +304,8 @@
         now[(3, "11")] = now[(2, "SD")] + now[(1, "DS")]
         fields = {}
         for f, name in enumerate(FIELDS):
-            if name in NO_VALUE or name in ALL_THREE:
+            steps = name in NO_VALUE or name in ALL_THREE
+            if steps and keep:
                 mid = ring[0, f, rows, :]
                 after = now[name] - mid
                 if emit is not None:
@@ -313,7 +314,10 @@
                 ring[1, f, rows, :] = after
                 continue
             if emit is not None:
-                fields[name] = ring[slot, f, rows, :], ring[1 - slot, f, rows, :], now[name]
+                old, mid = ring[slot, f, rows, :], ring[1 - slot, f, rows, :]
+                fields[name] = old, mid, now[name]
+                if steps:
+                    fields[name] = mid, mid - old, now[name] - mid
             ring[slot, f, rows, :] = now[name]
         if emit is not None:
             emit(t, energy_of(fields))
@@ -460,7 +464,7 @@
                     weight = weights[far("gx", bx - 1 if i == 2 else 0, bx), rows, :]
                     total[...] += jnp.where(own, weight * value, 0.0)
 
-            xy_pass(alongs[i % 2], ring, i % 2, emit if i >= 2 else None)
+            xy_pass(alongs[i % 2], ring, i % 2, emit if i >= 2 else None, keep=False)
         return carry
 
     lax.fori_loop(0, 2, one_side, 0)
@@ -732,12 +736,13 @@
     yr1, yr2 = swap(ys1, ys2, "gy")
     n = 3 * (by // 16)
     low, high = call(faces_kernel, [(n, 8, LANES)] * 2, cost=6_000_000)(displacement)
+    flags_here, low = lax.optimization_barrier((cell_flags, low))
+    coef = cell_coef(density, flags_here, trim_level)
+    coef, low = lax.optimization_barrier((coef, low))
     zs1, zs2, yr2 = call(ends_kernel, [(n + 1, 8, LANES)] * 2 + [(3 * bx, LANES)])(
         low, high, yr1, yr2
     )
     zr1, zr2 = swap(zs1, zs2, "gz")
-    flags_here, zs1 = lax.optimization_barrier((cell_flags, zs1))
-    coef = cell_coef(density, flags_here, trim_level)
     brick = (bx, by, LANES)
     rows = x_rows(by)[2]
     xs1, xs2, rims = call(

time: 74.2 us -> 73.8 us (level)
  no operation moved by 1% of the time
where the time goes in v5:
time: 73.8 us; the launch traced here: 73.6 us
  starting transfers between devices  37.6 us (51%)
  Pallas kernels  29 us (39%)
  waiting for transfers between devices  3.83 us (5%)
  local copies, waits for them, and re-layouts  1.9 us (3%)
  between operations  0.97 us (1%)
    pallas_call x1, Pallas kernels, body(): call(inner_kernel, [(bx - 2, by, LANES), (8, LANES), (REACH + 1, by, LANE...  15.5 us
    all_to_all x1, starting transfers between devices, body(): sums = lax.all_to_all(sums, AXES, split_axis=0, concat_axis=0, tiled=True)  15 us
    ppermute x5, starting transfers between devices, swap(): lax.ppermute(second, AXES, far_ones)  12.5 us
    ppermute x5, starting transfers between devices, swap(): lax.ppermute(first, AXES, near)  10.1 us
    pallas_call x1, Pallas kernels, body(): call(sweeps_kernel, [brick], [(cells, by + 24, LANES)] * 2, cost=20000000)  3.58 us
    pallas_call x1, Pallas kernels, body(): call(outer_kernel, [(cells, by, LANES), (cells // 2, 8, LANES), (cells //...  3.42 us
    pallas_call x1, Pallas kernels, body(): call(functools.partial(finish_kernel, float(bx * by * bz * devices)), [br...  3.27 us
    ppermute x5, waiting for transfers between devices, swap(): lax.ppermute(second, AXES, far_ones)  2.05 us
  transfers between devices with their start and end apart: 11, of which 2 were waited for; matrix products, arithmetic and copies ran while one was open for 1% of the time, Pallas kernels for 30%

profile of v5, /device:TPU:1, one launch (start us, length us, event | category | flops | bytes accessed | tf_op | source)
XLA Modules:
  0.0 73.6 jit_solution(14385393034864902658)
XLA Ops:
  0.6 0.0 copy-start
  0.6 1.9 %copy-done = f32[3,64,32,128]{3,2,1,0:T(8,128)S(1)} copy-done((f32[3,64,32,128]{3,2,1,0:T(8,128)S(1)}, f32[3,64,32,128]{3,2,1,0:T(8,128)}, u32[]{:S(2)}) %copy-start) | copy-done | bytes 3145752
  2.5 0.2 shard_map.60
  2.7 2.1 %collective-permute-start = (f32[192,128]{1,0:T(8,128)S(1)}, f32[192,128]{1,0:T(8,128)S(1)}, u32[]{:S(2)}, u32[]{:S(2)}) collective-permute-start(f32[192,128]{1,0:T(8,128)S(1)} %get-tuple-element.31), channel_id=1, source_target_pairs={{0,4},{1,5},{2,6},{3,7},{4,0},{5,1},{6,2},{7,3},{8,12},{9,13},{10,... | collective-permute-start | bytes 294920 | tf_op jit(solution)/shard_map/ppermute | solution.py:76
  4.8 1.3 %collective-permute-start.1 = (f32[192,128]{1,0:T(8,128)S(1)}, f32[192,128]{1,0:T(8,128)S(1)}, u32[]{:S(2)}, u32[]{:S(2)}) collective-permute-start(f32[192,128]{1,0:T(8,128)S(1)} %get-tuple-element.34), channel_id=1, source_target_pairs={{0,1},{1,0},{2,3},{3,2},{4,8},{5,9},{6,10},{7,11},{8,4},{9,5},{10,... | collective-permute-start | bytes 294920 | tf_op jit(solution)/shard_map/ppermute | solution.py:76
  6.2 1.7 %shard_map.59 = (f32[6,8,128]{2,1,0:T(8,128)S(1)}, f32[6,8,128]{2,1,0:T(8,128)S(1)}) custom-call(f32[3,64,32,128]{3,2,1,0:T(8,128)S(1)} %copy-done), custom_call_target="tpu_custom_call" | custom-call | flops 6000000 | bytes 6000000 | tf_op jit(solution)/shard_map/pallas_call | solution.py:738
  7.9 0.4 fusion.coef
  8.3 0.0 collective-permute-done.yr1
  8.3 0.0 collective-permute-done.1.yr2_raw
  8.3 0.1 shard_map.61
  8.4 2.4 %collective-permute-start.2 = (f32[7,8,128]{2,1,0:T(8,128)S(1)}, f32[7,8,128]{2,1,0:T(8,128)S(1)}, u32[]{:S(2)}, u32[]{:S(2)}) collective-permute-start(f32[7,8,128]{2,1,0:T(8,128)S(1)} %get-tuple-element.36), channel_id=1, source_target_pairs={{0,1},{1,0},{2,3},{3,2},{4,5},{5,4},{6,7},{7,6},{8,9},{9,8},{10,11... | collective-permute-start | bytes 86024 | tf_op jit(solution)/shard_map/ppermute | solution.py:76
  10.9 5.2 %collective-permute-start.3 = (f32[7,8,128]{2,1,0:T(8,128)S(1)}, f32[7,8,128]{2,1,0:T(8,128)S(1)}, u32[]{:S(2)}, u32[]{:S(2)}) collective-permute-start(f32[7,8,128]{2,1,0:T(8,128)S(1)} %get-tuple-element.37), channel_id=1, source_target_pairs={{0,4},{1,2},{2,1},{3,7},{4,0},{5,6},{6,5},{7,3},{8,12},{9,10},{10,... | collective-permute-start | bytes 86024 | tf_op jit(solution)/shard_map/ppermute | solution.py:76
  16.0 0.0 collective-permute-done.2.zr1
  16.0 2.0 %collective-permute-done.3.zr2 = f32[7,8,128]{2,1,0:T(8,128)S(1)} collective-permute-done((f32[7,8,128]{2,1,0:T(8,128)S(1)}, f32[7,8,128]{2,1,0:T(8,128)S(1)}, u32[]{:S(2)}, u32[]{:S(2)}) %collective-permute-start.3) | collective-permute-done | bytes 28704 | tf_op jit(solution)/shard_map/ppermute | solution.py:76
  18.1 0.1 shard_map.62
  18.2 0.9 %collective-permute-start.4 = (f32[872,128]{1,0:T(8,128)S(1)}, f32[872,128]{1,0:T(8,128)S(1)}, u32[]{:S(2)}, u32[]{:S(2)}) collective-permute-start(f32[872,128]{1,0:T(8,128)S(1)} %get-tuple-element.39), channel_id=1, source_target_pairs={{0,16},{1,17},{2,18},{3,19},{4,20},{5,21},{6,22},{7,23},{8,24},{9,... | collective-permute-start | bytes 1339400 | tf_op jit(solution)/shard_map/ppermute | solution.py:76
  19.1 0.0 collective-permute-start.5
  19.1 15.5 %shard_map.63 = (f32[62,32,128]{2,1,0:T(8,128)S(1)}, f32[8,128]{1,0:T(8,128)S(1)}, f32[5,32,128]{2,1,0:T(8,128)S(1)}) custom-call(f32[3,64,32,128]{3,2,1,0:T(8,128)S(1)} %copy-done.1, f32[64,32,128]{2,1,0:T(8,128)S(1)} %fusion.coef, f32[192,128]{1,0:T(8,128)S(1)} %collective-permute-done.yr1, f32[192,128]{1,0:T(8,128)S(1)} %get-tuple-element.35.yr2, ...), custom_call_target="tpu_custom_call" | custom-call | flops 60000000 | bytes 60000000 | tf_op jit(solution)/shard_map/pallas_call | solution.py:754
  34.6 0.0 collective-permute-done.4.xr1
  34.6 0.0 collective-permute-done.5.xr2
  34.6 3.4 %shard_map.64 = (f32[72,32,128]{2,1,0:T(8,128)S(1)}, f32[36,8,128]{2,1,0:T(8,128)S(1)}, f32[36,8,128]{2,1,0:T(8,128)S(1)}, f32[256,128]{1,0:T(8,128)}) custom-call(f32[3,64,32,128]{3,2,1,0:T(8,128)S(1)} %copy-done.1, f32[64,32,128]{2,1,0:T(8,128)S(1)} %fusion.coef, f32[192,128]{1,0:T(8,128)S(1)} %collective-permute-done.yr1, ...), custom_call_target="tpu_custom_call" | custom-call | tf_op jit(solution)/shard_map/pallas_call | solution.py:760
  38.1 15.0 %all-to-all-start = ((f32[256,1,128]{2,1,0:T(1,128)}), f32[256,1,128]{2,1,0:T(1,128)S(1)}, u32[]{:S(2)}, u32[]{:S(2)}) async-start(f32[256,1,128]{2,1,0:T(1,128)} %bitcast.1), calls=%async_computation | async-start | bytes 262144 | tf_op jit(solution)/shard_map/all_to_all | solution.py:783
  53.1 1.5 %collective-permute-start.6 = (f32[36,8,128]{2,1,0:T(8,128)S(1)}, f32[36,8,128]{2,1,0:T(8,128)S(1)}, u32[]{:S(2)}, u32[]{:S(2)}) collective-permute-start(f32[36,8,128]{2,1,0:T(8,128)S(1)} %get-tuple-element.45), channel_id=1, source_target_pairs={{0,4},{1,5},{2,6},{3,7},{4,0},{5,1},{6,2},{7,3},{8,12},{9,13},{10,... | collective-permute-start | bytes 442376 | tf_op jit(solution)/shard_map/ppermute | solution.py:76
  54.5 0.9 %collective-permute-start.7 = (f32[36,8,128]{2,1,0:T(8,128)S(1)}, f32[36,8,128]{2,1,0:T(8,128)S(1)}, u32[]{:S(2)}, u32[]{:S(2)}) collective-permute-start(f32[36,8,128]{2,1,0:T(8,128)S(1)} %get-tuple-element.46), channel_id=1, source_target_pairs={{0,1},{1,0},{2,3},{3,2},{4,8},{5,9},{6,10},{7,11},{8,4},{9,5},{10,... | collective-permute-start | bytes 442376 | tf_op jit(solution)/shard_map/ppermute | solution.py:76
  55.4 0.7 shard_map.65.both
  56.1 1.8 %collective-permute-done.6.yr1 = f32[36,8,128]{2,1,0:T(8,128)S(1)} collective-permute-done((f32[36,8,128]{2,1,0:T(8,128)S(1)}, f32[36,8,128]{2,1,0:T(8,128)S(1)}, u32[]{:S(2)}, u32[]{:S(2)}) %collective-permute-start.6) | collective-permute-done | bytes 147488 | tf_op jit(solution)/shard_map/ppermute | solution.py:76
  57.9 0.3 shard_map.66
  58.2 3.2 %collective-permute-start.8 = (f32[20,8,128]{2,1,0:T(8,128)S(1)}, f32[20,8,128]{2,1,0:T(8,128)S(1)}, u32[]{:S(2)}, u32[]{:S(2)}) collective-permute-start(f32[20,8,128]{2,1,0:T(8,128)S(1)} %get-tuple-element.49), channel_id=1, source_target_pairs={{0,1},{1,0},{2,3},{3,2},{4,5},{5,4},{6,7},{7,6},{8,9},{9,8},{10,11... | collective-permute-start | bytes 245768 | tf_op jit(solution)/shard_map/ppermute | solution.py:76
  61.4 5.2 %collective-permute-start.9 = (f32[20,8,128]{2,1,0:T(8,128)S(1)}, f32[20,8,128]{2,1,0:T(8,128)S(1)}, u32[]{:S(2)}, u32[]{:S(2)}) collective-permute-start(f32[20,8,128]{2,1,0:T(8,128)S(1)} %get-tuple-element.50), channel_id=1, source_target_pairs={{0,4},{1,2},{2,1},{3,7},{4,0},{5,6},{6,5},{7,3},{8,12},{9,10},{10,... | collective-permute-start | bytes 245768 | tf_op jit(solution)/shard_map/ppermute | solution.py:76
  66.5 3.6 %shard_map.67.inner = f32[64,32,128]{2,1,0:T(8,128)S(1)} custom-call(f32[72,32,128]{2,1,0:T(8,128)S(1)} %get-tuple-element.44.source, f32[72,8,128]{2,1,0:T(8,128)S(1)} %get-tuple-element.47.rim), custom_call_target="tpu_custom_call" | custom-call | flops 20000000 | bytes 20000000 | tf_op jit(solution)/shard_map/pallas_call | solution.py:794
  70.2 0.0 all-to-all-done
  70.2 3.3 %shard_map.69 = (f32[64,32,128]{2,1,0:T(8,128)}, f32[64,32,128]{2,1,0:T(8,128)}) custom-call(f32[64,32,128]{2,1,0:T(8,128)S(1)} %shard_map.67.inner, f32[40,3,8,128]{3,2,1,0:T(8,128)S(1)} %shard_map.68.strip, f32[64,32,128]{2,1,0:T(8,128)S(1)} %copy-done.2, f32[256,128]{1,0:T(8,128)S(1)} %bitcast.4), custom_call_target="tpu_custom_call" | custom-call | tf_op jit(solution)/shard_map/pallas_call | solution.py:799
  (12 shorter events, 0.1 us)
Async XLA Ops:
  0.6 1.9 %copy-start = (f32[3,64,32,128]{3,2,1,0:T(8,128)S(1)}, f32[3,64,32,128]{3,2,1,0:T(8,128)}, u32[]{:S(2)}) copy-start(f32[3,64,32,128]{3,2,1,0:T(8,128)} %disp.9) | copy-start | bytes 9437188
  2.5 5.3 %copy-start.2 = (f32[64,32,128]{2,1,0:T(8,128)S(1)}, f32[64,32,128]{2,1,0:T(8,128)}, u32[]{:S(2)}) copy-start(f32[64,32,128]{2,1,0:T(8,128)} %density.1) | copy-start | bytes 3145732
  2.5 5.4 %copy-start.3 = (s32[64,32,128]{2,1,0:T(8,128)S(1)}, s32[64,32,128]{2,1,0:T(8,128)}, u32[]{:S(2)}) copy-start(s32[64,32,128]{2,1,0:T(8,128)} %param.7) | copy-start | bytes 3145732
  2.5 5.4 %copy-start.4 = (s32[64,32,128]{2,1,0:T(8,128)S(1)}, s32[64,32,128]{2,1,0:T(8,128)}, u32[]{:S(2)}) copy-start(s32[64,32,128]{2,1,0:T(8,128)} %param.6) | copy-start | bytes 3145732
  2.7 5.6 %collective-permute-start = (f32[192,128]{1,0:T(8,128)S(1)}, f32[192,128]{1,0:T(8,128)S(1)}, u32[]{:S(2)}, u32[]{:S(2)}) collective-permute-start(f32[192,128]{1,0:T(8,128)S(1)} %get-tuple-element.31), channel_id=1, source_target_pairs={{0,4},{1,5},{2,6},{3,7},{4,0},{5,1},{6,2},{7,3},{8,12},{9,13},{10,... | collective-permute-start | bytes 294920 | tf_op jit(solution)/shard_map/ppermute | solution.py:76
  4.8 13.2 %copy-start.1 = (f32[3,64,32,128]{3,2,1,0:T(8,128)S(1)}, f32[3,64,32,128]{3,2,1,0:T(8,128)}, u32[]{:S(2)}) copy-start(f32[3,64,32,128]{3,2,1,0:T(8,128)} %disp.9) | copy-start | bytes 9437188
  4.8 3.5 %collective-permute-start.1 = (f32[192,128]{1,0:T(8,128)S(1)}, f32[192,128]{1,0:T(8,128)S(1)}, u32[]{:S(2)}, u32[]{:S(2)}) collective-permute-start(f32[192,128]{1,0:T(8,128)S(1)} %get-tuple-element.34), channel_id=1, source_target_pairs={{0,1},{1,0},{2,3},{3,2},{4,8},{5,9},{6,10},{7,11},{8,4},{9,5},{10,... | collective-permute-start | bytes 294920 | tf_op jit(solution)/shard_map/ppermute | solution.py:76
  8.4 7.6 %collective-permute-start.2 = (f32[7,8,128]{2,1,0:T(8,128)S(1)}, f32[7,8,128]{2,1,0:T(8,128)S(1)}, u32[]{:S(2)}, u32[]{:S(2)}) collective-permute-start(f32[7,8,128]{2,1,0:T(8,128)S(1)} %get-tuple-element.36), channel_id=1, source_target_pairs={{0,1},{1,0},{2,3},{3,2},{4,5},{5,4},{6,7},{7,6},{8,9},{9,8},{10,11... | collective-permute-start | bytes 86024 | tf_op jit(solution)/shard_map/ppermute | solution.py:76
  10.9 7.2 %collective-permute-start.3 = (f32[7,8,128]{2,1,0:T(8,128)S(1)}, f32[7,8,128]{2,1,0:T(8,128)S(1)}, u32[]{:S(2)}, u32[]{:S(2)}) collective-permute-start(f32[7,8,128]{2,1,0:T(8,128)S(1)} %get-tuple-element.37), channel_id=1, source_target_pairs={{0,4},{1,2},{2,1},{3,7},{4,0},{5,6},{6,5},{7,3},{8,12},{9,10},{10,... | collective-permute-start | bytes 86024 | tf_op jit(solution)/shard_map/ppermute | solution.py:76
  18.2 16.5 %collective-permute-start.4 = (f32[872,128]{1,0:T(8,128)S(1)}, f32[872,128]{1,0:T(8,128)S(1)}, u32[]{:S(2)}, u32[]{:S(2)}) collective-permute-start(f32[872,128]{1,0:T(8,128)S(1)} %get-tuple-element.39), channel_id=1, source_target_pairs={{0,16},{1,17},{2,18},{3,19},{4,20},{5,21},{6,22},{7,23},{8,24},{9,... | collective-permute-start | bytes 1339400 | tf_op jit(solution)/shard_map/ppermute | solution.py:76
  19.1 15.6 %collective-permute-start.5 = (f32[872,128]{1,0:T(8,128)S(1)}, f32[872,128]{1,0:T(8,128)S(1)}, u32[]{:S(2)}, u32[]{:S(2)}) collective-permute-start(f32[872,128]{1,0:T(8,128)S(1)} %get-tuple-element.40), channel_id=1, source_target_pairs={{0,1},{1,0},{2,3},{3,2},{4,5},{5,4},{6,7},{7,6},{8,9},{9,8},{10,11... | collective-permute-start | bytes 1339400 | tf_op jit(solution)/shard_map/ppermute | solution.py:76
  38.1 32.1 %all-to-all-start = ((f32[256,1,128]{2,1,0:T(1,128)}), f32[256,1,128]{2,1,0:T(1,128)S(1)}, u32[]{:S(2)}, u32[]{:S(2)}) async-start(f32[256,1,128]{2,1,0:T(1,128)} %bitcast.1), calls=%async_computation | async-start | bytes 262144 | tf_op jit(solution)/shard_map/all_to_all | solution.py:783
  53.1 4.8 %collective-permute-start.6 = (f32[36,8,128]{2,1,0:T(8,128)S(1)}, f32[36,8,128]{2,1,0:T(8,128)S(1)}, u32[]{:S(2)}, u32[]{:S(2)}) collective-permute-start(f32[36,8,128]{2,1,0:T(8,128)S(1)} %get-tuple-element.45), channel_id=1, source_target_pairs={{0,4},{1,5},{2,6},{3,7},{4,0},{5,1},{6,2},{7,3},{8,12},{9,13},{10,... | collective-permute-start | bytes 442376 | tf_op jit(solution)/shard_map/ppermute | solution.py:76
  54.5 3.4 %collective-permute-start.7 = (f32[36,8,128]{2,1,0:T(8,128)S(1)}, f32[36,8,128]{2,1,0:T(8,128)S(1)}, u32[]{:S(2)}, u32[]{:S(2)}) collective-permute-start(f32[36,8,128]{2,1,0:T(8,128)S(1)} %get-tuple-element.46), channel_id=1, source_target_pairs={{0,1},{1,0},{2,3},{3,2},{4,8},{5,9},{6,10},{7,11},{8,4},{9,5},{10,... | collective-permute-start | bytes 442376 | tf_op jit(solution)/shard_map/ppermute | solution.py:76
  58.2 11.9 %collective-permute-start.8 = (f32[20,8,128]{2,1,0:T(8,128)S(1)}, f32[20,8,128]{2,1,0:T(8,128)S(1)}, u32[]{:S(2)}, u32[]{:S(2)}) collective-permute-start(f32[20,8,128]{2,1,0:T(8,128)S(1)} %get-tuple-element.49), channel_id=1, source_target_pairs={{0,1},{1,0},{2,3},{3,2},{4,5},{5,4},{6,7},{7,6},{8,9},{9,8},{10,11... | collective-permute-start | bytes 245768 | tf_op jit(solution)/shard_map/ppermute | solution.py:76
  61.4 8.8 %collective-permute-start.9 = (f32[20,8,128]{2,1,0:T(8,128)S(1)}, f32[20,8,128]{2,1,0:T(8,128)S(1)}, u32[]{:S(2)}, u32[]{:S(2)}) collective-permute-start(f32[20,8,128]{2,1,0:T(8,128)S(1)} %get-tuple-element.50), channel_id=1, source_target_pairs={{0,4},{1,2},{2,1},{3,7},{4,0},{5,6},{6,5},{7,3},{8,12},{9,10},{10,... | collective-permute-start | bytes 245768 | tf_op jit(solution)/shard_map/ppermute | solution.py:76

commit v6 on v5

--- a/solution.py
+++ b/solution.py
@@ -504,8 +504,14 @@
         inside[y] = half_turn(jnp.where(top, last, first))
 
 
-def pack_kernel(source, both):
+def pack_kernel(source, both, filtered, *works):
     pack_columns(source, both.at[0], both.at[1], source.shape[1])
+    run_sweeps(source, None, filtered, works)
+
+
+def late_kernel(source, rim, filtered_in, w0, w1, w2, w3, filtered, *works):
+    del filtered_in, w0, w1, w2, w3
+    run_sweeps(source, rim, filtered, works)
 
 
 def corner_kernel(yr1, yr2, both, rim, rim_both, zs1, zs2):
@@ -537,13 +543,14 @@
         send(by // 2 + m, rim_packed[2 * m], rim_packed[2 * m + 1])
 
 
-def sweeps_kernel(source, rim, filtered, work0, work1):
+def run_sweeps(source, rim, filtered, works):
     cells, by, _ = source.shape
     bx = cells - 2 * REACH
     tiles = by // 8
     top = row_ids() < 4
     first_x, last_x = lax.axis_index("gx") == 0, lax.axis_index("gx") == lax.axis_size("gx") - 1
     first_y, last_y = lax.axis_index("gy") == 0, lax.axis_index("gy") == lax.axis_size("gy") - 1
+    late = rim is not None
 
     def put(ref, x, t, value):
         ref[x, 8 * t + 8 : 8 * t + 16, :] = value
@@ -553,9 +560,11 @@
             ref[x, by + 16 : by + 24, :] = value
 
     def begin(x, carry):
-        for t in range(tiles):
-            put(work0, x, t, POLY[4] * source[x, 8 * t : 8 * t + 8, :])
-        put(work0, x, tiles, POLY[4] * rim[x])
+        if late:
+            put(works[0], x, tiles, POLY[4] * rim[x])
+        else:
+            for t in range(tiles):
+                put(works[0], x, t, POLY[4] * source[x, 8 * t : 8 * t + 8, :])
         return carry
 
     lax.fori_loop(0, cells, begin, 0, unroll=8)
@@ -564,11 +573,16 @@
             jnp.logical_and(last_y, top), jnp.logical_and(first_y, jnp.logical_not(top))
         )
     )
+    edge = [0, tiles - 1]
     for k in range(4):
-        now, later = (work0, work1)[k % 2], (work0, work1)[(k + 1) % 2]
-
-        def sweep(x, k=k, now=now, later=later):
-            for t in range(tiles + (k < 3)):
+        now = works[k]
+        if late:
+            here = edge + ([tiles] if k < 3 else [])
+        else:
+            here = list(range(tiles)) if k < 3 else list(range(1, tiles - 1))
+
+        def sweep(x, k=k, now=now, here=here):
+            for t in here:
                 at = 8 * t + 8
                 mid = now[x, at : at + 8, :]
                 value = now[x - 1, at : at + 8, :] + now[x + 1, at : at + 8, :]
@@ -581,7 +595,7 @@
                 else:
                     if t == tiles:
                         value = jnp.where(rim_keep, value, 0.0)
-                    put(later, x, t, value)
+                    put(works[k + 1], x, t, value)
 
         first, left = (1, cells - 2) if k < 3 else (REACH, bx)
         group = max(g for g in range(2, 36) if left % g == 0)
@@ -593,6 +607,7 @@
 
         lax.fori_loop(0, left // group, sweeps, 0)
         if k < 3:
+            later = works[k + 1]
 
             @pl.when(first_x)
             def _(later=later):
@@ -716,11 +731,12 @@
             copy.wait()
 
 
-def call(kernel, outs, scratch=(), cost=0, placed=None):
+def call(kernel, outs, scratch=(), cost=0, placed=None, aliases=None):
     return pl.pallas_call(
         kernel,
         out_shape=[jax.ShapeDtypeStruct(s, F32) for s in outs],
         out_specs=placed or [VMEM] * len(outs),
+        input_output_aliases=aliases or {},
         scratch_shapes=[pltpu.VMEM(s, F32) if isinstance(s, tuple) else s for s in scratch],
         compiler_params=pltpu.CompilerParams(**PARAMS),
         cost_estimate=pl.CostEstimate(flops=cost, bytes_accessed=cost, transcendentals=0),
@@ -779,7 +795,8 @@
         placed=[VMEM] * 3 + [ANYWHERE],
     )(displacement, coef, yr1, yr2, rims, xr1, xr2, inner, partial, weights)
     yr1, yr2 = swap(ys1, ys2, "gy")
-    (both,) = call(pack_kernel, [(2, by, 8, LANES)], cost=6_000_000)(source)
+    work = [(cells, by + 24, LANES)] * 4
+    both, *early = call(pack_kernel, [(2, by, 8, LANES), brick] + work, cost=20_000_000)(source)
     sums = lax.all_to_all(sums, AXES, split_axis=0, concat_axis=0, tiled=True)
     rim, rim_both, zs1, zs2 = call(
         corner_kernel,
@@ -791,9 +808,12 @@
         ],
     )(yr1, yr2, both)
     zr1, zr2 = swap(zs1, zs2, "gz")
-    (middle,) = call(
-        sweeps_kernel, [brick], [(cells, by + 24, LANES)] * 2, cost=20_000_000
-    )(source, rim)
+    middle = call(
+        late_kernel,
+        [brick] + work,
+        cost=20_000_000,
+        aliases={i + 2: i for i in range(5)},
+    )(source, rim, *early)[0]
     strip_shape = (tall, 3, 8, LANES)
     (strip,) = call(strip_kernel, [strip_shape])(both, rim_both, zr1, zr2)
     return call(

time: 73.8 us -> 73.8 us (level)
  Pallas kernels: 29 us -> 31.3 us
  starting transfers between devices: 37.6 us -> 36.2 us
  waiting for transfers between devices: 3.83 us -> 2.75 us
    ppermute x5, waiting for transfers between devices: 1.78 us -> 0.01 us  [swap(): lax.ppermute(first, AXES, near)]
    pallas_call x2, Pallas kernels: 4.29 us -> 6 us  [the longest x1 3.72 us: body(): call(pack_kernel, [(2, by, 8, LANES), brick] + work, cost=20000000)(source)]
    ppermute x5, starting transfers between devices: 10.1 us -> 9.01 us  [swap(): lax.ppermute(first, AXES, near)]
  transfers between devices with their start and end apart: 11 -> 11, of which waited for: 2 -> 2; matrix products, arithmetic and copies ran while one was open for 1% -> 1% of each run, Pallas kernels for 30% -> 32%
where the time goes in v6:
time: 73.8 us; the launch traced here: 73.6 us
  starting transfers between devices  36.2 us (49%)
  Pallas kernels  31.3 us (42%)
  waiting for transfers between devices  2.75 us (4%)
  local copies, waits for them, and re-layouts  1.91 us (3%)
  between operations  1 us (1%)
    pallas_call x1, Pallas kernels, body(): call(inner_kernel, [(bx - 2, by, LANES), (8, LANES), (REACH + 1, by, LANE...  15.5 us
    all_to_all x1, starting transfers between devices, body(): sums = lax.all_to_all(sums, AXES, split_axis=0, concat_axis=0, tiled=True)  15 us
    ppermute x5, starting transfers between devices, swap(): lax.ppermute(second, AXES, far_ones)  12.2 us
    ppermute x5, starting transfers between devices, swap(): lax.ppermute(first, AXES, near)  9.01 us
    pallas_call x1, Pallas kernels, body(): call(outer_kernel, [(cells, by, LANES), (cells // 2, 8, LANES), (cells //...  4.08 us
    pallas_call x1, Pallas kernels, body(): call(pack_kernel, [(2, by, 8, LANES), brick] + work, cost=20000000)(source)  3.72 us
    pallas_call x1, Pallas kernels, body(): call(functools.partial(finish_kernel, float(bx * by * bz * devices)), [br...  3.27 us
    ppermute x5, waiting for transfers between devices, swap(): lax.ppermute(second, AXES, far_ones)  2.74 us
  transfers between devices with their start and end apart: 11, of which 2 were waited for; matrix products, arithmetic and copies ran while one was open for 1% of the time, Pallas kernels for 32%

profile of v6, /device:TPU:1, one launch (start us, length us, event | category | flops | bytes accessed | tf_op | source)
XLA Modules:
  0.0 73.6 jit_solution(17446172338734666083)
XLA Ops:
  0.6 0.0 copy-start
  0.6 1.9 %copy-done = f32[3,64,32,128]{3,2,1,0:T(8,128)S(1)} copy-done((f32[3,64,32,128]{3,2,1,0:T(8,128)S(1)}, f32[3,64,32,128]{3,2,1,0:T(8,128)}, u32[]{:S(2)}) %copy-start) | copy-done | bytes 3145752
  2.5 0.2 shard_map.60
  2.7 0.0 copy-start.2
  2.7 0.0 copy-start.3
  2.7 0.0 copy-start.4
  2.7 2.1 %collective-permute-start = (f32[192,128]{1,0:T(8,128)S(1)}, f32[192,128]{1,0:T(8,128)S(1)}, u32[]{:S(2)}, u32[]{:S(2)}) collective-permute-start(f32[192,128]{1,0:T(8,128)S(1)} %get-tuple-element.38), channel_id=1, source_target_pairs={{0,4},{1,5},{2,6},{3,7},{4,0},{5,1},{6,2},{7,3},{8,12},{9,13},{10,... | collective-permute-start | bytes 294920 | tf_op jit(solution)/shard_map/ppermute | solution.py:76
  4.9 1.3 %collective-permute-start.1 = (f32[192,128]{1,0:T(8,128)S(1)}, f32[192,128]{1,0:T(8,128)S(1)}, u32[]{:S(2)}, u32[]{:S(2)}) collective-permute-start(f32[192,128]{1,0:T(8,128)S(1)} %get-tuple-element.41), channel_id=1, source_target_pairs={{0,1},{1,0},{2,3},{3,2},{4,8},{5,9},{6,10},{7,11},{8,4},{9,5},{10,... | collective-permute-start | bytes 294920 | tf_op jit(solution)/shard_map/ppermute | solution.py:76
  6.2 1.7 %shard_map.59 = (f32[6,8,128]{2,1,0:T(8,128)S(1)}, f32[6,8,128]{2,1,0:T(8,128)S(1)}) custom-call(f32[3,64,32,128]{3,2,1,0:T(8,128)S(1)} %copy-done), custom_call_target="tpu_custom_call" | custom-call | flops 6000000 | bytes 6000000 | tf_op jit(solution)/shard_map/pallas_call | solution.py:754
  7.9 0.0 copy-start.1
  7.9 0.4 fusion.coef
  8.3 0.0 collective-permute-done.yr1
  8.4 0.1 shard_map.61
  8.5 2.4 %collective-permute-start.2 = (f32[7,8,128]{2,1,0:T(8,128)S(1)}, f32[7,8,128]{2,1,0:T(8,128)S(1)}, u32[]{:S(2)}, u32[]{:S(2)}) collective-permute-start(f32[7,8,128]{2,1,0:T(8,128)S(1)} %get-tuple-element.43), channel_id=1, source_target_pairs={{0,1},{1,0},{2,3},{3,2},{4,5},{5,4},{6,7},{7,6},{8,9},{9,8},{10,11... | collective-permute-start | bytes 86024 | tf_op jit(solution)/shard_map/ppermute | solution.py:76
  10.9 5.2 %collective-permute-start.3 = (f32[7,8,128]{2,1,0:T(8,128)S(1)}, f32[7,8,128]{2,1,0:T(8,128)S(1)}, u32[]{:S(2)}, u32[]{:S(2)}) collective-permute-start(f32[7,8,128]{2,1,0:T(8,128)S(1)} %get-tuple-element.44), channel_id=1, source_target_pairs={{0,4},{1,2},{2,1},{3,7},{4,0},{5,6},{6,5},{7,3},{8,12},{9,10},{10,... | collective-permute-start | bytes 86024 | tf_op jit(solution)/shard_map/ppermute | solution.py:76
  16.1 0.0 collective-permute-done.2.zr1
  16.1 2.0 %collective-permute-done.3.zr2 = f32[7,8,128]{2,1,0:T(8,128)S(1)} collective-permute-done((f32[7,8,128]{2,1,0:T(8,128)S(1)}, f32[7,8,128]{2,1,0:T(8,128)S(1)}, u32[]{:S(2)}, u32[]{:S(2)}) %collective-permute-start.3) | collective-permute-done | bytes 28704 | tf_op jit(solution)/shard_map/ppermute | solution.py:76
  18.1 0.1 shard_map.62
  18.2 0.9 %collective-permute-start.4 = (f32[872,128]{1,0:T(8,128)S(1)}, f32[872,128]{1,0:T(8,128)S(1)}, u32[]{:S(2)}, u32[]{:S(2)}) collective-permute-start(f32[872,128]{1,0:T(8,128)S(1)} %get-tuple-element.46), channel_id=1, source_target_pairs={{0,16},{1,17},{2,18},{3,19},{4,20},{5,21},{6,22},{7,23},{8,24},{9,... | collective-permute-start | bytes 1339400 | tf_op jit(solution)/shard_map/ppermute | solution.py:76
  19.1 0.0 collective-permute-start.5
  19.1 15.5 %shard_map.63 = (f32[62,32,128]{2,1,0:T(8,128)S(1)}, f32[8,128]{1,0:T(8,128)S(1)}, f32[5,32,128]{2,1,0:T(8,128)S(1)}) custom-call(f32[3,64,32,128]{3,2,1,0:T(8,128)S(1)} %copy-done.1, f32[64,32,128]{2,1,0:T(8,128)S(1)} %fusion.coef, f32[192,128]{1,0:T(8,128)S(1)} %collective-permute-done.yr1, f32[192,128]{1,0:T(8,128)S(1)} %get-tuple-element.42.yr2, ...), custom_call_target="tpu_custom_call" | custom-call | flops 60000000 | bytes 60000000 | tf_op jit(solution)/shard_map/pallas_call | solution.py:770
  34.7 4.1 %shard_map.64 = (f32[72,32,128]{2,1,0:T(8,128)S(1)}, f32[36,8,128]{2,1,0:T(8,128)}, f32[36,8,128]{2,1,0:T(8,128)S(1)}, f32[256,128]{1,0:T(8,128)}) custom-call(f32[3,64,32,128]{3,2,1,0:T(8,128)S(1)} %copy-done.1, f32[64,32,128]{2,1,0:T(8,128)S(1)} %fusion.coef, f32[192,128]{1,0:T(8,128)S(1)} %collective-permute-done.yr1, ...), custom_call_target="tpu_custom_call" | custom-call | tf_op jit(solution)/shard_map/pallas_call | solution.py:776
  38.8 15.0 %all-to-all-start = ((f32[256,1,128]{2,1,0:T(1,128)}), f32[256,1,128]{2,1,0:T(1,128)S(1)}, u32[]{:S(2)}, u32[]{:S(2)}) async-start(f32[256,1,128]{2,1,0:T(1,128)} %bitcast.1), calls=%async_computation | async-start | bytes 262144 | tf_op jit(solution)/shard_map/all_to_all | solution.py:800
  53.8 1.5 %collective-permute-start.6 = (f32[36,8,128]{2,1,0:T(8,128)}, f32[36,8,128]{2,1,0:T(8,128)S(1)}, u32[]{:S(2)}, u32[]{:S(2)}) collective-permute-start(f32[36,8,128]{2,1,0:T(8,128)} %get-tuple-element.52), channel_id=1, source_target_pairs={{0,4},{1,5},{2,6},{3,7},{4,0},{5,1},{6,2},{7,3},{8,12},{9,13},{10,... | collective-permute-start | bytes 442376 | tf_op jit(solution)/shard_map/ppermute | solution.py:76
  55.2 0.9 %collective-permute-start.7 = (f32[36,8,128]{2,1,0:T(8,128)S(1)}, f32[36,8,128]{2,1,0:T(8,128)S(1)}, u32[]{:S(2)}, u32[]{:S(2)}) collective-permute-start(f32[36,8,128]{2,1,0:T(8,128)S(1)} %get-tuple-element.53), channel_id=1, source_target_pairs={{0,1},{1,0},{2,3},{3,2},{4,8},{5,9},{6,10},{7,11},{8,4},{9,5},{10,... | collective-permute-start | bytes 442376 | tf_op jit(solution)/shard_map/ppermute | solution.py:76
  56.1 3.7 %shard_map.65 = (f32[2,32,8,128]{3,2,1,0:T(8,128)S(1)}, f32[64,32,128]{2,1,0:T(8,128)S(1)}, f32[72,56,128]{2,1,0:T(8,128)S(1)}, f32[72,56,128]{2,1,0:T(8,128)S(1...) custom-call(f32[72,32,128]{2,1,0:T(8,128)S(1)} %get-tuple-element.51.source), custom_call_target="tpu_custom_call" | custom-call | flops 20000000 | bytes 20000000 | tf_op jit(solution)/shard_map/pallas_call | solution.py:799
  59.8 0.3 shard_map.66
  60.2 2.1 %collective-permute-start.8 = (f32[20,8,128]{2,1,0:T(8,128)S(1)}, f32[20,8,128]{2,1,0:T(8,128)S(1)}, u32[]{:S(2)}, u32[]{:S(2)}) collective-permute-start(f32[20,8,128]{2,1,0:T(8,128)S(1)} %get-tuple-element.63), channel_id=1, source_target_pairs={{0,1},{1,0},{2,3},{3,2},{4,5},{5,4},{6,7},{7,6},{8,9},{9,8},{10,11... | collective-permute-start | bytes 245768 | tf_op jit(solution)/shard_map/ppermute | solution.py:76
  62.3 4.9 %collective-permute-start.9 = (f32[20,8,128]{2,1,0:T(8,128)S(1)}, f32[20,8,128]{2,1,0:T(8,128)S(1)}, u32[]{:S(2)}, u32[]{:S(2)}) collective-permute-start(f32[20,8,128]{2,1,0:T(8,128)S(1)} %get-tuple-element.64), channel_id=1, source_target_pairs={{0,4},{1,2},{2,1},{3,7},{4,0},{5,6},{6,5},{7,3},{8,12},{9,10},{10,... | collective-permute-start | bytes 245768 | tf_op jit(solution)/shard_map/ppermute | solution.py:76
  67.1 2.3 %shard_map.67 = (f32[64,32,128]{2,1,0:T(8,128)S(1)}, f32[72,56,128]{2,1,0:T(8,128)S(1)}, f32[72,56,128]{2,1,0:T(8,128)S(1)}, f32[72,56,128]{2,1,0:T(8,128)S(1)}, f32[72,56,128]{2,1,0:T(8,128)S(1)}) custom-call(f32[72,32,128]{2,1,0:T(8,128)S(1)} %get-tuple-element.51.source, ...), custom_call_target="tpu_custom_call", output_to_operand_aliasing={{0}: (2, {}), {1}: (3, {}), {2}: (4, {}), {3}: (5, {}), {4}... | custom-call | flops 20000000 | bytes 20000000 | tf_op jit(solution)/shard_map/pallas_call | solution.py:811
  69.4 0.7 collective-permute-done.9.zr2
  70.2 3.3 %shard_map.69 = (f32[64,32,128]{2,1,0:T(8,128)}, f32[64,32,128]{2,1,0:T(8,128)}) custom-call(f32[64,32,128]{2,1,0:T(8,128)S(1)} %get-tuple-element.61.inner, f32[40,3,8,128]{3,2,1,0:T(8,128)S(1)} %shard_map.68.strip, f32[64,32,128]{2,1,0:T(8,128)S(1)} %copy-done.2, f32[256,128]{1,0:T(8,128)S(1)} %bitcast.4), custom_call_target="tpu_custom_call" | custom-call | tf_op jit(solution)/shard_map/pallas_call | solution.py:819
  (12 shorter events, 0.1 us)
Async XLA Ops:
  0.6 1.9 %copy-start = (f32[3,64,32,128]{3,2,1,0:T(8,128)S(1)}, f32[3,64,32,128]{3,2,1,0:T(8,128)}, u32[]{:S(2)}) copy-start(f32[3,64,32,128]{3,2,1,0:T(8,128)} %disp.9) | copy-start | bytes 9437188
  2.7 5.2 %copy-start.2 = (f32[64,32,128]{2,1,0:T(8,128)S(1)}, f32[64,32,128]{2,1,0:T(8,128)}, u32[]{:S(2)}) copy-start(f32[64,32,128]{2,1,0:T(8,128)} %density.1) | copy-start | bytes 3145732
  2.7 5.2 %copy-start.3 = (s32[64,32,128]{2,1,0:T(8,128)S(1)}, s32[64,32,128]{2,1,0:T(8,128)}, u32[]{:S(2)}) copy-start(s32[64,32,128]{2,1,0:T(8,128)} %param.7) | copy-start | bytes 3145732
  2.7 5.2 %copy-start.4 = (s32[64,32,128]{2,1,0:T(8,128)S(1)}, s32[64,32,128]{2,1,0:T(8,128)}, u32[]{:S(2)}) copy-start(s32[64,32,128]{2,1,0:T(8,128)} %param.6) | copy-start | bytes 3145732
  2.7 5.6 %collective-permute-start = (f32[192,128]{1,0:T(8,128)S(1)}, f32[192,128]{1,0:T(8,128)S(1)}, u32[]{:S(2)}, u32[]{:S(2)}) collective-permute-start(f32[192,128]{1,0:T(8,128)S(1)} %get-tuple-element.38), channel_id=1, source_target_pairs={{0,4},{1,5},{2,6},{3,7},{4,0},{5,1},{6,2},{7,3},{8,12},{9,13},{10,... | collective-permute-start | bytes 294920 | tf_op jit(solution)/shard_map/ppermute | solution.py:76
  4.9 3.5 %collective-permute-start.1 = (f32[192,128]{1,0:T(8,128)S(1)}, f32[192,128]{1,0:T(8,128)S(1)}, u32[]{:S(2)}, u32[]{:S(2)}) collective-permute-start(f32[192,128]{1,0:T(8,128)S(1)} %get-tuple-element.41), channel_id=1, source_target_pairs={{0,1},{1,0},{2,3},{3,2},{4,8},{5,9},{6,10},{7,11},{8,4},{9,5},{10,... | collective-permute-start | bytes 294920 | tf_op jit(solution)/shard_map/ppermute | solution.py:76
  7.9 10.2 %copy-start.1 = (f32[3,64,32,128]{3,2,1,0:T(8,128)S(1)}, f32[3,64,32,128]{3,2,1,0:T(8,128)}, u32[]{:S(2)}) copy-start(f32[3,64,32,128]{3,2,1,0:T(8,128)} %disp.9) | copy-start | bytes 9437188
  8.5 7.6 %collective-permute-start.2 = (f32[7,8,128]{2,1,0:T(8,128)S(1)}, f32[7,8,128]{2,1,0:T(8,128)S(1)}, u32[]{:S(2)}, u32[]{:S(2)}) collective-permute-start(f32[7,8,128]{2,1,0:T(8,128)S(1)} %get-tuple-element.43), channel_id=1, source_target_pairs={{0,1},{1,0},{2,3},{3,2},{4,5},{5,4},{6,7},{7,6},{8,9},{9,8},{10,11... | collective-permute-start | bytes 86024 | tf_op jit(solution)/shard_map/ppermute | solution.py:76
  10.9 7.2 %collective-permute-start.3 = (f32[7,8,128]{2,1,0:T(8,128)S(1)}, f32[7,8,128]{2,1,0:T(8,128)S(1)}, u32[]{:S(2)}, u32[]{:S(2)}) collective-permute-start(f32[7,8,128]{2,1,0:T(8,128)S(1)} %get-tuple-element.44), channel_id=1, source_target_pairs={{0,4},{1,2},{2,1},{3,7},{4,0},{5,6},{6,5},{7,3},{8,12},{9,10},{10,... | collective-permute-start | bytes 86024 | tf_op jit(solution)/shard_map/ppermute | solution.py:76
  18.2 16.5 %collective-permute-start.4 = (f32[872,128]{1,0:T(8,128)S(1)}, f32[872,128]{1,0:T(8,128)S(1)}, u32[]{:S(2)}, u32[]{:S(2)}) collective-permute-start(f32[872,128]{1,0:T(8,128)S(1)} %get-tuple-element.46), channel_id=1, source_target_pairs={{0,16},{1,17},{2,18},{3,19},{4,20},{5,21},{6,22},{7,23},{8,24},{9,... | collective-permute-start | bytes 1339400 | tf_op jit(solution)/shard_map/ppermute | solution.py:76
  19.1 15.6 %collective-permute-start.5 = (f32[872,128]{1,0:T(8,128)S(1)}, f32[872,128]{1,0:T(8,128)S(1)}, u32[]{:S(2)}, u32[]{:S(2)}) collective-permute-start(f32[872,128]{1,0:T(8,128)S(1)} %get-tuple-element.47), channel_id=1, source_target_pairs={{0,1},{1,0},{2,3},{3,2},{4,5},{5,4},{6,7},{7,6},{8,9},{9,8},{10,11... | collective-permute-start | bytes 1339400 | tf_op jit(solution)/shard_map/ppermute | solution.py:76
  38.8 31.4 %all-to-all-start = ((f32[256,1,128]{2,1,0:T(1,128)}), f32[256,1,128]{2,1,0:T(1,128)S(1)}, u32[]{:S(2)}, u32[]{:S(2)}) async-start(f32[256,1,128]{2,1,0:T(1,128)} %bitcast.1), calls=%async_computation | async-start | bytes 262144 | tf_op jit(solution)/shard_map/all_to_all | solution.py:800
  53.8 6.1 %collective-permute-start.6 = (f32[36,8,128]{2,1,0:T(8,128)}, f32[36,8,128]{2,1,0:T(8,128)S(1)}, u32[]{:S(2)}, u32[]{:S(2)}) collective-permute-start(f32[36,8,128]{2,1,0:T(8,128)} %get-tuple-element.52), channel_id=1, source_target_pairs={{0,4},{1,5},{2,6},{3,7},{4,0},{5,1},{6,2},{7,3},{8,12},{9,13},{10,... | collective-permute-start | bytes 442376 | tf_op jit(solution)/shard_map/ppermute | solution.py:76
  55.2 4.6 %collective-permute-start.7 = (f32[36,8,128]{2,1,0:T(8,128)S(1)}, f32[36,8,128]{2,1,0:T(8,128)S(1)}, u32[]{:S(2)}, u32[]{:S(2)}) collective-permute-start(f32[36,8,128]{2,1,0:T(8,128)S(1)} %get-tuple-element.53), channel_id=1, source_target_pairs={{0,1},{1,0},{2,3},{3,2},{4,8},{5,9},{6,10},{7,11},{8,4},{9,5},{10,... | collective-permute-start | bytes 442376 | tf_op jit(solution)/shard_map/ppermute | solution.py:76
  60.2 9.3 %collective-permute-start.8 = (f32[20,8,128]{2,1,0:T(8,128)S(1)}, f32[20,8,128]{2,1,0:T(8,128)S(1)}, u32[]{:S(2)}, u32[]{:S(2)}) collective-permute-start(f32[20,8,128]{2,1,0:T(8,128)S(1)} %get-tuple-element.63), channel_id=1, source_target_pairs={{0,1},{1,0},{2,3},{3,2},{4,5},{5,4},{6,7},{7,6},{8,9},{9,8},{10,11... | collective-permute-start | bytes 245768 | tf_op jit(solution)/shard_map/ppermute | solution.py:76
  62.3 7.9 %collective-permute-start.9 = (f32[20,8,128]{2,1,0:T(8,128)S(1)}, f32[20,8,128]{2,1,0:T(8,128)S(1)}, u32[]{:S(2)}, u32[]{:S(2)}) collective-permute-start(f32[20,8,128]{2,1,0:T(8,128)S(1)} %get-tuple-element.64), channel_id=1, source_target_pairs={{0,4},{1,2},{2,1},{3,7},{4,0},{5,6},{6,5},{7,3},{8,12},{9,10},{10,... | collective-permute-start | bytes 245768 | tf_op jit(solution)/shard_map/ppermute | solution.py:76
